TPU v7x, 128 devices: a whole 4x4x4 slice. The times are simulated.
128 devices in a mesh: site: 32 (over y, z_lo, x), freq: 4 (over z_hi, core).
Axes of the slice: x: 4, y: 4, z: 4 (z_hi: 2, z_lo: 2; z = z_hi * 2 + z_lo), core: 2. Of those that a mesh axis runs over, the one named last changes fastest.
Arguments:
- green_tangent: float32 [128, 2, 2, 128, 512], P('site', None, None, None, 'freq'), may hold values from -6 to 6
- green_plus: float32 [128, 2, 128, 512], P('freq', None, 'site'), may hold values from -6 to 6
- green_mirror: float32 [128, 2, 128, 512], P('freq', None, 'site'), may hold values from -6 to 6
- potential: float32 [128, 2, 128, 512], P('freq', None, 'site'), may hold values from -6 to 6
- bubble: float32 [128, 2, 128, 512], P('site', None, None, 'freq'), may hold values from -0.5 to 0.5
Outputs:
- sigma_tangent: float32 [128, 2, 2, 128, 512], P('site', None, None, None, 'freq')
All inputs are finite; a program needn't handle non-finite values.
Results may differ from a plain program's by a relative error of at most 0.000092.
Values sent between devices are 32-bit elements; how exact they have to be, the bound alone decides.
No kernel may reach another device: no remote copies, remote signals or barrier semaphores. Data moves between devices by JAX's collectives and lax.ppermute only.
A program may use at most 128 MiB of HBM per device.

v0:
```python
import math

import jax
import jax.numpy as jnp
from jax import lax
from jax.sharding import PartitionSpec as P

NX = 128
NY = 128
NF = 512


HIGHEST = lax.Precision.HIGHEST
HUBBARD = 1.0
ROWS_FORM = "xtsyf,xk->ktsyf"
COLS_FORM = "xtsyf,yk->xtskf"
TIME_FORM = "xtsyf,fk->xtsyk"


def phase_table(number, factor, offset, period, sign, inward):
    indices = jnp.arange(number, dtype=jnp.int32)
    shifted = factor * indices + offset
    numerator = jnp.mod(shifted[:, None] * indices[None, :], period)
    angle = sign * 2.0 * math.pi / period * numerator.astype(jnp.float32)
    scaling = 1.0 / math.sqrt(number)
    cosine = jnp.cos(angle) * scaling
    sine = jnp.sin(angle) * scaling
    if inward:
        return (cosine, sine)
    return (cosine.T, sine.T)


def transform(source, table, form):
    cosine, sine = table
    real_part = source[:, :, :, 0]
    imag_part = source[:, :, :, 1]
    real_cos = jnp.einsum(form, real_part, cosine, precision=HIGHEST)
    real_sin = jnp.einsum(form, real_part, sine, precision=HIGHEST)
    imag_cos = jnp.einsum(form, imag_part, cosine, precision=HIGHEST)
    imag_sin = jnp.einsum(form, imag_part, sine, precision=HIGHEST)
    return jnp.stack([real_cos - imag_sin, real_sin + imag_cos], axis=3)


def complex_product(left, right):
    return jnp.stack(
        [
            left[:, :, 0] * right[:, :, 0] - left[:, :, 1] * right[:, :, 1],
            left[:, :, 0] * right[:, :, 1] + left[:, :, 1] * right[:, :, 0],
        ],
        axis=2,
    )


def inverse_square(real_part, imag_part):
    magnitude = real_part * real_part + imag_part * imag_part
    inv_real = real_part / magnitude
    inv_imag = -imag_part / magnitude
    return (inv_real * inv_real - inv_imag * inv_imag, 2.0 * inv_real * inv_imag)


def rpa_weight(bubble):
    chi_real = HUBBARD * bubble[:, 0]
    chi_imag = HUBBARD * bubble[:, 1]
    spin_real, spin_imag = inverse_square(1.0 - chi_real, -chi_imag)
    charge_real, charge_imag = inverse_square(1.0 + chi_real, chi_imag)
    factor = HUBBARD * HUBBARD
    return jnp.stack(
        [
            factor * (1.5 * spin_real + 0.5 * charge_real - 1.0),
            factor * (1.5 * spin_imag + 0.5 * charge_imag),
        ],
        axis=1,
    )


def into_real(source, tables):
    source = transform(source, tables[1], COLS_FORM)
    source = lax.all_to_all(source, "site", split_axis=4, concat_axis=0, tiled=True)
    source = transform(source, tables[0], ROWS_FORM)
    source = lax.all_to_all(source, "freq", split_axis=0, concat_axis=5, tiled=True)
    return transform(source, tables[2], TIME_FORM)


def into_momentum(source, tables):
    source = transform(source, tables[2], TIME_FORM)
    source = lax.all_to_all(source, "freq", split_axis=5, concat_axis=0, tiled=True)
    source = transform(source, tables[0], ROWS_FORM)
    source = lax.all_to_all(source, "site", split_axis=0, concat_axis=4, tiled=True)
    return transform(source, tables[1], COLS_FORM)


def tangent_block(green_tangent, green_plus, green_mirror, potential, weight, table_sets):
    fermion_in, boson_out, boson_in, fermion_out = table_sets
    mirror = jnp.stack([green_tangent[:, :, 0], -green_tangent[:, :, 1]], axis=2)
    paired = into_real(jnp.stack([green_tangent, mirror], axis=2), fermion_in)
    plus_part = paired[:, :, 0]
    minus_part = jnp.stack([paired[:, :, 1, 0], -paired[:, :, 1, 1]], axis=2)
    base_plus = green_plus[:, None]
    chi_change = -(
        complex_product(plus_part, green_mirror[:, None]) + complex_product(base_plus, minus_part)
    )
    chi_q = into_momentum(chi_change[:, :, None], boson_out)[:, :, 0]
    pot_q = complex_product(weight[:, None], chi_q)
    pot_change = into_real(pot_q[:, :, None], boson_in)[:, :, 0]
    sigma_real = complex_product(potential[:, None], plus_part) + complex_product(
        pot_change, base_plus
    )
    return into_momentum(sigma_real[:, :, None], fermion_out)[:, :, 0]


def local(green_tangent, green_plus, green_mirror, potential, bubble):
    fermion_in = (
        phase_table(NX, 1, 0, NX, 1.0, True),
        phase_table(NY, 1, 0, NY, 1.0, True),
        phase_table(NF, 2, 1 - NF, 2 * NF, -1.0, True),
    )
    boson_out = (
        phase_table(NX, 1, 0, NX, -1.0, False),
        phase_table(NY, 1, 0, NY, -1.0, False),
        phase_table(NF, 1, -(NF // 2), NF, 1.0, False),
    )
    boson_in = (
        phase_table(NX, 1, 0, NX, 1.0, True),
        phase_table(NY, 1, 0, NY, 1.0, True),
        phase_table(NF, 1, -(NF // 2), NF, -1.0, True),
    )
    fermion_out = (
        phase_table(NX, 1, 0, NX, -1.0, False),
        phase_table(NY, 1, 0, NY, -1.0, False),
        phase_table(NF, 2, 1 - NF, 2 * NF, 1.0, False),
    )
    table_sets = (fermion_in, boson_out, boson_in, fermion_out)
    weight = rpa_weight(bubble)
    results = [
        tangent_block(
            green_tangent[:, member : member + 1],
            green_plus,
            green_mirror,
            potential,
            weight,
            table_sets,
        )
        for member in range(green_tangent.shape[1])
    ]
    return jnp.concatenate(results, axis=1)


def solution(mesh):
    in_specs = (
        P("site", None, None, None, "freq"),
        P("freq", None, "site", None),
        P("freq", None, "site", None),
        P("freq", None, "site", None),
        P("site", None, None, "freq"),
    )
    out_specs = P("site", None, None, None, "freq")
    return jax.shard_map(local, mesh=mesh, in_specs=in_specs, out_specs=out_specs, check_vma=False)
```

profile of v0, /device:TPU:0, one launch (start us, length us, event | category | flops | bytes accessed | tf_op | source)
XLA Modules:
  0.0 468.7 jit_solution(13963516671610519250)
XLA Ops:
  7.2 8.8 %all-to-all-start = ((f32[4,1,2,2,128,128]{5,2,0,3,1,4:T(2,128)}), f32[4,1,2,2,128,128]{5,2,0,3,1,4:T(2,128)S(1)}, u32[]{:S(2)}, u32[]{:S(2)}) async-start(f32[4,1,2,2,128,128]{5,2,0,3,1,4:T(2,128)} %copy.75), calls=%async_computation | async-start | bytes 2097152 | tf_op jit(solution)/shard_map/all_to_all | solution.py:78
  21.3 11.3 %all-to-all-done = f32[4,1,2,2,128,128]{5,2,0,3,1,4:T(2,128)S(1)} async-done(((f32[4,1,2,2,128,128]{5,2,0,3,1,4:T(2,128)}), f32[4,1,2,2,128,128]{5,2,0,3,1,4:T(2,128)S(1)}, u32[]{:S(2)}, u32[]{:S(2)}) %all-to-all-start) | async-done | bytes 1048608 | tf_op jit(solution)/shard_map/all_to_all | solution.py:78
  32.6 5.3 %all-to-all-start.8 = ((f32[4,1,2,2,128,128]{5,2,0,3,1,4:T(2,128)}), f32[4,1,2,2,128,128]{5,2,0,3,1,4:T(2,128)}, u32[]{:S(2)}, u32[]{:S(2)}) async-start(f32[4,1,2,2,128,128]{5,2,0,3,1,4:T(2,128)} %copy.115), calls=%async_computation.8 | async-start | bytes 2097152 | tf_op jit(solution)/shard_map/all_to_all | solution.py:78
  43.3 10.0 %all-to-all-done.8 = f32[4,1,2,2,128,128]{5,2,0,3,1,4:T(2,128)} async-done(((f32[4,1,2,2,128,128]{5,2,0,3,1,4:T(2,128)}), f32[4,1,2,2,128,128]{5,2,0,3,1,4:T(2,128)}, u32[]{:S(2)}, u32[]{:S(2)}) %all-to-all-start.8) | async-done | bytes 1048608 | tf_op jit(solution)/shard_map/all_to_all | solution.py:78
  58.3 4.8 %all-to-all-start.1 = ((f32[128,1,2,2,4,128]{5,4,2,3,1,0:T(4,128)}), f32[128,1,2,2,4,128]{5,4,2,3,1,0:T(4,128)S(1)}, u32[]{:S(2)}, u32[]{:S(2)}) async-start(f32[128,1,2,2,4,128]{5,4,2,3,1,0:T(4,128)} %copy.81), calls=%async_computation.1 | async-start | bytes 2097152 | tf_op jit(solution)/shard_map/all_to_all | solution.py:80
  68.4 10.8 %all-to-all-done.1 = f32[128,1,2,2,4,128]{5,4,2,3,1,0:T(4,128)S(1)} async-done(((f32[128,1,2,2,4,128]{5,4,2,3,1,0:T(4,128)}), f32[128,1,2,2,4,128]{5,4,2,3,1,0:T(4,128)S(1)}, u32[]{:S(2)}, u32[]{:S(2)}) %all-to-all-start.1) | async-done | bytes 1048608 | tf_op jit(solution)/shard_map/all_to_all | solution.py:80
  84.7 5.0 %fusion.96 = f32[32,2,4,512]{3,0,2,1:T(8,128)S(1)} fusion(s32[512]{0:T(512)S(1)} %multiply_add_fusion.5, f32[32,1,2,2,4,512]{5,0,4,2,3,1:T(8,128)S(1)} %all_to_all.215), kind=kOutput, calls=%fused_computation.159 | convolution fusion | flops 809238528 | bytes 1050624 | tf_op jit(solution)/shard_map/xtsyf,fk->xtsyk/dot_general | solution.py:38
  89.7 5.0 %fusion.91 = f32[32,2,4,512]{3,0,2,1:T(8,128)S(1)} fusion(s32[512]{0:T(512)S(1)} %multiply_add_fusion.5, f32[32,1,2,2,4,512]{5,0,4,2,3,1:T(8,128)S(1)} %all_to_all.215), kind=kOutput, calls=%fused_computation.154 | convolution fusion | flops 809238528 | bytes 1050624 | tf_op jit(solution)/shard_map/xtsyf,fk->xtsyk/dot_general | solution.py:37
  94.7 5.2 %fusion.2 = f32[32,1,2,1,4,512]{5,0,4,3,2,1:T(8,128)S(1)} fusion(f32[32,2,4,512]{3,0,2,1:T(8,128)S(1)} %fusion.96, s32[512]{0:T(512)S(1)} %multiply_add_fusion.5, f32[32,1,2,2,4,512]{5,0,4,2,3,1:T(8,128)S(1)} %all_to_all.215), kind=kOutput, calls=%fused_computation.11 | convolution fusion | flops 809369600 | bytes 1574912 | tf_op jit(solution)/shard_map/xtsyf,fk->xtsyk/dot_general | solution.py:39
  99.9 5.0 %convolution_subtract_fusion.1 = f32[32,2,4,512]{3,0,2,1:T(8,128)S(1)} fusion(f32[32,2,4,512]{3,0,2,1:T(8,128)S(1)} %fusion.91, s32[512]{0:T(512)S(1)} %multiply_add_fusion.5, f32[32,1,2,2,4,512]{5,0,4,2,3,1:T(8,128)S(1)} %all_to_all.215), kind=kOutput, calls=%fused_computation.12 | convolution fusion | flops 809369600 | bytes 1574912 | tf_op jit(solution)/shard_map/xtsyf,fk->xtsyk/dot_general | solution.py:40
  107.0 5.5 %fusion.78 = f32[32,4,512]{2,0,1:T(8,128)S(1)} fusion(s32[512]{0:T(512)S(1)} %iota_add_fusion, f32[32,1,1,2,4,512]{5,0,4,3,2,1:T(8,128)S(1)} %fusion.113), kind=kOutput, calls=%fused_computation.141 | convolution fusion | flops 406585344 | bytes 526336 | tf_op jit(solution)/shard_map/xtsyf,fk->xtsyk/dot_general | solution.py:38
  112.5 5.0 %fusion.85 = f32[32,4,512]{2,0,1:T(8,128)S(1)} fusion(s32[512]{0:T(512)S(1)} %iota_add_fusion, f32[32,1,1,2,4,512]{5,0,4,3,2,1:T(8,128)S(1)} %fusion.113), kind=kOutput, calls=%fused_computation.148 | convolution fusion | flops 406585344 | bytes 526336 | tf_op jit(solution)/shard_map/xtsyf,fk->xtsyk/dot_general | solution.py:37
  117.6 5.2 %fusion.45 = f32[32,1,1,1,4,512]{5,0,4,3,2,1:T(8,128)S(1)} fusion(f32[32,4,512]{2,0,1:T(8,128)S(1)} %fusion.78, s32[512]{0:T(512)S(1)} %iota_add_fusion, f32[32,1,1,2,4,512]{5,0,4,3,2,1:T(8,128)S(1)} %fusion.113), kind=kOutput, calls=%fused_computation.98 | convolution fusion | flops 406650880 | bytes 788480 | tf_op jit(solution)/shard_map/xtsyf,fk->xtsyk/dot_general | solution.py:39
  122.8 5.0 %fusion.46 = f32[32,1,1,1,4,512]{5,0,4,3,2,1:T(8,128)S(1)} fusion(f32[32,4,512]{2,0,1:T(8,128)S(1)} %fusion.85, s32[512]{0:T(512)S(1)} %iota_add_fusion, f32[32,1,1,2,4,512]{5,0,4,3,2,1:T(8,128)S(1)} %fusion.113), kind=kOutput, calls=%fused_computation.100 | convolution fusion | flops 406650880 | bytes 788480 | tf_op jit(solution)/shard_map/xtsyf,fk->xtsyk/dot_general | solution.py:40
  131.0 4.7 %all-to-all-start.2 = ((f32[4,1,32768]{2,1,0:T(1,128)}), f32[4,1,32768]{2,1,0:T(1,128)S(1)}, u32[]{:S(2)}, u32[]{:S(2)}) async-start(f32[4,1,32768]{2,1,0:T(1,128)} %reshape.1117), calls=%async_computation.2 | async-start | bytes 1048576 | tf_op jit(solution)/shard_map/all_to_all | solution.py:86
  139.4 6.7 %all-to-all-done.2 = f32[4,1,32768]{2,1,0:T(1,128)S(1)} async-done(((f32[4,1,32768]{2,1,0:T(1,128)}), f32[4,1,32768]{2,1,0:T(1,128)S(1)}, u32[]{:S(2)}, u32[]{:S(2)}) %all-to-all-start.2) | async-done | bytes 524320 | tf_op jit(solution)/shard_map/all_to_all | solution.py:86
  161.0 5.0 %all-to-all-start.3 = ((f32[128,1,1,2,4,128]{5,4,3,2,1,0:T(4,128)}), f32[128,1,1,2,4,128]{5,4,3,2,1,0:T(4,128)S(1)}, u32[]{:S(2)}, u32[]{:S(2)}) async-start(f32[128,1,1,2,4,128]{5,4,3,2,1,0:T(4,128)} %copy.90), calls=%async_computation.3 | async-start | bytes 1048576 | tf_op jit(solution)/shard_map/all_to_all | solution.py:88
  166.0 5.0 %fusion.93 = f32[32,2,4,512]{3,0,2,1:T(8,128)S(1)} fusion(s32[512]{0:T(512)S(1)} %multiply_add_fusion.5, f32[32,1,2,2,4,512]{5,0,4,2,3,1:T(8,128)S(1)} %copy-done.8), kind=kOutput, calls=%fused_computation.156 | convolution fusion | flops 809238528 | bytes 1050624 | tf_op jit(solution)/shard_map/xtsyf,fk->xtsyk/dot_general | solution.py:38
  171.0 5.0 %fusion = f32[32,1,2,1,4,512]{5,0,4,3,2,1:T(8,128)S(1)} fusion(f32[32,2,4,512]{3,0,2,1:T(8,128)S(1)} %fusion.93, s32[512]{0:T(512)S(1)} %multiply_add_fusion.5, f32[32,1,2,2,4,512]{5,0,4,2,3,1:T(8,128)S(1)} %copy-done.8), kind=kOutput, calls=%fused_computation.7 | convolution fusion | flops 809369600 | bytes 1574912 | tf_op jit(solution)/shard_map/xtsyf,fk->xtsyk/dot_general | solution.py:39
  183.9 7.3 %all-to-all-start.4 = ((f32[4,1,1,2,128,128]{5,0,3,2,1,4:T(4,128)}), f32[4,1,1,2,128,128]{5,0,3,2,1,4:T(4,128)S(1)}, u32[]{:S(2)}, u32[]{:S(2)}) async-start(f32[4,1,1,2,128,128]{5,0,3,2,1,4:T(4,128)} %copy.96), calls=%async_computation.4 | async-start | bytes 1048576 | tf_op jit(solution)/shard_map/all_to_all | solution.py:78
  191.2 5.0 %fusion.88 = f32[32,2,4,512]{3,0,2,1:T(8,128)S(1)} fusion(s32[512]{0:T(512)S(1)} %multiply_add_fusion.5, f32[32,1,2,2,4,512]{5,0,4,2,3,1:T(8,128)S(1)} %copy-done.8), kind=kOutput, calls=%fused_computation.151 | convolution fusion | flops 809238528 | bytes 1050624 | tf_op jit(solution)/shard_map/xtsyf,fk->xtsyk/dot_general | solution.py:37
  196.2 5.8 %fusion.1 = f32[32,1,2,1,4,512]{5,0,4,3,2,1:T(8,128)} fusion(f32[32,2,4,512]{3,0,2,1:T(8,128)S(1)} %fusion.88, s32[512]{0:T(512)S(1)} %multiply_add_fusion.5, f32[32,1,2,2,4,512]{5,0,4,2,3,1:T(8,128)S(1)} %copy-done.8), kind=kOutput, calls=%fused_computation.9 | convolution fusion | flops 809369600 | bytes 1574912 | tf_op jit(solution)/shard_map/xtsyf,fk->xtsyk/dot_general | solution.py:40
  211.9 8.3 %all-to-all-done.5 = f32[128,1,1,2,4,128]{5,4,3,2,1,0:T(4,128)S(1)} async-done(((f32[128,1,1,2,4,128]{5,4,3,2,1,0:T(4,128)}), f32[128,1,1,2,4,128]{5,4,3,2,1,0:T(4,128)S(1)}, u32[]{:S(2)}, u32[]{:S(2)}) %all-to-all-start.5) | async-done | bytes 524320 | tf_op jit(solution)/shard_map/all_to_all | solution.py:80
  220.8 4.6 fusion.66
  230.0 4.8 %fusion.43 = f32[32,1,1,1,4,512]{5,0,4,3,2,1:T(8,128)S(1)} fusion(f32[32,4,512]{2,0,1:T(8,128)S(1)} %fusion.66, s32[512]{0:T(512)S(1)} %iota_add_fusion, f32[32,1,1,2,4,512]{5,0,4,3,2,1:T(8,128)S(1)} %all_to_all.231), kind=kOutput, calls=%fused_computation.94 | convolution fusion | flops 406650880 | bytes 788480 | tf_op jit(solution)/shard_map/xtsyf,fk->xtsyk/dot_general | solution.py:39
  234.8 4.6 fusion.44
  240.6 5.4 %fusion.75 = f32[32,4,512]{2,0,1:T(8,128)S(1)} fusion(s32[512]{0:T(512)S(1)} %iota_add_fusion, f32[32,1,1,2,4,512]{5,0,4,3,2,1:T(8,128)S(1)} %fusion.114), kind=kOutput, calls=%fused_computation.138 | convolution fusion | flops 406585344 | bytes 526336 | tf_op jit(solution)/shard_map/xtsyf,fk->xtsyk/dot_general | solution.py:38
  246.0 5.0 %fusion.82 = f32[32,4,512]{2,0,1:T(8,128)S(1)} fusion(s32[512]{0:T(512)S(1)} %iota_add_fusion, f32[32,1,1,2,4,512]{5,0,4,3,2,1:T(8,128)S(1)} %fusion.114), kind=kOutput, calls=%fused_computation.145 | convolution fusion | flops 406585344 | bytes 526336 | tf_op jit(solution)/shard_map/xtsyf,fk->xtsyk/dot_general | solution.py:37
  251.1 5.0 %fusion.39 = f32[32,1,1,1,4,512]{5,0,4,3,2,1:T(8,128)S(1)} fusion(f32[32,4,512]{2,0,1:T(8,128)S(1)} %fusion.75, s32[512]{0:T(512)S(1)} %iota_add_fusion, f32[32,1,1,2,4,512]{5,0,4,3,2,1:T(8,128)S(1)} %fusion.114), kind=kOutput, calls=%fused_computation.86 | convolution fusion | flops 406650880 | bytes 788480 | tf_op jit(solution)/shard_map/xtsyf,fk->xtsyk/dot_general | solution.py:39
  256.1 5.0 %fusion.40 = f32[32,1,1,1,4,512]{5,0,4,3,2,1:T(8,128)S(1)} fusion(f32[32,4,512]{2,0,1:T(8,128)S(1)} %fusion.82, s32[512]{0:T(512)S(1)} %iota_add_fusion, f32[32,1,1,2,4,512]{5,0,4,3,2,1:T(8,128)S(1)} %fusion.114), kind=kOutput, calls=%fused_computation.88 | convolution fusion | flops 406650880 | bytes 788480 | tf_op jit(solution)/shard_map/xtsyf,fk->xtsyk/dot_general | solution.py:40
  271.0 5.0 %fusion.54 = f32[32,4,512]{2,0,1:T(8,128)S(1)} fusion(s32[512]{0:T(512)S(1)} %multiply_add_fusion.5, f32[32,1,1,2,4,512]{5,0,4,3,2,1:T(8,128)S(1)} %maximum_add_fusion), kind=kOutput, calls=%fused_computation.117 | convolution fusion | flops 406585344 | bytes 526336 | tf_op jit(solution)/shard_map/xtsyf,fk->xtsyk/dot_general | solution.py:38
  276.0 5.9 %fusion.41 = f32[32,1,1,1,4,512]{5,0,4,3,2,1:T(8,128)} fusion(f32[32,4,512]{2,0,1:T(8,128)S(1)} %fusion.54, s32[512]{0:T(512)S(1)} %multiply_add_fusion.5, f32[32,1,1,2,4,512]{5,0,4,3,2,1:T(8,128)S(1)} %maximum_add_fusion), kind=kOutput, calls=%fused_computation.90 | convolution fusion | flops 406650880 | bytes 788480 | tf_op jit(solution)/shard_map/xtsyf,fk->xtsyk/dot_general | solution.py:39
  296.3 8.8 %all-to-all-start.11 = ((f32[128,1,1,2,4,128]{5,4,3,2,1,0:T(4,128)}), f32[128,1,1,2,4,128]{5,4,3,2,1,0:T(4,128)}, u32[]{:S(2)}, u32[]{:S(2)}) async-start(f32[128,1,1,2,4,128]{5,4,3,2,1,0:T(4,128)} %copy.125), calls=%async_computation.11 | async-start | bytes 1048576 | tf_op jit(solution)/shard_map/all_to_all | solution.py:88
  305.2 5.0 %fusion.61 = f32[32,4,512]{2,0,1:T(8,128)S(1)} fusion(s32[512]{0:T(512)S(1)} %multiply_add_fusion.5, f32[32,1,1,2,4,512]{5,0,4,3,2,1:T(8,128)S(1)} %copy-done.13), kind=kOutput, calls=%fused_computation.124 | convolution fusion | flops 406585344 | bytes 526336 | tf_op jit(solution)/shard_map/xtsyf,fk->xtsyk/dot_general | solution.py:37
  310.2 5.0 %fusion.42 = f32[32,1,1,1,4,512]{5,0,4,3,2,1:T(8,128)S(1)} fusion(f32[32,4,512]{2,0,1:T(8,128)S(1)} %fusion.61, s32[512]{0:T(512)S(1)} %multiply_add_fusion.5, f32[32,1,1,2,4,512]{5,0,4,3,2,1:T(8,128)S(1)} %copy-done.13), kind=kOutput, calls=%fused_computation.92 | convolution fusion | flops 406650880 | bytes 788480 | tf_op jit(solution)/shard_map/xtsyf,fk->xtsyk/dot_general | solution.py:40
  320.1 5.6 %all-to-all-start.6 = ((f32[4,1,32768]{2,1,0:T(1,128)}), f32[4,1,32768]{2,1,0:T(1,128)S(1)}, u32[]{:S(2)}, u32[]{:S(2)}) async-start(f32[4,1,32768]{2,1,0:T(1,128)} %reshape.1119), calls=%async_computation.6 | async-start | bytes 1048576 | tf_op jit(solution)/shard_map/all_to_all | solution.py:86
  336.0 7.9 %all-to-all-start.12 = ((f32[4,1,1,2,128,128]{5,0,3,2,1,4:T(4,128)}), f32[4,1,1,2,128,128]{5,0,3,2,1,4:T(4,128)}, u32[]{:S(2)}, u32[]{:S(2)}) async-start(f32[4,1,1,2,128,128]{5,0,3,2,1,4:T(4,128)} %copy.131), calls=%async_computation.12 | async-start | bytes 1048576 | tf_op jit(solution)/shard_map/all_to_all | solution.py:78
  349.5 5.8 %all-to-all-done.12 = f32[4,1,1,2,128,128]{5,0,3,2,1,4:T(4,128)} async-done(((f32[4,1,1,2,128,128]{5,0,3,2,1,4:T(4,128)}), f32[4,1,1,2,128,128]{5,0,3,2,1,4:T(4,128)}, u32[]{:S(2)}, u32[]{:S(2)}) %all-to-all-start.12) | async-done | bytes 524320 | tf_op jit(solution)/shard_map/all_to_all | solution.py:78
  366.3 7.8 %all-to-all-done.13 = f32[128,1,1,2,4,128]{5,4,3,2,1,0:T(4,128)S(1)} async-done(((f32[128,1,1,2,4,128]{5,4,3,2,1,0:T(4,128)}), f32[128,1,1,2,4,128]{5,4,3,2,1,0:T(4,128)S(1)}, u32[]{:S(2)}, u32[]{:S(2)}) %all-to-all-start.13) | async-done | bytes 524320 | tf_op jit(solution)/shard_map/all_to_all | solution.py:80
  388.5 4.8 %fusion.37 = f32[32,1,1,1,4,512]{5,0,4,3,2,1:T(8,128)S(1)} fusion(f32[32,4,512]{2,0,1:T(8,128)S(1)} %fusion.63, s32[512]{0:T(512)S(1)} %iota_add_fusion, f32[32,1,1,2,4,512]{5,0,4,3,2,1:T(8,128)S(1)} %all_to_all.263), kind=kOutput, calls=%fused_computation.82 | convolution fusion | flops 406650880 | bytes 788480 | tf_op jit(solution)/shard_map/xtsyf,fk->xtsyk/dot_general | solution.py:39
  393.3 4.6 fusion.38
  399.0 5.2 %fusion.51 = f32[32,4,512]{2,0,1:T(8,128)S(1)} fusion(s32[512]{0:T(512)S(1)} %multiply_add_fusion.5, f32[32,1,1,2,4,512]{5,0,4,3,2,1:T(8,128)S(1)} %maximum_add_fusion.2), kind=kOutput, calls=%fused_computation.114 | convolution fusion | flops 406585344 | bytes 526336 | tf_op jit(solution)/shard_map/xtsyf,fk->xtsyk/dot_general | solution.py:38
  404.2 5.0 %fusion.35 = f32[32,1,1,1,4,512]{5,0,4,3,2,1:T(8,128)S(1)} fusion(f32[32,4,512]{2,0,1:T(8,128)S(1)} %fusion.51, s32[512]{0:T(512)S(1)} %multiply_add_fusion.5, f32[32,1,1,2,4,512]{5,0,4,3,2,1:T(8,128)S(1)} %maximum_add_fusion.2), kind=kOutput, calls=%fused_computation.78 | convolution fusion | flops 406650880 | bytes 788480 | tf_op jit(solution)/shard_map/xtsyf,fk->xtsyk/dot_general | solution.py:39
  409.2 5.0 %fusion.58 = f32[32,4,512]{2,0,1:T(8,128)S(1)} fusion(s32[512]{0:T(512)S(1)} %multiply_add_fusion.5, f32[32,1,1,2,4,512]{5,0,4,3,2,1:T(8,128)S(1)} %maximum_add_fusion.2), kind=kOutput, calls=%fused_computation.121 | convolution fusion | flops 406585344 | bytes 526336 | tf_op jit(solution)/shard_map/xtsyf,fk->xtsyk/dot_general | solution.py:37
  414.3 5.4 %fusion.36 = f32[32,1,1,1,4,512]{5,0,4,3,2,1:T(8,128)S(1)} fusion(f32[32,4,512]{2,0,1:T(8,128)S(1)} %fusion.58, s32[512]{0:T(512)S(1)} %multiply_add_fusion.5, f32[32,1,1,2,4,512]{5,0,4,3,2,1:T(8,128)S(1)} %maximum_add_fusion.2), kind=kOutput, calls=%fused_computation.80 | convolution fusion | flops 406650880 | bytes 788480 | tf_op jit(solution)/shard_map/xtsyf,fk->xtsyk/dot_general | solution.py:40
  427.2 9.6 %all-to-all-done.14 = f32[4,1,32768]{2,1,0:T(1,128)S(1)} async-done(((f32[4,1,32768]{2,1,0:T(1,128)}), f32[4,1,32768]{2,1,0:T(1,128)S(1)}, u32[]{:S(2)}, u32[]{:S(2)}) %all-to-all-start.14) | async-done | bytes 524320 | tf_op jit(solution)/shard_map/all_to_all | solution.py:86
  444.7 8.5 %all-to-all-start.15 = ((f32[128,1,1,2,4,128]{5,4,3,2,1,0:T(4,128)}), f32[128,1,1,2,4,128]{5,4,3,2,1,0:T(4,128)S(1)}, u32[]{:S(2)}, u32[]{:S(2)}) async-start(f32[128,1,1,2,4,128]{5,4,3,2,1,0:T(4,128)} %copy.141), calls=%async_computation.15 | async-start | bytes 1048576 | tf_op jit(solution)/shard_map/all_to_all | solution.py:88
  455.2 9.4 %all-to-all-done.15 = f32[128,1,1,2,4,128]{5,4,3,2,1,0:T(4,128)S(1)} async-done(((f32[128,1,1,2,4,128]{5,4,3,2,1,0:T(4,128)}), f32[128,1,1,2,4,128]{5,4,3,2,1,0:T(4,128)S(1)}, u32[]{:S(2)}, u32[]{:S(2)}) %all-to-all-start.15) | async-done | bytes 524320 | tf_op jit(solution)/shard_map/all_to_all | solution.py:88
  (217 shorter events, 173.3 us)
Async XLA Ops:
  0.0 1.5 copy-start.4
  7.2 25.4 %all-to-all-start = ((f32[4,1,2,2,128,128]{5,2,0,3,1,4:T(2,128)}), f32[4,1,2,2,128,128]{5,2,0,3,1,4:T(2,128)S(1)}, u32[]{:S(2)}, u32[]{:S(2)}) async-start(f32[4,1,2,2,128,128]{5,2,0,3,1,4:T(2,128)} %copy.75), calls=%async_computation | async-start | bytes 2097152 | tf_op jit(solution)/shard_map/all_to_all | solution.py:78
  19.5 18.4 %copy-start.14 = (f32[32,2,4,512]{3,2,1,0:T(4,128)S(1)}, f32[32,2,4,512]{3,2,1,0:T(4,128)}, u32[]{:S(2)}) copy-start(f32[32,2,4,512]{3,2,1,0:T(4,128)} %param.6) | copy-start | bytes 1572868
  21.3 16.9 %copy-start.16 = (f32[32,2,4,512]{3,2,1,0:T(4,128)S(1)}, f32[32,2,4,512]{3,2,1,0:T(4,128)}, u32[]{:S(2)}) copy-start(f32[32,2,4,512]{3,2,1,0:T(4,128)} %param.7) | copy-start | bytes 1572868
  21.3 16.9 %copy-start.17 = (f32[32,2,4,512]{3,2,1,0:T(4,128)S(1)}, f32[32,2,4,512]{3,2,1,0:T(4,128)}, u32[]{:S(2)}) copy-start(f32[32,2,4,512]{3,2,1,0:T(4,128)} %param.8) | copy-start | bytes 1572868
  32.6 20.6 %all-to-all-start.8 = ((f32[4,1,2,2,128,128]{5,2,0,3,1,4:T(2,128)}), f32[4,1,2,2,128,128]{5,2,0,3,1,4:T(2,128)}, u32[]{:S(2)}, u32[]{:S(2)}) async-start(f32[4,1,2,2,128,128]{5,2,0,3,1,4:T(2,128)} %copy.115), calls=%async_computation.8 | async-start | bytes 2097152 | tf_op jit(solution)/shard_map/all_to_all | solution.py:78
  39.7 65.4 %copy-start = (f32[32,1,2,4,512]{4,0,3,2,1:T(8,128)}, f32[32,1,2,4,512]{4,0,3,2,1:T(8,128)S(1)}, u32[]{:S(2)}) copy-start(f32[32,1,2,4,512]{4,0,3,2,1:T(8,128)S(1)} %get-tuple-element.43) | copy-start | bytes 1572868
  53.2 1.6 copy-start.6
  53.2 2.5 copy-start.5
  58.3 20.8 %all-to-all-start.1 = ((f32[128,1,2,2,4,128]{5,4,2,3,1,0:T(4,128)}), f32[128,1,2,2,4,128]{5,4,2,3,1,0:T(4,128)S(1)}, u32[]{:S(2)}, u32[]{:S(2)}) async-start(f32[128,1,2,2,4,128]{5,4,2,3,1,0:T(4,128)} %copy.81), calls=%async_computation.1 | async-start | bytes 2097152 | tf_op jit(solution)/shard_map/all_to_all | solution.py:80
  79.1 51.9 %all-to-all-start.9 = ((f32[128,1,2,2,4,128]{5,4,2,3,1,0:T(4,128)}), f32[128,1,2,2,4,128]{5,4,2,3,1,0:T(4,128)}, u32[]{:S(2)}, u32[]{:S(2)}) async-start(f32[128,1,2,2,4,128]{5,4,2,3,1,0:T(4,128)} %copy.121), calls=%async_computation.9 | async-start | bytes 2097152 | tf_op jit(solution)/shard_map/all_to_all | solution.py:80
  104.9 1.0 copy-start.2
  128.9 6.8 %copy-start.15 = (f32[4,2,128,128]{3,2,1,0:T(8,128)S(1)}, f32[4,2,128,128]{3,2,1,0:T(8,128)}, u32[]{:S(2)}) copy-start(f32[4,2,128,128]{3,2,1,0:T(8,128)} %param.9) | copy-start | bytes 1572868
  131.0 15.1 %all-to-all-start.2 = ((f32[4,1,32768]{2,1,0:T(1,128)}), f32[4,1,32768]{2,1,0:T(1,128)S(1)}, u32[]{:S(2)}, u32[]{:S(2)}) async-start(f32[4,1,32768]{2,1,0:T(1,128)} %reshape.1117), calls=%async_computation.2 | async-start | bytes 1048576 | tf_op jit(solution)/shard_map/all_to_all | solution.py:86
  158.1 7.8 %copy-start.8 = (f32[32,1,2,2,4,512]{5,0,4,2,3,1:T(8,128)S(1)}, f32[32,1,2,2,4,512]{5,0,4,2,3,1:T(8,128)}, u32[]{:S(2)}) copy-start(f32[32,1,2,2,4,512]{5,0,4,2,3,1:T(8,128)} %all_to_all.247) | copy-start | bytes 3145732
  161.0 16.0 %all-to-all-start.3 = ((f32[128,1,1,2,4,128]{5,4,3,2,1,0:T(4,128)}), f32[128,1,1,2,4,128]{5,4,3,2,1,0:T(4,128)S(1)}, u32[]{:S(2)}, u32[]{:S(2)}) async-start(f32[128,1,1,2,4,128]{5,4,3,2,1,0:T(4,128)} %copy.90), calls=%async_computation.3 | async-start | bytes 1048576 | tf_op jit(solution)/shard_map/all_to_all | solution.py:88
  183.9 18.2 %all-to-all-start.4 = ((f32[4,1,1,2,128,128]{5,0,3,2,1,4:T(4,128)}), f32[4,1,1,2,128,128]{5,0,3,2,1,4:T(4,128)S(1)}, u32[]{:S(2)}, u32[]{:S(2)}) async-start(f32[4,1,1,2,128,128]{5,0,3,2,1,4:T(4,128)} %copy.96), calls=%async_computation.4 | async-start | bytes 1048576 | tf_op jit(solution)/shard_map/all_to_all | solution.py:78
  205.3 5.6 %copy-start.1 = (f32[32,1,2,4,512]{4,0,3,2,1:T(8,128)S(1)}, f32[32,1,2,4,512]{4,0,3,2,1:T(8,128)}, u32[]{:S(2)}) copy-start(f32[32,1,2,4,512]{4,0,3,2,1:T(8,128)} %copy-done) | copy-start | bytes 1572868
  205.3 5.6 %copy-start.3 = (f32[32,1,2,4,512]{4,0,3,2,1:T(8,128)S(1)}, f32[32,1,2,4,512]{4,0,3,2,1:T(8,128)}, u32[]{:S(2)}) copy-start(f32[32,1,2,4,512]{4,0,3,2,1:T(8,128)} %get-tuple-element.44) | copy-start | bytes 1572868
  206.4 13.8 %all-to-all-start.5 = ((f32[128,1,1,2,4,128]{5,4,3,2,1,0:T(4,128)}), f32[128,1,1,2,4,128]{5,4,3,2,1,0:T(4,128)S(1)}, u32[]{:S(2)}, u32[]{:S(2)}) async-start(f32[128,1,1,2,4,128]{5,4,3,2,1,0:T(4,128)} %copy.102), calls=%async_computation.5 | async-start | bytes 1048576 | tf_op jit(solution)/shard_map/all_to_all | solution.py:80
  234.8 4.7 %copy-start.7 = (f32[32,1,2,1,4,512]{5,0,4,3,2,1:T(8,128)S(1)}, f32[32,1,2,1,4,512]{5,0,4,3,2,1:T(8,128)}, u32[]{:S(2)}) copy-start(f32[32,1,2,1,4,512]{5,0,4,3,2,1:T(8,128)} %fusion.1) | copy-start | bytes 1572868
  239.4 1.1 copy-start.10
  239.4 1.0 copy-start.11
  266.0 15.9 %all-to-all-start.10 = ((f32[4,1,32768]{2,1,0:T(1,128)}), f32[4,1,32768]{2,1,0:T(1,128)S(1)}, u32[]{:S(2)}, u32[]{:S(2)}) async-start(f32[4,1,32768]{2,1,0:T(1,128)} %reshape.1113), calls=%async_computation.10 | async-start | bytes 1048576 | tf_op jit(solution)/shard_map/all_to_all | solution.py:86
  271.0 5.1 %copy-start.12 = (f32[32,1,1,2,4,512]{5,0,4,3,2,1:T(8,128)}, f32[32,1,1,2,4,512]{5,0,4,3,2,1:T(8,128)S(1)}, u32[]{:S(2)}) copy-start(f32[32,1,1,2,4,512]{5,0,4,3,2,1:T(8,128)S(1)} %maximum_add_fusion) | copy-start | bytes 1572868
  293.5 11.7 %copy-start.13 = (f32[32,1,1,2,4,512]{5,0,4,3,2,1:T(8,128)S(1)}, f32[32,1,1,2,4,512]{5,0,4,3,2,1:T(8,128)}, u32[]{:S(2)}) copy-start(f32[32,1,1,2,4,512]{5,0,4,3,2,1:T(8,128)} %copy-done.12) | copy-start | bytes 1572868
  296.3 23.8 %all-to-all-start.11 = ((f32[128,1,1,2,4,128]{5,4,3,2,1,0:T(4,128)}), f32[128,1,1,2,4,128]{5,4,3,2,1,0:T(4,128)}, u32[]{:S(2)}, u32[]{:S(2)}) async-start(f32[128,1,1,2,4,128]{5,4,3,2,1,0:T(4,128)} %copy.125), calls=%async_computation.11 | async-start | bytes 1048576 | tf_op jit(solution)/shard_map/all_to_all | solution.py:88
  310.2 5.1 %copy-start.18 = (f32[32,1,1,1,4,512]{5,0,4,3,2,1:T(8,128)S(1)}, f32[32,1,1,1,4,512]{5,0,4,3,2,1:T(8,128)}, u32[]{:S(2)}) copy-start(f32[32,1,1,1,4,512]{5,0,4,3,2,1:T(8,128)} %fusion.41) | copy-start | bytes 786436
  320.1 15.9 %all-to-all-start.6 = ((f32[4,1,32768]{2,1,0:T(1,128)}), f32[4,1,32768]{2,1,0:T(1,128)S(1)}, u32[]{:S(2)}, u32[]{:S(2)}) async-start(f32[4,1,32768]{2,1,0:T(1,128)} %reshape.1119), calls=%async_computation.6 | async-start | bytes 1048576 | tf_op jit(solution)/shard_map/all_to_all | solution.py:86
  336.0 19.3 %all-to-all-start.12 = ((f32[4,1,1,2,128,128]{5,0,3,2,1,4:T(4,128)}), f32[4,1,1,2,128,128]{5,0,3,2,1,4:T(4,128)}, u32[]{:S(2)}, u32[]{:S(2)}) async-start(f32[4,1,1,2,128,128]{5,0,3,2,1,4:T(4,128)} %copy.131), calls=%async_computation.12 | async-start | bytes 1048576 | tf_op jit(solution)/shard_map/all_to_all | solution.py:78
  360.3 13.8 %all-to-all-start.13 = ((f32[128,1,1,2,4,128]{5,4,3,2,1,0:T(4,128)}), f32[128,1,1,2,4,128]{5,4,3,2,1,0:T(4,128)S(1)}, u32[]{:S(2)}, u32[]{:S(2)}) async-start(f32[128,1,1,2,4,128]{5,4,3,2,1,0:T(4,128)} %copy.137), calls=%async_computation.13 | async-start | bytes 1048576 | tf_op jit(solution)/shard_map/all_to_all | solution.py:80
  374.1 48.8 %all-to-all-start.7 = ((f32[128,1,1,2,4,128]{5,4,3,2,1,0:T(4,128)}), f32[128,1,1,2,4,128]{5,4,3,2,1,0:T(4,128)S(1)}, u32[]{:S(2)}, u32[]{:S(2)}) async-start(f32[128,1,1,2,4,128]{5,4,3,2,1,0:T(4,128)} %copy.106), calls=%async_computation.7 | async-start | bytes 1048576 | tf_op jit(solution)/shard_map/all_to_all | solution.py:88
  397.9 1.0 copy-start.9
  422.9 13.8 %all-to-all-start.14 = ((f32[4,1,32768]{2,1,0:T(1,128)}), f32[4,1,32768]{2,1,0:T(1,128)S(1)}, u32[]{:S(2)}, u32[]{:S(2)}) async-start(f32[4,1,32768]{2,1,0:T(1,128)} %reshape.1115), calls=%async_computation.14 | async-start | bytes 1048576 | tf_op jit(solution)/shard_map/all_to_all | solution.py:86
  444.7 19.9 %all-to-all-start.15 = ((f32[128,1,1,2,4,128]{5,4,3,2,1,0:T(4,128)}), f32[128,1,1,2,4,128]{5,4,3,2,1,0:T(4,128)S(1)}, u32[]{:S(2)}, u32[]{:S(2)}) async-start(f32[128,1,1,2,4,128]{5,4,3,2,1,0:T(4,128)} %copy.141), calls=%async_computation.15 | async-start | bytes 1048576 | tf_op jit(solution)/shard_map/all_to_all | solution.py:88
where the time goes:
time: 478 us; the launch traced here: 469 us
  matrix products  216 us (45%)
  starting transfers between devices  89.7 us (19%)
  waiting for transfers between devices  83.2 us (17%)
  local copies, waits for them, and re-layouts  58.9 us (12%)
  other arithmetic  18.9 us (4%)
    dot_general x24, matrix products, transform(): imag_sin = jnp.einsum(form, imag_part, sine, precision=HIGHEST)  54.5 us
    dot_general x24, matrix products, transform(): real_sin = jnp.einsum(form, real_part, sine, precision=HIGHEST)  54.4 us
    dot_general x24, matrix products, transform(): imag_cos = jnp.einsum(form, imag_part, cosine, precision=HIGHEST)  54.1 us
    dot_general x24, matrix products, transform(): real_cos = jnp.einsum(form, real_part, cosine, precision=HIGHEST)  53.2 us
    all_to_all x4, starting transfers between devices, into_real(): lax.all_to_all(source, 'site', split_axis=4, concat_axis=0, tiled=True)  29.3 us
    all_to_all x4, waiting for transfers between devices, into_real(): lax.all_to_all(source, 'site', split_axis=4, concat_axis=0, tiled=True)  27.1 us
    all_to_all x4, waiting for transfers between devices, into_real(): lax.all_to_all(source, 'freq', split_axis=0, concat_axis=5, tiled=True)  26.9 us
    all_to_all x4, starting transfers between devices, into_momentum(): lax.all_to_all(source, 'site', split_axis=0, concat_axis=4, tiled=True)  26.8 us
  transfers between devices with their start and end apart: 16, of which 11 were waited for; matrix products, arithmetic and copies ran while one was open for 37% of the time, Pallas kernels for 0%

commit v1 on v0

v1 whole, which is shorter than its diff:
```python
import math

import jax
import jax.numpy as jnp
import ml_dtypes
import numpy as np
from jax import lax
from jax.experimental import pallas as pl
from jax.experimental.pallas import tpu as pltpu
from jax.sharding import PartitionSpec as P

N = 128
NF = 512
BOTH = ("site", "freq")
CHIPS = 64
BF16 = jnp.bfloat16
F32 = jnp.float32


def column(chip, slab):
    site, z_hi = divmod(chip, 2)
    base = 4 * site + z_hi if site < 16 else 4 * (31 - site) + 2 + z_hi
    if slab == 0:
        return base
    return (N - base) % N if base else N // 2


COLUMN = np.array([[column(chip, slab) for chip in range(CHIPS)] for slab in range(2)])
HOLDER = {int(COLUMN[slab, chip]): 2 * chip + slab for chip in range(CHIPS) for slab in range(2)}


def phases(rows, cols, period, sign, number):
    turns = np.mod(np.outer(rows, cols), period)
    return np.exp(sign * 2j * math.pi / period * turns) / math.sqrt(number)


def real_form(matrix):
    return np.stack(
        [np.stack([matrix.real, -matrix.imag], 1), np.stack([matrix.imag, matrix.real], 1)]
    )


def split(table):
    table = table.astype(np.float32)
    high = table.astype(ml_dtypes.bfloat16)
    low = (table - high.astype(np.float32)).astype(ml_dtypes.bfloat16)
    return np.stack([high, low])


IDX = np.arange(N)
TIME = np.arange(NF)
FERMI = 2 * TIME + 1 - NF
BOSE = TIME - NF // 2


def y_to_columns():
    return split(real_form(phases(COLUMN.reshape(-1), IDX, N, 1, N)).reshape(256, 256))


def y_to_momenta():
    return split(real_form(phases(IDX, COLUMN.reshape(-1), N, -1, N)).reshape(256, 256))


def x_in(sign):
    return real_form(phases(IDX, IDX, N, sign, N)).transpose(0, 1, 3, 2).reshape(256, 256)


def x_in_pair():
    minus = x_in(-1).reshape(2, 128, 256) * np.array([1.0, -1.0])[:, None, None]
    return split(np.concatenate([x_in(1), minus.reshape(256, 256)]))


def x_out():
    return split(real_form(phases(IDX, IDX, N, -1, N)).transpose(1, 0, 2, 3).reshape(256, 256))


def t_in(levels, period, sign):
    table = real_form(phases(TIME, levels, period, sign, NF))
    table = table.reshape(2, 4, 128, 2, NF).transpose(3, 4, 1, 0, 2)
    return split(table.reshape(1024, 1024))


def t_out(levels, period, sign):
    table = real_form(phases(levels, TIME, period, sign, NF))
    table = table.reshape(2, NF, 2, 4, 128).transpose(3, 2, 4, 0, 1)
    return split(table.reshape(1024, 1024))


def dot(a, b):
    return lax.dot_general(a, b, (((1,), (0,)), ((), ())), preferred_element_type=F32)


def halves(value):
    high = value.astype(BF16)
    return high, (value - high.astype(F32)).astype(BF16)


def dot3(a_high, a_low, b_high, b_low):
    return dot(a_high, b_high) + (dot(a_high, b_low) + dot(a_low, b_high))


def slab_rows(core, slot, row):
    return pl.ds((core * 2 + slot) * 8 + row, CHIPS, stride=32)


def store_columns(result, core, out_ref):
    for slot in range(2):
        slab = slot ^ core
        for kx in range(4):
            for part in range(2):
                top = part * 128 + slab * CHIPS
                out_ref[slab_rows(core, slot, kx * 2 + part), :] = result[
                    top : top + CHIPS, kx * 128 : kx * 128 + 128
                ]


def load_columns(core, in_ref):
    blocks = []
    for kx in range(4):
        pieces = []
        for part in range(2):
            for slab in range(2):
                pieces.append(in_ref[slab_rows(core, slab ^ core, kx * 2 + part), :])
        blocks.append(jnp.concatenate(pieces, axis=0))
    return jnp.concatenate(blocks, axis=1)


def first_kernel(table_ref, green_ref, out_ref):
    for core in range(2):
        source = jnp.concatenate(
            [green_ref[kx, core].reshape(256, 128) for kx in range(4)], axis=1
        )
        high, low = halves(source)
        result = dot3(table_ref[0], table_ref[1], high, low)
        store_columns(result, core, out_ref)


def inverse_square(real_part, imag_part):
    scale = 1.0 / (real_part * real_part + imag_part * imag_part)
    inv_real = real_part * scale
    inv_imag = -imag_part * scale
    return (inv_real * inv_real - inv_imag * inv_imag, 2.0 * inv_real * inv_imag)


def middle_kernel(in_table_ref, out_table_ref, bubble_ref, in_ref, out_ref):
    weight_real, weight_imag = [], []
    for kx in range(4):
        chi_real = bubble_ref[kx, 0]
        chi_imag = bubble_ref[kx, 1]
        spin_real, spin_imag = inverse_square(1.0 - chi_real, -chi_imag)
        charge_real, charge_imag = inverse_square(1.0 + chi_real, chi_imag)
        weight_real.append(1.5 * spin_real + 0.5 * charge_real - 1.0)
        weight_imag.append(1.5 * spin_imag + 0.5 * charge_imag)
    weight_real = jnp.concatenate(weight_real, axis=1)
    weight_imag = jnp.concatenate(weight_imag, axis=1)
    for core in range(2):
        high, low = halves(load_columns(core, in_ref))
        chi = dot3(in_table_ref[0], in_table_ref[1], high, low)
        real, imag = chi[:128], chi[128:]
        pot = jnp.concatenate(
            [
                weight_real * real - weight_imag * imag,
                weight_real * imag + weight_imag * real,
            ],
            axis=0,
        )
        high, low = halves(pot)
        result = dot3(out_table_ref[0], out_table_ref[1], high, low)
        store_columns(result, core, out_ref)


def last_kernel(table_ref, in_ref, out_ref):
    for core in range(2):
        high, low = halves(load_columns(core, in_ref))
        result = dot3(table_ref[0], table_ref[1], high, low)
        for kx in range(4):
            for part in range(2):
                out_ref[kx, core, part] = result[
                    part * 128 : part * 128 + 128, kx * 128 : kx * 128 + 128
                ]


def place():
    site = lax.axis_index("site")
    freq = lax.axis_index("freq")
    z_hi = freq // 2
    core = lax.rem(freq, 2)
    row = jnp.where(site < 16, z_hi, 2 + z_hi)
    image = lax.rem(4 - row, 4)
    own = jnp.where(core == 0, row, image)
    other = jnp.where(core == 0, image, row)
    alone = jnp.logical_and(site == 0, z_hi == 0)
    return alone, own, other


def gather_slot(in_ref, slot):
    return jnp.concatenate(
        [in_ref[:, freq, slot].reshape(256, 128) for freq in range(4)], axis=1
    )


def beside(result):
    return jnp.concatenate([result[:128], result[128:]], axis=1)


def finish(x_out_ref, acc_ref, out_ref):
    for slot in range(2):
        top = slot * 128
        source = jnp.concatenate(
            [acc_ref[top : top + 128, :512], acc_ref[top : top + 128, 512:]], axis=0
        )
        high, low = halves(source)
        result = dot3(x_out_ref[0], x_out_ref[1], high, low)
        for freq in range(4):
            out_ref[:, freq, slot] = result[:, freq * 128 : freq * 128 + 128].reshape(32, 8, 128)


def accumulate(step, t_out_ref, work_ref, acc_ref):
    update = dot3(work_ref[0], work_ref[1], t_out_ref[0], t_out_ref[1])

    @pl.when(step == 0)
    def _():
        acc_ref[...] = update

    @pl.when(step > 0)
    def _():
        acc_ref[...] += update


def put_halves(ref, rows, value):
    high, low = halves(value)
    ref[0, rows, :] = high
    ref[1, rows, :] = low


def chi_kernel(
    x_in_ref, t_in_ref, t_out_ref, x_out_ref, in_ref,
    own0, own1, own2, own3, other0, other1, other2, other3,
    out_ref, plus_ref, left_ref, time_ref, work_ref, acc_ref,
):
    step = pl.program_id(0)
    alone, own_row, other_row = place()

    @pl.when(step == 0)
    def _():
        for slot in range(2):
            high, low = halves(gather_slot(in_ref, slot))
            result = dot3(x_in_ref[0], x_in_ref[1], high, low)
            put_halves(left_ref, pl.ds(slot * 128, 128), beside(result[:256]))
            image = jnp.where(alone, slot, 1 - slot)
            rows = pl.ds(pl.multiple_of(256 + image * 128, 128), 128)
            put_halves(left_ref, rows, beside(result[256:]))

    time_ref[...] = dot3(left_ref[0], left_ref[1], t_in_ref[0], t_in_ref[1])
    for slot, row, pieces in (
        (0, own_row, (own0, own1, own2, own3)),
        (1, other_row, (other0, other1, other2, other3)),
    ):
        for shift, piece in enumerate(pieces):
            block = lax.rem(row - shift + 4, 4)
            start = pl.multiple_of(slot * 128 + block * 32, 32)
            rows = pl.ds(start, 32)
            plus = time_ref[rows, :]
            minus = time_ref[pl.ds(256 + start, 32), :]
            plus_real, plus_imag = plus[:, :128], plus[:, 128:]
            minus_real, minus_imag = minus[:, :128], -minus[:, 128:]
            base_real, base_imag = piece[0, 0], piece[0, 1]
            mirror_real, mirror_imag = piece[1, 0], piece[1, 1]
            chi_real = (
                plus_real * mirror_real - plus_imag * mirror_imag
                + base_real * minus_real - base_imag * minus_imag
            )
            chi_imag = (
                plus_real * mirror_imag + plus_imag * mirror_real
                + base_real * minus_imag + base_imag * minus_real
            )
            put_halves(work_ref, rows, -jnp.concatenate([chi_real, chi_imag], axis=1))
            plus_ref[rows, :] = plus
    accumulate(step, t_out_ref, work_ref, acc_ref)

    @pl.when(step == 3)
    def _():
        finish(x_out_ref, acc_ref, out_ref)


def sigma_kernel(
    x_in_ref, t_in_ref, t_out_ref, x_out_ref, in_ref, plus_ref,
    own0, own1, own2, own3, other0, other1, other2, other3,
    out_ref, left_ref, time_ref, work_ref, acc_ref,
):
    step = pl.program_id(0)
    _, own_row, other_row = place()

    @pl.when(step == 0)
    def _():
        for slot in range(2):
            high, low = halves(gather_slot(in_ref, slot))
            result = dot3(x_in_ref[0], x_in_ref[1], high, low)
            put_halves(left_ref, pl.ds(slot * 128, 128), beside(result))

    time_ref[...] = dot3(left_ref[0], left_ref[1], t_in_ref[0], t_in_ref[1])
    for slot, row, pieces in (
        (0, own_row, (own0, own1, own2, own3)),
        (1, other_row, (other0, other1, other2, other3)),
    ):
        for shift, piece in enumerate(pieces):
            block = lax.rem(row - shift + 4, 4)
            rows = pl.ds(pl.multiple_of(slot * 128 + block * 32, 32), 32)
            change = time_ref[rows, :]
            plus = plus_ref[rows, :]
            change_real, change_imag = change[:, :128], change[:, 128:]
            plus_real, plus_imag = plus[:, :128], plus[:, 128:]
            base_real, base_imag = piece[0, 0], piece[0, 1]
            pot_real, pot_imag = piece[2, 0], piece[2, 1]
            real = (
                pot_real * plus_real - pot_imag * plus_imag
                + change_real * base_real - change_imag * base_imag
            )
            imag = (
                pot_real * plus_imag + pot_imag * plus_real
                + change_real * base_imag + change_imag * base_real
            )
            put_halves(work_ref, rows, jnp.concatenate([real, imag], axis=1))
    accumulate(step, t_out_ref, work_ref, acc_ref)

    @pl.when(step == 3)
    def _():
        finish(x_out_ref, acc_ref, out_ref)


PARAMS = pltpu.CompilerParams(vmem_limit_bytes=40 * 1024 * 1024)


def simple_call(body, name, out_shape, flops, *operands):
    size = sum(operand.size * operand.dtype.itemsize for operand in operands)
    return pl.pallas_call(
        body,
        out_shape=jax.ShapeDtypeStruct(out_shape, F32),
        compiler_params=PARAMS,
        cost_estimate=pl.CostEstimate(
            flops=flops, bytes_accessed=size + 4 * math.prod(out_shape), transcendentals=0
        ),
        name=name,
    )(*operands)


def whole(shape):
    return pl.BlockSpec(shape, lambda step: (0,) * len(shape))


def real_space_call(body, name, tables, source, plus, pieces):
    x_table, t_table, t_back, x_back = tables
    wide = x_table.shape[1]
    piece_spec = pl.BlockSpec((3, 2, 32, 128), lambda step: (0, 0, 0, step))
    plus_spec = pl.BlockSpec((256, 256), lambda step: (0, step))
    in_specs = [
        whole((2, wide, 256)),
        pl.BlockSpec((2, 1024, 256), lambda step: (0, 0, step)),
        pl.BlockSpec((2, 256, 1024), lambda step: (0, step, 0)),
        whole((2, 256, 256)),
        whole((32, 4, 2, 8, 128)),
    ]
    operands = [x_table, t_table, t_back, x_back, source.reshape(32, 4, 2, 8, 128)]
    out_shape = [jax.ShapeDtypeStruct((32, 4, 2, 8, 128), F32)]
    out_specs = [whole((32, 4, 2, 8, 128))]
    if plus is None:
        out_shape.append(jax.ShapeDtypeStruct((256, 1024), F32))
        out_specs.append(plus_spec)
    else:
        in_specs.append(plus_spec)
        operands.append(plus)
    return pl.pallas_call(
        body,
        grid=(4,),
        in_specs=in_specs + [piece_spec] * 8,
        out_specs=out_specs,
        out_shape=out_shape,
        scratch_shapes=[
            pltpu.VMEM((2, wide, 1024), BF16),
            pltpu.VMEM((wide, 256), F32),
            pltpu.VMEM((2, 256, 256), BF16),
            pltpu.VMEM((256, 1024), F32),
        ],
        compiler_params=PARAMS,
        cost_estimate=pl.CostEstimate(
            flops=6 * 1024 * 1024 * (wide + 256), bytes_accessed=12 << 20, transcendentals=0
        ),
        name=name,
    )(*operands, *pieces)


def exchange(source):
    source = source.reshape(128, 16, 128)
    return lax.all_to_all(source, BOTH, split_axis=0, concat_axis=0, tiled=True)


def move_pieces(arrays):
    freq = lax.axis_index("freq")
    stacked = jnp.stack([array.transpose(2, 1, 0, 3) for array in arrays], axis=1)
    own, other = [], []
    for shift in range(4):
        row = lax.rem(freq + shift, 4)
        piece = lax.dynamic_index_in_dim(stacked, row, 0, keepdims=False)
        routes = [
            (4 * site + f, HOLDER[4 * site + (f + shift) % 4]) for site in range(32) for f in range(4)
        ]
        own.append(lax.ppermute(piece, BOTH, routes))
    for piece in own:
        other.append(lax.ppermute(piece, BOTH, [(n, n ^ 1) for n in range(128)]))
    return own + other


def local(green_tangent, green_plus, green_mirror, potential, bubble):
    pieces = move_pieces([green_plus, green_mirror, potential])
    columns, momenta = jnp.asarray(y_to_columns()), jnp.asarray(y_to_momenta())
    back = jnp.asarray(x_out())
    chi_tables = (
        jnp.asarray(x_in_pair()),
        jnp.asarray(t_in(FERMI, 2 * NF, -1)),
        jnp.asarray(t_out(BOSE, NF, 1)),
        back,
    )
    sigma_tables = (
        jnp.asarray(split(x_in(1))),
        jnp.asarray(t_in(BOSE, NF, -1)),
        jnp.asarray(t_out(FERMI, 2 * NF, 1)),
        back,
    )
    flops = 2 * 3 * 256 * 256 * 1024
    sent = simple_call(first_kernel, "first", (2048, 128), flops, columns, green_tangent)
    held = exchange(sent)
    sent, plus = real_space_call(chi_kernel, "chi", chi_tables, held, None, pieces)
    held = exchange(sent).reshape(2048, 128)
    sent = simple_call(middle_kernel, "middle", (2048, 128), 2 * flops, momenta, columns, bubble, held)
    held = exchange(sent)
    (sent,) = real_space_call(sigma_kernel, "sigma", sigma_tables, held, plus, pieces)
    held = exchange(sent).reshape(2048, 128)
    return simple_call(last_kernel, "last", (4, 2, 2, 128, 128), flops, momenta, held)


def solution(mesh):
    in_specs = (
        P("site", None, None, None, "freq"),
        P("freq", None, "site", None),
        P("freq", None, "site", None),
        P("freq", None, "site", None),
        P("site", None, None, "freq"),
    )
    out_specs = P("site", None, None, None, "freq")
    return jax.shard_map(local, mesh=mesh, in_specs=in_specs, out_specs=out_specs, check_vma=False)
```

time: 478 us -> 167 us (0.35); the launches traced: 469 us -> 166 us
  matrix products: 216 us -> 0 us
  blocking collectives: 0 us -> 69.4 us
  waiting for transfers between devices: 83.2 us -> 20.1 us
  starting transfers between devices: 89.7 us -> 32.8 us
  local copies, waits for them, and re-layouts: 58.9 us -> 11.9 us
  Pallas kernels: 0 us -> 31.7 us
  other arithmetic: 18.9 us -> 0.41 us
    dot_general x96 -> x0, matrix products: 216 us -> none  [the longest x24 54.5 us: transform(): imag_sin = jnp.einsum(form, imag_part, sine, precision=HIGHEST)]
    all_to_all x16 -> x1, waiting for transfers between devices: 83.2 us -> 0.01 us  [exchange(): return lax.all_to_all(source, BOTH, split_axis=0, concat_axis=0, tiled=True)]
    all_to_all x16 -> x1, starting transfers between devices: 89.7 us -> 11.1 us  [exchange(): return lax.all_to_all(source, BOTH, split_axis=0, concat_axis=0, tiled=True)]
    all_to_all x0 -> x3, blocking collectives: none -> 69.4 us  [exchange(): return lax.all_to_all(source, BOTH, split_axis=0, concat_axis=0, tiled=True)]
    pallas_call x0 -> x5, Pallas kernels: none -> 31.7 us  [the longest x2 25.1 us: real_space_call(): pl.pallas_call(body, grid=(4,), in_specs=in_specs + [piece_spec] * 8, out...]
    another operation x17 -> x0, local copies, waits for them, and re-layouts: 22.1 us -> none  [the longest x16 22 us: transform(): return jnp.stack([real_cos - imag_sin, real_sin + imag_cos], axis=3)]
    ppermute x0 -> x8, starting transfers between devices: none -> 21.6 us  [the longest x4 20.9 us: move_pieces(): own.append(lax.ppermute(piece, BOTH, routes))]
    ppermute x0 -> x8, waiting for transfers between devices: none -> 20.1 us  [the longest x4 18.9 us: move_pieces(): own.append(lax.ppermute(piece, BOTH, routes))]
  transfers between devices with their start and end apart: 16 -> 9, of which waited for: 11 -> 4; matrix products, arithmetic and copies ran while one was open for 37% -> 1% of each run, Pallas kernels for 0% -> 0%
where the time goes in v1:
time: 167 us; the launch traced here: 166 us
  blocking collectives  69.4 us (42%)
  starting transfers between devices  32.8 us (20%)
  Pallas kernels  31.7 us (19%)
  waiting for transfers between devices  20.1 us (12%)
  local copies, waits for them, and re-layouts  11.9 us (7%)
    all_to_all x3, blocking collectives, exchange(): return lax.all_to_all(source, BOTH, split_axis=0, concat_axis=0, tiled=True)  69.4 us
    pallas_call x2, Pallas kernels, real_space_call(): pl.pallas_call(body, grid=(4,), in_specs=in_specs + [piece_spec] * 8, out...  25.1 us
    ppermute x4, starting transfers between devices, move_pieces(): own.append(lax.ppermute(piece, BOTH, routes))  20.9 us
    ppermute x4, waiting for transfers between devices, move_pieces(): own.append(lax.ppermute(piece, BOTH, routes))  18.9 us
    all_to_all x1, starting transfers between devices, exchange(): return lax.all_to_all(source, BOTH, split_axis=0, concat_axis=0, tiled=True)  11.1 us
    unnamed x40, local copies, waits for them, and re-layouts  9.92 us
    pallas_call x3, Pallas kernels, simple_call(): pl.pallas_call(body, out_shape=jax.ShapeDtypeStruct(out_shape, F32), comp...  6.58 us
  transfers between devices with their start and end apart: 9, of which 4 were waited for; matrix products, arithmetic and copies ran while one was open for 1% of the time, Pallas kernels for 0%

profile of v1, /device:TPU:0, one launch (start us, length us, event | category | flops | bytes accessed | tf_op | source)
XLA Modules:
  0.0 166.4 jit_solution(10412821976620534315)
XLA Ops:
  0.0 0.9 copy-done.2
  1.0 1.2 copy-done.4
  2.2 2.0 %first.1 = f32[2048,128]{1,0:T(8,128)} custom-call(bf16[2,256,256]{2,1,0:T(8,128)(2,1)S(1)} %copy-done.2, f32[4,2,2,128,128]{4,3,2,1,0:T(8,128)S(1)} %copy-done.4), custom_call_target="tpu_custom_call" | custom-call | flops 402653184 | bytes 2359296 | tf_op jit(solution)/shard_map/first/pallas_call | solution.py:336
  4.2 11.1 %all-to-all-start = ((f32[128,16,128]{2,1,0:T(8,128)}), f32[128,16,128]{2,1,0:T(8,128)S(1)}, u32[]{:S(2)}, u32[]{:S(2)}) async-start(f32[128,16,128]{2,1,0:T(8,128)} %bitcast), calls=%async_computation | async-start | bytes 2097152 | tf_op jit(solution)/shard_map/all_to_all | solution.py:394
  15.4 0.4 pad_maximum_fusion
  15.8 1.7 constant_dynamic-slice_fusion
  17.5 0.1 copy.26
  17.5 0.7 collective-permute-start
  18.2 0.1 copy.25
  18.3 10.8 %collective-permute-start.1 = (f32[3,2,32,512]{3,2,1,0:T(8,128)S(1)}, f32[3,2,32,512]{3,2,1,0:T(8,128)S(1)}, u32[]{:S(2)}, u32[]{:S(2)}) collective-permute-start(f32[3,2,32,512]{3,2,1,0:T(8,128)S(1)} %bitcast.41), channel_id=1, source_target_pairs={{0,2},{1,124},{2,126},{3,0},{4,6},{5,120},{6,122},{7,4},{8,10},{9,... | collective-permute-start | bytes 1179656 | tf_op jit(solution)/shard_map/ppermute | solution.py:407
  29.1 0.1 copy.24
  29.1 2.3 %collective-permute-start.2 = (f32[3,2,32,512]{3,2,1,0:T(8,128)S(1)}, f32[3,2,32,512]{3,2,1,0:T(8,128)S(1)}, u32[]{:S(2)}, u32[]{:S(2)}) collective-permute-start(f32[3,2,32,512]{3,2,1,0:T(8,128)S(1)} %bitcast.40), channel_id=1, source_target_pairs={{0,124},{1,126},{2,0},{3,2},{4,120},{5,122},{6,4},{7,6},{8,116},{9... | collective-permute-start | bytes 1179656 | tf_op jit(solution)/shard_map/ppermute | solution.py:407
  31.4 0.1 copy.23
  31.5 7.2 %collective-permute-start.3 = (f32[3,2,32,512]{3,2,1,0:T(8,128)S(1)}, f32[3,2,32,512]{3,2,1,0:T(8,128)S(1)}, u32[]{:S(2)}, u32[]{:S(2)}) collective-permute-start(f32[3,2,32,512]{3,2,1,0:T(8,128)S(1)} %bitcast.39), channel_id=1, source_target_pairs={{0,126},{1,0},{2,2},{3,124},{4,122},{5,4},{6,6},{7,120},{8,118},{9... | collective-permute-start | bytes 1179656 | tf_op jit(solution)/shard_map/ppermute | solution.py:407
  38.7 0.0 collective-permute-done.own0
  38.7 0.2 collective-permute-start.4
  38.9 18.1 %collective-permute-done.1.own1 = f32[3,2,32,512]{3,2,1,0:T(8,128)S(1)} collective-permute-done((f32[3,2,32,512]{3,2,1,0:T(8,128)S(1)}, f32[3,2,32,512]{3,2,1,0:T(8,128)S(1)}, u32[]{:S(2)}, u32[]{:S(2)}) %collective-permute-start.1) | collective-permute-done | bytes 393248 | tf_op jit(solution)/shard_map/ppermute | solution.py:407
  57.0 0.0 collective-permute-start.5
  57.0 0.8 collective-permute-done.2.own2
  57.8 0.0 collective-permute-start.6
  57.8 0.0 collective-permute-done.3.own3
  57.8 0.5 collective-permute-start.7
  58.3 0.0 collective-permute-done.4.other0
  58.3 0.4 collective-permute-done.5.other1
  58.7 0.8 collective-permute-done.6.other2
  59.5 0.8 copy-done.6
  60.3 0.0 collective-permute-done.7.other3
  60.3 0.8 copy-done.9
  61.0 0.0 all-to-all-done
  61.0 1.0 copy-done.7
  62.0 1.0 copy-done.10
  63.0 0.9 copy-done.12
  64.0 2.2 %copy-done.15 = bf16[2,1024,1024]{2,1,0:T(8,128)(2,1)S(1)} copy-done((bf16[2,1024,1024]{2,1,0:T(8,128)(2,1)S(1)}, bf16[2,1024,1024]{2,1,0:T(8,128)(2,1)}, u32[]{:S(2)}) %copy-start.15) | copy-done | bytes 4194328
  66.2 1.0 copy-done.16
  67.2 13.6 %chi.1 = (f32[32,4,2,8,128]{4,3,2,1,0:T(8,128)S(1)}, f32[256,1024]{1,0:T(8,128)S(1)}) custom-call(bf16[2,512,256]{2,1,0:T(8,128)(2,1)S(1)} %copy-done.16, bf16[2,1024,1024]{2,1,0:T(8,128)(2,1)S(1)} %copy-done.15, bf16[2,1024,1024]{2,1,0:T(8,128)(2,1)} %constant.54.clone.t_out_ref, bf16[2,256,256]{2,1,0:T(8,128)(2,1)S(1)} %copy-done.12, ...), custom_call_target="tpu_custom_call" | custom-call | flops 4831838208 | bytes 12582912 | tf_op jit(solution)/shard_map/chi/pallas_call | solution.py:372
  80.8 0.0 copy-start.1
  80.8 0.0 copy-start.3
  80.8 0.0 copy-start.5
  80.8 0.0 copy-start.14
  80.9 23.2 %all_to_all.20 = f32[128,16,128]{2,1,0:T(8,128)S(1)} all-to-all(f32[128,16,128]{2,1,0:T(8,128)S(1)} %bitcast.35), channel_id=1, replica_groups=mesh['site'=32,'freq'=4] {'site','freq'}, dimensions={0} | all-to-all | bytes 2097152 | tf_op jit(solution)/shard_map/all_to_all | solution.py:394
  104.0 0.0 copy-done.3
  104.0 0.0 copy-start
  104.1 2.6 %middle.1 = f32[2048,128]{1,0:T(8,128)S(1)} custom-call(bf16[2,256,256]{2,1,0:T(8,128)(2,1)S(1)} %copy-done.1, bf16[2,256,256]{2,1,0:T(8,128)(2,1)S(1)} %copy-done.3, f32[4,2,128,128]{3,2,1,0:T(8,128)S(1)} %copy-done.5, f32[2048,128]{1,0:T(8,128)S(1)} %bitcast.29), custom_call_target="tpu_custom_call" | custom-call | flops 805306368 | bytes 3145728 | tf_op jit(solution)/shard_map/middle/pallas_call | solution.py:336
  106.6 0.0 copy-start.13
  106.6 23.2 %all_to_all.21 = f32[128,16,128]{2,1,0:T(8,128)S(1)} all-to-all(f32[128,16,128]{2,1,0:T(8,128)S(1)} %bitcast.30), channel_id=1, replica_groups=mesh['site'=32,'freq'=4] {'site','freq'}, dimensions={0} | all-to-all | bytes 2097152 | tf_op jit(solution)/shard_map/all_to_all | solution.py:394
  129.8 11.5 %sigma.1 = f32[32,4,2,8,128]{4,3,2,1,0:T(8,128)S(1)} custom-call(bf16[2,256,256]{2,1,0:T(8,128)(2,1)S(1)} %copy-done.14, bf16[2,1024,1024]{2,1,0:T(8,128)(2,1)S(1)} %copy-done, bf16[2,1024,1024]{2,1,0:T(8,128)(2,1)} %constant.57.clone.t_out_ref, bf16[2,256,256]{2,1,0:T(8,128)(2,1)S(1)} %copy-done.13, f32[32,4,2,8,128]{4,3,2,1,0:T(8,128)S(1)} %bitcast.32, ...), custom_call_target="tpu_custom_call" | custom-call | flops 3221225472 | bytes 12582912 | tf_op jit(solution)/shard_map/sigma/pallas_call | solution.py:372
  141.3 23.0 %all_to_all.22 = f32[128,16,128]{2,1,0:T(8,128)S(1)} all-to-all(f32[128,16,128]{2,1,0:T(8,128)S(1)} %bitcast.33), channel_id=1, replica_groups=mesh['site'=32,'freq'=4] {'site','freq'}, dimensions={0} | all-to-all | bytes 2097152 | tf_op jit(solution)/shard_map/all_to_all | solution.py:394
  164.4 2.1 %last.1 = f32[4,2,2,128,128]{4,3,2,1,0:T(8,128)} custom-call(bf16[2,256,256]{2,1,0:T(8,128)(2,1)S(1)} %copy-done.1, f32[2048,128]{1,0:T(8,128)S(1)} %bitcast.31), custom_call_target="tpu_custom_call" | custom-call | flops 402653184 | bytes 2359296 | tf_op jit(solution)/shard_map/last/pallas_call | solution.py:336
  (24 shorter events, 0.0 us)
Async XLA Ops:
  0.0 0.9 copy-start.2
  1.0 1.2 copy-start.4
  4.1 11.2 %copy-start.17 = (f32[32,2,4,512]{3,2,1,0:T(4,128)S(1)}, f32[32,2,4,512]{3,2,1,0:T(4,128)}, u32[]{:S(2)}) copy-start(f32[32,2,4,512]{3,2,1,0:T(4,128)} %param.17) | copy-start | bytes 1572868
  4.1 11.2 %copy-start.18 = (f32[32,2,4,512]{3,2,1,0:T(4,128)S(1)}, f32[32,2,4,512]{3,2,1,0:T(4,128)}, u32[]{:S(2)}) copy-start(f32[32,2,4,512]{3,2,1,0:T(4,128)} %param.16) | copy-start | bytes 1572868
  4.2 11.2 %copy-start.19 = (f32[32,2,4,512]{3,2,1,0:T(4,128)S(1)}, f32[32,2,4,512]{3,2,1,0:T(4,128)}, u32[]{:S(2)}) copy-start(f32[32,2,4,512]{3,2,1,0:T(4,128)} %param.15) | copy-start | bytes 1572868
  4.2 56.9 %all-to-all-start = ((f32[128,16,128]{2,1,0:T(8,128)}), f32[128,16,128]{2,1,0:T(8,128)S(1)}, u32[]{:S(2)}, u32[]{:S(2)}) async-start(f32[128,16,128]{2,1,0:T(8,128)} %bitcast), calls=%async_computation | async-start | bytes 2097152 | tf_op jit(solution)/shard_map/all_to_all | solution.py:394
  17.5 21.2 %collective-permute-start = (f32[3,2,32,512]{3,2,1,0:T(8,128)S(1)}, f32[3,2,32,512]{3,2,1,0:T(8,128)S(1)}, u32[]{:S(2)}, u32[]{:S(2)}) collective-permute-start(f32[3,2,32,512]{3,2,1,0:T(8,128)S(1)} %bitcast.42), channel_id=1, source_target_pairs={{0,0},{1,2},{2,124},{3,126},{4,4},{5,6},{6,120},{7,122},{8,8},{9,1... | collective-permute-start | bytes 1179656 | tf_op jit(solution)/shard_map/ppermute | solution.py:407
  18.3 38.7 %collective-permute-start.1 = (f32[3,2,32,512]{3,2,1,0:T(8,128)S(1)}, f32[3,2,32,512]{3,2,1,0:T(8,128)S(1)}, u32[]{:S(2)}, u32[]{:S(2)}) collective-permute-start(f32[3,2,32,512]{3,2,1,0:T(8,128)S(1)} %bitcast.41), channel_id=1, source_target_pairs={{0,2},{1,124},{2,126},{3,0},{4,6},{5,120},{6,122},{7,4},{8,10},{9,... | collective-permute-start | bytes 1179656 | tf_op jit(solution)/shard_map/ppermute | solution.py:407
  29.1 28.6 %collective-permute-start.2 = (f32[3,2,32,512]{3,2,1,0:T(8,128)S(1)}, f32[3,2,32,512]{3,2,1,0:T(8,128)S(1)}, u32[]{:S(2)}, u32[]{:S(2)}) collective-permute-start(f32[3,2,32,512]{3,2,1,0:T(8,128)S(1)} %bitcast.40), channel_id=1, source_target_pairs={{0,124},{1,126},{2,0},{3,2},{4,120},{5,122},{6,4},{7,6},{8,116},{9... | collective-permute-start | bytes 1179656 | tf_op jit(solution)/shard_map/ppermute | solution.py:407
  31.5 26.3 %collective-permute-start.3 = (f32[3,2,32,512]{3,2,1,0:T(8,128)S(1)}, f32[3,2,32,512]{3,2,1,0:T(8,128)S(1)}, u32[]{:S(2)}, u32[]{:S(2)}) collective-permute-start(f32[3,2,32,512]{3,2,1,0:T(8,128)S(1)} %bitcast.39), channel_id=1, source_target_pairs={{0,126},{1,0},{2,2},{3,124},{4,122},{5,4},{6,6},{7,120},{8,118},{9... | collective-permute-start | bytes 1179656 | tf_op jit(solution)/shard_map/ppermute | solution.py:407
  38.7 19.6 %collective-permute-start.4 = (f32[3,2,32,512]{3,2,1,0:T(8,128)S(1)}, f32[3,2,32,512]{3,2,1,0:T(8,128)S(1)}, u32[]{:S(2)}, u32[]{:S(2)}) collective-permute-start(f32[3,2,32,512]{3,2,1,0:T(8,128)S(1)} %collective-permute-done.own0), channel_id=1, source_target_pairs={{0,1},{1,0},{2,3},{3,2},{4,5},{5,4},{6,7},{7,6},{8,9},{9,8},{10,11... | collective-permute-start | bytes 1179656 | tf_op jit(solution)/shard_map/ppermute | solution.py:409
  57.0 1.7 %collective-permute-start.5 = (f32[3,2,32,512]{3,2,1,0:T(8,128)S(1)}, f32[3,2,32,512]{3,2,1,0:T(8,128)S(1)}, u32[]{:S(2)}, u32[]{:S(2)}) collective-permute-start(f32[3,2,32,512]{3,2,1,0:T(8,128)S(1)} %collective-permute-done.1.own1), channel_id=1, source_target_pairs={{0,1},{1,0},{2,3},{3,2},{4,5},{5,4},{6,7},{7,6},{8,9},{9,8},{10,11... | collective-permute-start | bytes 1179656 | tf_op jit(solution)/shard_map/ppermute | solution.py:409
  57.8 1.7 %collective-permute-start.6 = (f32[3,2,32,512]{3,2,1,0:T(8,128)S(1)}, f32[3,2,32,512]{3,2,1,0:T(8,128)S(1)}, u32[]{:S(2)}, u32[]{:S(2)}) collective-permute-start(f32[3,2,32,512]{3,2,1,0:T(8,128)S(1)} %collective-permute-done.2.own2), channel_id=1, source_target_pairs={{0,1},{1,0},{2,3},{3,2},{4,5},{5,4},{6,7},{7,6},{8,9},{9,8},{10,11... | collective-permute-start | bytes 1179656 | tf_op jit(solution)/shard_map/ppermute | solution.py:409
  57.8 2.5 %collective-permute-start.7 = (f32[3,2,32,512]{3,2,1,0:T(8,128)S(1)}, f32[3,2,32,512]{3,2,1,0:T(8,128)S(1)}, u32[]{:S(2)}, u32[]{:S(2)}) collective-permute-start(f32[3,2,32,512]{3,2,1,0:T(8,128)S(1)} %collective-permute-done.3.own3), channel_id=1, source_target_pairs={{0,1},{1,0},{2,3},{3,2},{4,5},{5,4},{6,7},{7,6},{8,9},{9,8},{10,11... | collective-permute-start | bytes 1179656 | tf_op jit(solution)/shard_map/ppermute | solution.py:409
  59.5 0.8 copy-start.6
  60.3 0.8 copy-start.9
  61.0 1.0 copy-start.7
  62.0 1.0 copy-start.10
  63.0 0.9 copy-start.12
  64.0 2.2 %copy-start.15 = (bf16[2,1024,1024]{2,1,0:T(8,128)(2,1)S(1)}, bf16[2,1024,1024]{2,1,0:T(8,128)(2,1)}, u32[]{:S(2)}) copy-start(bf16[2,1024,1024]{2,1,0:T(8,128)(2,1)} %constant.53.clone.t_in_ref) | copy-start | bytes 12582916
  66.2 1.0 copy-start.16
  80.8 23.2 %copy-start.1 = (bf16[2,256,256]{2,1,0:T(8,128)(2,1)S(1)}, bf16[2,256,256]{2,1,0:T(8,128)(2,1)}, u32[]{:S(2)}) copy-start(bf16[2,256,256]{2,1,0:T(8,128)(2,1)} %constant.50.clone.in_table_ref.table_ref) | copy-start | bytes 786436
  80.8 23.2 %copy-start.3 = (bf16[2,256,256]{2,1,0:T(8,128)(2,1)S(1)}, bf16[2,256,256]{2,1,0:T(8,128)(2,1)}, u32[]{:S(2)}) copy-start(bf16[2,256,256]{2,1,0:T(8,128)(2,1)} %constant.49.clone.table_ref.out_table_ref) | copy-start | bytes 786436
  80.8 23.2 %copy-start.5 = (f32[4,2,128,128]{3,2,1,0:T(8,128)S(1)}, f32[4,2,128,128]{3,2,1,0:T(8,128)}, u32[]{:S(2)}) copy-start(f32[4,2,128,128]{3,2,1,0:T(8,128)} %bubble_ref.1) | copy-start | bytes 1572868
  80.8 49.0 %copy-start.14 = (bf16[2,256,256]{2,1,0:T(8,128)(2,1)S(1)}, bf16[2,256,256]{2,1,0:T(8,128)(2,1)}, u32[]{:S(2)}) copy-start(bf16[2,256,256]{2,1,0:T(8,128)(2,1)} %constant.55.clone.x_in_ref) | copy-start | bytes 786436
  104.0 25.8 %copy-start = (bf16[2,1024,1024]{2,1,0:T(8,128)(2,1)S(1)}, bf16[2,1024,1024]{2,1,0:T(8,128)(2,1)}, u32[]{:S(2)}) copy-start(bf16[2,1024,1024]{2,1,0:T(8,128)(2,1)} %constant.56.clone.t_in_ref) | copy-start | bytes 12582916
  106.6 23.2 %copy-start.8 = (f32[3,2,32,512]{3,2,1,0:T(8,128)S(1)}, f32[3,2,32,512]{3,2,1,0:T(8,128)}, u32[]{:S(2)}) copy-start(f32[3,2,32,512]{3,2,1,0:T(8,128)} %copy-done.6) | copy-start | bytes 1179652
  106.6 23.2 %copy-start.11 = (f32[3,2,32,512]{3,2,1,0:T(8,128)S(1)}, f32[3,2,32,512]{3,2,1,0:T(8,128)}, u32[]{:S(2)}) copy-start(f32[3,2,32,512]{3,2,1,0:T(8,128)} %copy-done.9) | copy-start | bytes 1179652
  106.6 23.2 %copy-start.13 = (bf16[2,256,256]{2,1,0:T(8,128)(2,1)S(1)}, bf16[2,256,256]{2,1,0:T(8,128)(2,1)}, u32[]{:S(2)}) copy-start(bf16[2,256,256]{2,1,0:T(8,128)(2,1)} %constant.51.clone.x_out_ref) | copy-start | bytes 786436

commit v2 on v1

v2 whole, which is shorter than its diff:
```python
import math

import jax
import jax.numpy as jnp
import ml_dtypes
import numpy as np
from jax import lax
from jax.experimental import pallas as pl
from jax.experimental.pallas import tpu as pltpu
from jax.sharding import PartitionSpec as P

N = 128
NF = 512
BOTH = ("site", "freq")
CHIPS = 64
BF16 = jnp.bfloat16
F32 = jnp.float32


def column(chip, slab):
    site, z_hi = divmod(chip, 2)
    own = 4 * site + (z_hi if site < 16 else 2 - z_hi)
    if slab == 0:
        return own
    return (N - own) % N if own else N // 2


COLUMN = np.array([[column(chip, slab) for chip in range(CHIPS)] for slab in range(2)])


def routes(shift):
    pairs = []
    for chip in range(CHIPS):
        source = int(COLUMN[shift // 2, chip]) // 4 * 2 + (chip % 2 ^ shift % 2)
        pairs += [(2 * source + core, 2 * chip + core) for core in range(2)]
    return pairs


def phases(rows, cols, period, sign, number):
    turns = np.mod(np.outer(rows, cols), period)
    return np.exp(sign * 2j * math.pi / period * turns) / math.sqrt(number)


def real_form(matrix):
    return np.stack(
        [np.stack([matrix.real, -matrix.imag], 1), np.stack([matrix.imag, matrix.real], 1)]
    )


def split(table):
    table = table.astype(np.float32)
    high = table.astype(ml_dtypes.bfloat16)
    low = (table - high.astype(np.float32)).astype(ml_dtypes.bfloat16)
    return np.stack([high, low])


IDX = np.arange(N)
FERMI = (1 - NF) / 2
BOSE = -(NF // 2)


def y_to_columns():
    return split(real_form(phases(COLUMN.reshape(-1), IDX, N, 1, N)).reshape(256, 256))


def y_to_momenta():
    return split(real_form(phases(IDX, COLUMN.reshape(-1), N, -1, N)).reshape(256, 256))


def x_in(sign):
    return real_form(phases(IDX, IDX, N, sign, N)).transpose(0, 1, 3, 2).reshape(256, 256)


def x_in_pair():
    minus = x_in(-1).reshape(2, 128, 256) * np.array([1.0, -1.0])[:, None, None]
    return split(np.concatenate([x_in(1), minus.reshape(256, 256)]))


def x_out():
    return split(real_form(phases(IDX, IDX, N, -1, N)).transpose(1, 0, 2, 3).reshape(256, 256))


def t_phases(offset, sign, step):
    times = 4 * IDX + step
    return phases((IDX + offset), times, NF, sign, NF)


def t_in(offset, sign):
    tables = [real_form(t_phases(offset, sign, c).T).reshape(256, 256).T for c in range(4)]
    return split(np.stack(tables)).transpose(1, 0, 2, 3)


def t_out(offset, sign):
    tables = [real_form(t_phases(offset, sign, c)).reshape(256, 256).T for c in range(4)]
    return split(np.stack(tables)).transpose(1, 0, 2, 3)


def t_order():
    order = np.zeros((NF, NF), np.float32)
    place = np.arange(NF)
    order[4 * (place % N) + place // N, place] = 1
    return order.astype(ml_dtypes.bfloat16)


def dot(a, b):
    return lax.dot_general(a, b, (((1,), (0,)), ((), ())), preferred_element_type=F32)


def halves(value):
    high = value.astype(BF16)
    return high, (value - high.astype(F32)).astype(BF16)


def dot3(a_high, a_low, b_high, b_low):
    return dot(a_high, b_high) + (dot(a_high, b_low) + dot(a_low, b_high))


def slab_rows(core, slab, row):
    return pl.ds((core * 2 + slab) * 8 + row, CHIPS, stride=32)


def store_columns(result, core, out_ref):
    for slab in range(2):
        for kx in range(4):
            for part in range(2):
                top = part * 128 + slab * CHIPS
                out_ref[slab_rows(core, slab, kx * 2 + part), :] = result[
                    top : top + CHIPS, kx * 128 : kx * 128 + 128
                ]


def load_columns(core, in_ref):
    blocks = []
    for kx in range(4):
        pieces = []
        for part in range(2):
            for slab in range(2):
                pieces.append(in_ref[slab_rows(core, slab, kx * 2 + part), :])
        blocks.append(jnp.concatenate(pieces, axis=0))
    return jnp.concatenate(blocks, axis=1)


def fetch(source, target, sem):
    copy = pltpu.make_async_copy(source, target, sem)
    copy.start()
    return copy.wait


def first_kernel(table_hbm, green_hbm, out_ref, table_ref, green_ref, sems):
    table_here = fetch(table_hbm, table_ref, sems.at[0])
    green_here = [
        fetch(green_hbm.at[:, tangent], green_ref.at[tangent], sems.at[1 + tangent])
        for tangent in range(2)
    ]
    for tangent in range(2):
        green_here[tangent]()
        source = jnp.concatenate(
            [green_ref[tangent, kx].reshape(256, 128) for kx in range(4)], axis=1
        )
        high, low = halves(source)
        if tangent == 0:
            table_here()
        result = dot3(table_ref[0], table_ref[1], high, low)
        store_columns(result, tangent, out_ref)


def inverse_square(real_part, imag_part):
    scale = 1.0 / (real_part * real_part + imag_part * imag_part)
    inv_real = real_part * scale
    inv_imag = -imag_part * scale
    return (inv_real * inv_real - inv_imag * inv_imag, 2.0 * inv_real * inv_imag)


def middle_kernel(
    in_table_hbm, out_table_hbm, bubble_hbm, in_ref, out_ref,
    in_table_ref, out_table_ref, bubble_ref, sems,
):
    bubble_here = fetch(bubble_hbm, bubble_ref, sems.at[0])
    in_table_here = fetch(in_table_hbm, in_table_ref, sems.at[1])
    out_table_here = fetch(out_table_hbm, out_table_ref, sems.at[2])
    columns = [halves(load_columns(core, in_ref)) for core in range(2)]
    bubble_here()
    weight_real, weight_imag = [], []
    for kx in range(4):
        chi_real = bubble_ref[kx, 0]
        chi_imag = bubble_ref[kx, 1]
        spin_real, spin_imag = inverse_square(1.0 - chi_real, -chi_imag)
        charge_real, charge_imag = inverse_square(1.0 + chi_real, chi_imag)
        weight_real.append(1.5 * spin_real + 0.5 * charge_real - 1.0)
        weight_imag.append(1.5 * spin_imag + 0.5 * charge_imag)
    weight_real = jnp.concatenate(weight_real, axis=1)
    weight_imag = jnp.concatenate(weight_imag, axis=1)
    for core in range(2):
        high, low = columns[core]
        if core == 0:
            in_table_here()
        chi = dot3(in_table_ref[0], in_table_ref[1], high, low)
        real, imag = chi[:128], chi[128:]
        pot = jnp.concatenate(
            [
                weight_real * real - weight_imag * imag,
                weight_real * imag + weight_imag * real,
            ],
            axis=0,
        )
        high, low = halves(pot)
        if core == 0:
            out_table_here()
        result = dot3(out_table_ref[0], out_table_ref[1], high, low)
        store_columns(result, core, out_ref)


def last_kernel(table_hbm, in_ref, out_hbm, table_ref, out_ref, sems):
    table_here = fetch(table_hbm, table_ref, sems.at[0])
    sent = []
    for core in range(2):
        high, low = halves(load_columns(core, in_ref))
        if core == 0:
            table_here()
        result = dot3(table_ref[0], table_ref[1], high, low)
        for kx in range(4):
            for part in range(2):
                out_ref[core, kx, part] = result[
                    part * 128 : part * 128 + 128, kx * 128 : kx * 128 + 128
                ]
        sent.append(fetch(out_ref.at[core], out_hbm.at[:, core], sems.at[1 + core]))
    for gone in sent:
        gone()


def place_of(place):
    freq = lax.axis_index("freq")
    shift, swapped = place % 4, place // 4
    return shift // 2, lax.bitwise_xor(freq, 2 * (shift % 2) + swapped)


def gather_slab(in_ref, slot):
    return jnp.concatenate(
        [in_ref[:, freq, slot].reshape(256, 128) for freq in range(4)], axis=1
    )


def turned(real, imag, quarter):
    return ((real, imag), (-imag, real), (-real, -imag), (imag, -real))[quarter % 4]


def to_left(result, rows, left_ref):
    for high in range(4):
        lanes = slice(high * 128, high * 128 + 128)
        left_ref[high, rows, :] = jnp.concatenate(
            [result[:128, lanes], result[128:, lanes]], axis=1
        )


def to_times(step, left_ref, t_in_ref, sign):
    real, imag = left_ref[0, :, :128], left_ref[0, :, 128:]
    for high in range(1, 4):
        more = turned(left_ref[high, :, :128], left_ref[high, :, 128:], sign * high * step)
        real, imag = real + more[0], imag + more[1]
    first, second = halves(jnp.concatenate([real, imag], axis=1))
    return dot3(first, second, t_in_ref[step, 0], t_in_ref[step, 1])


def finish(x_out_ref, acc_ref, out_ref):
    for slab in range(2):
        rows = slice(slab * 128, slab * 128 + 128)
        source = jnp.concatenate(
            [
                jnp.concatenate([acc_ref[high, rows, :128] for high in range(4)], axis=1),
                jnp.concatenate([acc_ref[high, rows, 128:] for high in range(4)], axis=1),
            ],
            axis=0,
        )
        high, low = halves(source)
        result = dot3(x_out_ref[0], x_out_ref[1], high, low)
        for freq in range(4):
            out_ref[:, freq, slab] = result[:, freq * 128 : freq * 128 + 128].reshape(32, 8, 128)


def accumulate(step, first, second, t_out_ref, acc_ref):
    update = dot3(first, second, t_out_ref[step, 0], t_out_ref[step, 1])
    real, imag = update[:, :128], update[:, 128:]
    for high in range(4):
        if step:
            acc_ref[high] += jnp.concatenate(turned(real, imag, high * step), axis=1)
        else:
            acc_ref[high] = update


def prepare_kernel(order_hbm, *refs):
    pieces, (out_hbm, order_ref, out_ref, sems) = refs[:8], refs[8:]
    order_here = fetch(order_hbm, order_ref, sems.at[0])
    for place, ref in enumerate(pieces):
        arrays = ref.shape[0]
        value = ref[...].reshape(arrays * 64, NF)
        first = value.astype(BF16)
        rest = value - first.astype(F32)
        second, third = halves(rest)
        if place == 0:
            order_here()
        order = order_ref[...]
        moved = (dot(first, order) + dot(second, order)) + dot(third, order)
        slab, block = place_of(place)
        rows = pl.ds(pl.multiple_of(slab * 128 + block * 32, 32), 32)
        for array in range(arrays):
            for part in range(2):
                top = (array * 2 + part) * 32
                out_ref[array, part, rows, :] = moved[top : top + 32]
    fetch(out_ref, out_hbm, sems.at[1])()


def time_lanes(step, width):
    return pl.ds(step * width, width)


def fetch_fields(field_hbm, field_ref, sems):
    return [
        fetch(
            field_hbm.at[pl.ds(0, field_ref.shape[0]), :, :, time_lanes(step, 128)],
            field_ref.at[:, :, :, time_lanes(step, 128)],
            sems.at[step],
        )
        for step in range(4)
    ]


def fetch_tables(hbm_refs, refs, sems):
    return [fetch(hbm, ref, sems.at[place]) for place, (hbm, ref) in enumerate(zip(hbm_refs, refs))]


def chi_kernel(*refs):
    tables_hbm, in_ref, base_hbm, out_ref, plus_hbm = refs[:4], *refs[4:8]
    tables, (base_ref, plus_ref, left_ref, acc_ref, sems, base_sems, plus_sems) = refs[8:12], refs[12:]
    x_in_ref, t_in_ref, t_out_ref, x_out_ref = tables
    x_in_here, t_in_here, t_out_here, x_out_here = fetch_tables(tables_hbm, tables, sems)
    base_here = fetch_fields(base_hbm, base_ref, base_sems)
    site, freq = lax.axis_index("site"), lax.axis_index("freq")
    alone = jnp.logical_and(site == 0, freq < 2)

    for slab in range(2):
        high, low = halves(gather_slab(in_ref, slab))
        if slab == 0:
            x_in_here()
        result = dot3(x_in_ref[0], x_in_ref[1], high, low)
        to_left(result[:256], pl.ds(slab * 128, 128), left_ref)
        image = jnp.where(alone, slab, 1 - slab)
        rows = pl.ds(pl.multiple_of(256 + image * 128, 128), 128)
        to_left(result[256:], rows, left_ref)

    t_in_here()
    plus_gone = []
    for step in range(4):
        times = to_times(step, left_ref, t_in_ref, -1)
        plus, minus = times[:256], times[256:]
        lanes = time_lanes(step, 256)
        plus_ref[:, lanes] = plus
        plus_gone.append(fetch(plus_ref.at[:, lanes], plus_hbm.at[:, lanes], plus_sems.at[step]))
        plus_real, plus_imag = plus[:, :128], plus[:, 128:]
        minus_real, minus_imag = minus[:, :128], -minus[:, 128:]
        base_here[step]()
        block = time_lanes(step, 128)
        base_real, base_imag = base_ref[0, 0, :, block], base_ref[0, 1, :, block]
        mirror_real, mirror_imag = base_ref[1, 0, :, block], base_ref[1, 1, :, block]
        chi_real = (
            plus_real * mirror_real - plus_imag * mirror_imag
            + base_real * minus_real - base_imag * minus_imag
        )
        chi_imag = (
            plus_real * mirror_imag + plus_imag * mirror_real
            + base_real * minus_imag + base_imag * minus_real
        )
        first, second = halves(-jnp.concatenate([chi_real, chi_imag], axis=1))
        if step == 0:
            t_out_here()
        accumulate(step, first, second, t_out_ref, acc_ref)
    x_out_here()
    finish(x_out_ref, acc_ref, out_ref)
    for gone in plus_gone:
        gone()


def sigma_kernel(*refs):
    tables_hbm, (in_ref, base_hbm, pot_hbm, plus_hbm, out_ref) = refs[:4], refs[4:9]
    tables, refs = refs[9:13], refs[13:]
    base_ref, pot_ref, plus_ref, left_ref, acc_ref, sems, base_sems, pot_sems, plus_sem = refs
    x_in_ref, t_in_ref, t_out_ref, x_out_ref = tables
    x_in_here, t_in_here, t_out_here, x_out_here = fetch_tables(tables_hbm, tables, sems)
    plus_here = fetch(plus_hbm, plus_ref, plus_sem.at[0])
    base_here = fetch_fields(base_hbm, base_ref, base_sems)
    pot_here = fetch_fields(pot_hbm, pot_ref, pot_sems)

    for slab in range(2):
        high, low = halves(gather_slab(in_ref, slab))
        if slab == 0:
            x_in_here()
        result = dot3(x_in_ref[0], x_in_ref[1], high, low)
        to_left(result, pl.ds(slab * 128, 128), left_ref)

    t_in_here()
    for step in range(4):
        change = to_times(step, left_ref, t_in_ref, -1)
        if step == 0:
            plus_here()
        base_here[step]()
        pot_here[step]()
        plus = plus_ref[:, time_lanes(step, 256)]
        block = time_lanes(step, 128)
        change_real, change_imag = change[:, :128], change[:, 128:]
        plus_real, plus_imag = plus[:, :128], plus[:, 128:]
        base_real, base_imag = base_ref[0, 0, :, block], base_ref[0, 1, :, block]
        pot_real, pot_imag = pot_ref[0, 0, :, block], pot_ref[0, 1, :, block]
        real = (
            pot_real * plus_real - pot_imag * plus_imag
            + change_real * base_real - change_imag * base_imag
        )
        imag = (
            pot_real * plus_imag + pot_imag * plus_real
            + change_real * base_imag + change_imag * base_real
        )
        first, second = halves(jnp.concatenate([real, imag], axis=1))
        if step == 0:
            t_out_here()
        accumulate(step, first, second, t_out_ref, acc_ref)
    x_out_here()
    finish(x_out_ref, acc_ref, out_ref)


PARAMS = pltpu.CompilerParams(vmem_limit_bytes=24 * 1024 * 1024)
WORK = 3 << 31
HBM = pl.BlockSpec(memory_space=pltpu.HBM)
HERE = pl.BlockSpec(memory_space=pltpu.VMEM)


def call(body, name, in_specs, out_specs, out_shape, scratch, flops, *operands):
    size = sum(operand.size * operand.dtype.itemsize for operand in operands)
    return pl.pallas_call(
        body,
        in_specs=in_specs,
        out_specs=out_specs,
        out_shape=[
            pltpu.HBM(shape, F32) if spec is HBM else jax.ShapeDtypeStruct(shape, F32)
            for shape, spec in zip(out_shape, out_specs)
        ],
        scratch_shapes=scratch,
        compiler_params=PARAMS,
        cost_estimate=pl.CostEstimate(flops=flops, bytes_accessed=size, transcendentals=0),
        name=name,
    )(*[
        pltpu.with_memory_space_constraint(operand, pltpu.HBM) if spec is HBM else operand
        for operand, spec in zip(operands, in_specs)
    ])


def like(array):
    return pltpu.VMEM(array.shape, array.dtype)


def sems(number):
    return pltpu.SemaphoreType.DMA((number,))


SLABS = (32, 4, 2, 8, 128)
TURN = 2 * 3 * 256 * 256 * 1024


def first_call(table, green):
    scratch = [like(table), pltpu.VMEM((2, 4, 2, 128, 128), F32), sems(3)]
    return call(
        first_kernel, "first", [HBM, HBM], [HERE], [(2048, 128)], scratch, TURN, table, green
    )[0]


def middle_call(momenta, columns, bubble, held):
    scratch = [like(momenta), like(columns), like(bubble), sems(3)]
    return call(
        middle_kernel, "middle", [HBM, HBM, HBM, HERE], [HERE], [(2048, 128)], scratch, 2 * TURN,
        momenta, columns, bubble, held,
    )[0]


def last_call(table, held):
    shape = (4, 2, 2, 128, 128)
    scratch = [like(table), pltpu.VMEM((2, 4, 2, 128, 128), F32), sems(3)]
    return call(last_kernel, "last", [HBM, HERE], [HBM], [shape], scratch, TURN, table, held)[0]


def prepare_call(pieces):
    shape = (pieces[0].shape[0], 2, 256, NF)
    order = jnp.asarray(t_order())
    scratch = [like(order), pltpu.VMEM(shape, F32), sems(2)]
    return call(
        prepare_kernel, "prepare", [HBM] + [HERE] * 8, [HBM], [shape], scratch, WORK, order, *pieces
    )[0]


def field(arrays):
    return pltpu.VMEM((arrays, 2, 256, NF), F32)


PLUS = (256, 1024)


def chi_call(tables, held, base):
    scratch = [
        *map(like, tables), field(2), pltpu.VMEM(PLUS, F32), pltpu.VMEM((4, 512, 256), F32),
        pltpu.VMEM((4, 256, 256), F32), sems(4), sems(4), sems(4),
    ]
    return call(
        chi_kernel, "chi", [HBM] * 4 + [HERE, HBM], [HERE, HBM], [SLABS, PLUS], scratch, 7 * TURN,
        *tables, held.reshape(SLABS), base,
    )


def sigma_call(tables, held, base, pot, plus):
    scratch = [
        *map(like, tables), field(1), field(1), pltpu.VMEM(PLUS, F32),
        pltpu.VMEM((4, 256, 256), F32), pltpu.VMEM((4, 256, 256), F32), sems(4), sems(4), sems(4), sems(1),
    ]
    return call(
        sigma_kernel, "sigma", [HBM] * 4 + [HERE, HBM, HBM, HBM], [HERE], [SLABS], scratch, 4 * TURN,
        *tables, held.reshape(SLABS), base, pot, plus,
    )[0]


def exchange(source):
    source = source.reshape(128, 16, 128)
    return lax.all_to_all(source, BOTH, split_axis=0, concat_axis=0, tiled=True)


def pack(arrays):
    site, freq = lax.axis_index("site"), lax.axis_index("freq")
    z_hi = freq // 2
    low = (z_hi, 1 - z_hi, 2 + z_hi, 3 - z_hi)
    high = (2 - z_hi, 1 + z_hi, 3 * z_hi, 3 - 3 * z_hi)
    stacked = jnp.stack([array.transpose(2, 1, 0, 3) for array in arrays], axis=1)
    return [
        lax.dynamic_index_in_dim(stacked, jnp.where(site < 16, low[k], high[k]), 0, keepdims=False)
        for k in range(4)
    ]


def send(rows):
    return [rows[0]] + [lax.ppermute(rows[shift], BOTH, routes(shift)) for shift in (1, 2, 3)]


def both_cores(own):
    return own + [lax.ppermute(piece, "freq", [(f, f ^ 1) for f in range(4)]) for piece in own]


def local(green_tangent, green_plus, green_mirror, potential, bubble):
    base = prepare_call(both_cores(send(pack([green_plus, green_mirror]))))
    columns, momenta = jnp.asarray(y_to_columns()), jnp.asarray(y_to_momenta())
    back = jnp.asarray(x_out())
    chi_tables = (
        jnp.asarray(x_in_pair()), jnp.asarray(t_in(FERMI, -1)), jnp.asarray(t_out(BOSE, 1)), back
    )
    sigma_tables = (
        jnp.asarray(split(x_in(1))), jnp.asarray(t_in(BOSE, -1)), jnp.asarray(t_out(FERMI, 1)), back
    )
    sent = first_call(columns, green_tangent)
    potential, sent = lax.optimization_barrier((potential, sent))
    held = exchange(sent)
    sent, plus = chi_call(chi_tables, held, base)
    potential, sent = lax.optimization_barrier((potential, sent))
    own = send(pack([potential]))
    held = exchange(sent).reshape(2048, 128)
    sent = middle_call(momenta, columns, bubble, held)
    own, sent = lax.optimization_barrier((own, sent))
    pot = prepare_call(both_cores(own))
    held = exchange(sent)
    sent = sigma_call(sigma_tables, held, base, pot, plus)
    held = exchange(sent).reshape(2048, 128)
    return last_call(momenta, held)


def solution(mesh):
    in_specs = (
        P("site", None, None, None, "freq"),
        P("freq", None, "site", None),
        P("freq", None, "site", None),
        P("freq", None, "site", None),
        P("site", None, None, "freq"),
    )
    out_specs = P("site", None, None, None, "freq")
    return jax.shard_map(local, mesh=mesh, in_specs=in_specs, out_specs=out_specs, check_vma=False)
```

time: 167 us -> 138 us (0.83)
  blocking collectives: 69.4 us -> 23 us
  waiting for transfers between devices: 20.1 us -> 38 us
  local copies, waits for them, and re-layouts: 11.9 us -> 0.57 us
  starting transfers between devices: 32.8 us -> 41.4 us
  other arithmetic: 0.41 us -> 3.85 us
    all_to_all x3 -> x1, blocking collectives: 69.4 us -> 23 us  [exchange(): return lax.all_to_all(source, BOTH, split_axis=0, concat_axis=0, tiled=True)]
    all_to_all x1 -> x3, waiting for transfers between devices: 0.01 us -> 31 us  [exchange(): return lax.all_to_all(source, BOTH, split_axis=0, concat_axis=0, tiled=True)]
    ppermute x8 -> x14, waiting for transfers between devices: 20.1 us -> 7.01 us  [the longest x6 4.59 us: send(): lax.ppermute(rows[shift], BOTH, routes(shift))]
    unnamed x40 -> x2, local copies, waits for them, and re-layouts: 9.92 us -> 0.01 us
    all_to_all x1 -> x3, starting transfers between devices: 11.1 us -> 19.4 us  [exchange(): return lax.all_to_all(source, BOTH, split_axis=0, concat_axis=0, tiled=True)]
    another operation x1, other arithmetic: 0.41 us -> 3.85 us  [pack(): jnp.stack([array.transpose(2, 1, 0, 3) for array in arrays], axis=1)]
    dynamic_slice x5 -> x4, local copies, waits for them, and re-layouts: 1.95 us -> 0.21 us  [pack(): lax.dynamic_index_in_dim(stacked, jnp.where(site < 16, low[k], high[k]),...]
    pallas_call x5 -> x7, Pallas kernels: 31.7 us -> 30.6 us  [call(): pl.pallas_call(body, in_specs=in_specs, out_specs=out_specs, out_shape=[p...]
  transfers between devices with their start and end apart: 9 -> 17, of which waited for: 4 -> 11; matrix products, arithmetic and copies ran while one was open for 1% -> 0% of each run, Pallas kernels for 0% -> 12%
where the time goes in v2:
time: 138 us
  starting transfers between devices  41.4 us (30%)
  waiting for transfers between devices  38 us (28%)
  Pallas kernels  30.6 us (22%)
  blocking collectives  23 us (17%)
  other arithmetic  3.85 us (3%)
    all_to_all x3, waiting for transfers between devices, exchange(): return lax.all_to_all(source, BOTH, split_axis=0, concat_axis=0, tiled=True)  31 us
    pallas_call x7, Pallas kernels, call(): pl.pallas_call(body, in_specs=in_specs, out_specs=out_specs, out_shape=[p...  30.6 us
    all_to_all x1, blocking collectives, exchange(): return lax.all_to_all(source, BOTH, split_axis=0, concat_axis=0, tiled=True)  23 us
    ppermute x6, starting transfers between devices, send(): lax.ppermute(rows[shift], BOTH, routes(shift))  19.8 us
    all_to_all x3, starting transfers between devices, exchange(): return lax.all_to_all(source, BOTH, split_axis=0, concat_axis=0, tiled=True)  19.4 us
    ppermute x6, waiting for transfers between devices, send(): lax.ppermute(rows[shift], BOTH, routes(shift))  4.59 us
    another operation x1, other arithmetic, pack(): jnp.stack([array.transpose(2, 1, 0, 3) for array in arrays], axis=1)  3.85 us
  transfers between devices with their start and end apart: 17, of which 11 were waited for; matrix products, arithmetic and copies ran while one was open for 0% of the time, Pallas kernels for 12%

profile of v2, /device:TPU:0, one launch (start us, length us, event | category | flops | bytes accessed | tf_op | source)
XLA Modules:
  0.0 137.7 jit_solution(14130792839447441155)
XLA Ops:
  0.0 3.9 %fusion = (f32[1,2,2,32,512]{4,0,2,3,1:T(1,128)S(1)}, f32[1,2,2,32,512]{4,0,2,3,1:T(1,128)S(1)}, f32[1,2,2,32,512]{4,0,2,3,1:T(1,128)S(1)}, f32[1,2,2,32,512]{4,0,2,3,1:T(1,128)S(1)}) fusion(s32[]{:T(128)S(6)} %select_n.48, f32[4,1,2,32,512]{4,0,2,3,1:T(4,128)} %bitcast.41, f32[4,1,2,32,512]{4,0,2,3,1:T(4,128)} %bitcast.42, s32[]{:T(128)S(6)} %select_n.42, ...), kind=kLoop, calls=%fused_computation.8 | loop fusion | flops 262144 | bytes 2097168 | tf_op jit(solution)/shard_map/stack | solution.py:535
  3.9 0.1 copy.30
  3.9 6.7 %collective-permute-start.1 = (f32[2,2,32,512]{3,2,1,0:T(8,128)S(1)}, f32[2,2,32,512]{3,2,1,0:T(8,128)S(1)}, u32[]{:S(2)}, u32[]{:S(2)}) collective-permute-start(f32[2,2,32,512]{3,2,1,0:T(8,128)S(1)} %bitcast.45), channel_id=1, source_target_pairs={{64,0},{65,1},{126,2},{127,3},{124,4},{125,5},{122,6},{123,7},{120... | collective-permute-start | bytes 786440 | tf_op jit(solution)/shard_map/ppermute | solution.py:543
  10.6 0.1 copy.31
  10.7 3.7 %collective-permute-start = (f32[2,2,32,512]{3,2,1,0:T(8,128)S(1)}, f32[2,2,32,512]{3,2,1,0:T(8,128)S(1)}, u32[]{:S(2)}, u32[]{:S(2)}) collective-permute-start(f32[2,2,32,512]{3,2,1,0:T(8,128)S(1)} %bitcast.44), channel_id=1, source_target_pairs={{2,0},{3,1},{0,2},{1,3},{6,4},{7,5},{4,6},{5,7},{10,8},{11,9},{8,1... | collective-permute-start | bytes 786440 | tf_op jit(solution)/shard_map/ppermute | solution.py:543
  14.4 0.1 copy.29
  14.4 0.1 collective-permute-start.2
  14.5 3.4 %first.1 = f32[2048,128]{1,0:T(8,128)} custom-call(bf16[2,256,256]{2,1,0:T(8,128)(2,1)} %constant.73.clone.table_hbm.out_table_hbm, f32[4,2,2,128,128]{4,3,2,1,0:T(8,128)} %green_hbm.1), custom_call_target="tpu_custom_call" | custom-call | flops 402653184 | bytes 1310720 | tf_op jit(solution)/shard_map/first/pallas_call | solution.py:436
  17.9 9.0 %all-to-all-start = ((f32[128,16,128]{2,1,0:T(8,128)}), f32[128,16,128]{2,1,0:T(8,128)S(1)}, u32[]{:S(2)}, u32[]{:S(2)}) async-start(f32[128,16,128]{2,1,0:T(8,128)} %bitcast), calls=%async_computation | async-start | bytes 2097152 | tf_op jit(solution)/shard_map/all_to_all | solution.py:527
  27.0 0.1 copy.32
  27.0 0.1 collective-permute-start.3
  27.1 0.0 collective-permute-done.1.refs_2_
  27.2 0.5 collective-permute-start.5
  27.6 3.6 %collective-permute-done.refs_1_ = f32[2,2,32,512]{3,2,1,0:T(8,128)S(1)} collective-permute-done((f32[2,2,32,512]{3,2,1,0:T(8,128)S(1)}, f32[2,2,32,512]{3,2,1,0:T(8,128)S(1)}, u32[]{:S(2)}, u32[]{:S(2)}) %collective-permute-start) | collective-permute-done | bytes 262176 | tf_op jit(solution)/shard_map/ppermute | solution.py:543
  31.2 0.0 collective-permute-start.4
  31.2 0.0 collective-permute-done.2.refs_3_
  31.2 0.5 collective-permute-start.6
  31.8 0.0 collective-permute-done.3.refs_4_
  31.8 0.0 collective-permute-done.5.refs_6_
  31.8 1.0 collective-permute-done.4.refs_5_
  32.8 0.4 collective-permute-done.6.refs_7_
  33.1 4.2 %prepare.2.refs_5_ = f32[2,2,256,512]{3,2,1,0:T(8,128)} custom-call(bf16[512,512]{1,0:T(8,128)(2,1)} %constant.72.clone.order_hbm, f32[2,2,32,512]{3,2,1,0:T(8,128)S(1)} %bitcast.40, f32[2,2,32,512]{3,2,1,0:T(8,128)S(1)} %collective-permute-done.refs_1_, f32[2,2,32,512]{3,2,1,0:T(8,128)S(1)} %collective-permute-done.1.refs_2_, ...), custom_call_target="tpu_custom_call" | custom-call | flops 6442450944 | bytes 2621440 | tf_op jit(solution)/shard_map/prepare/pallas_call | solution.py:436
  37.3 8.7 %all-to-all-done = f32[128,16,128]{2,1,0:T(8,128)S(1)} async-done(((f32[128,16,128]{2,1,0:T(8,128)}), f32[128,16,128]{2,1,0:T(8,128)S(1)}, u32[]{:S(2)}, u32[]{:S(2)}) %all-to-all-start) | async-done | bytes 1048608 | tf_op jit(solution)/shard_map/all_to_all | solution.py:527
  46.0 7.2 %chi.1 = (f32[32,4,2,8,128]{4,3,2,1,0:T(8,128)}, f32[256,1024]{1,0:T(8,128)}) custom-call(bf16[2,512,256]{2,1,0:T(8,128)(2,1)} %constant.76.clone.refs_0_, bf16[4,2,256,256]{3,2,1,0:T(8,128)(2,1)} %constant.77.clone.refs_1_, bf16[4,2,256,256]{3,2,1,0:T(8,128)(2,1)} %constant.78.clone.refs_2_, bf16[2,256,256]{2,1,0:T(8,128)(2,1)} %constant.75.clone.refs_3_, ...), custom_call_target="tpu_custom_call" | custom-call | flops 2818572288 | bytes 6029312 | tf_op jit(solution)/shard_map/chi/pallas_call | solution.py:436
  53.2 0.0 copy-start
  53.2 4.8 %all-to-all-start.1 = ((f32[128,16,128]{2,1,0:T(8,128)}), f32[128,16,128]{2,1,0:T(8,128)S(1)}, u32[]{:S(2)}, u32[]{:S(2)}) async-start(f32[128,16,128]{2,1,0:T(8,128)} %bitcast.14), calls=%async_computation.1 | async-start | bytes 2097152 | tf_op jit(solution)/shard_map/all_to_all | solution.py:527
  58.0 0.3 copy.21
  58.4 7.4 %collective-permute-start.9 = (f32[1,2,32,512]{3,2,1,0:T(8,128)S(1)}, f32[1,2,32,512]{3,2,1,0:T(8,128)S(1)}, u32[]{:S(2)}, u32[]{:S(2)}) collective-permute-start(f32[1,2,32,512]{3,2,1,0:T(8,128)S(1)} %get-tuple-element.31), channel_id=1, source_target_pairs={{66,0},{67,1},{124,2},{125,3},{126,4},{127,5},{120,6},{121,7},{122... | collective-permute-start | bytes 393224 | tf_op jit(solution)/shard_map/ppermute | solution.py:543
  65.8 0.0 collective-permute-start.8
  65.8 1.9 %collective-permute-start.7 = (f32[1,2,32,512]{3,2,1,0:T(8,128)S(1)}, f32[1,2,32,512]{3,2,1,0:T(8,128)S(1)}, u32[]{:S(2)}, u32[]{:S(2)}) collective-permute-start(f32[1,2,32,512]{3,2,1,0:T(8,128)S(1)} %get-tuple-element.33), channel_id=1, source_target_pairs={{2,0},{3,1},{0,2},{1,3},{6,4},{7,5},{4,6},{5,7},{10,8},{11,9},{8,1... | collective-permute-start | bytes 393224 | tf_op jit(solution)/shard_map/ppermute | solution.py:543
  67.7 9.7 %all-to-all-done.1 = f32[128,16,128]{2,1,0:T(8,128)S(1)} async-done(((f32[128,16,128]{2,1,0:T(8,128)}), f32[128,16,128]{2,1,0:T(8,128)S(1)}, u32[]{:S(2)}, u32[]{:S(2)}) %all-to-all-start.1) | async-done | bytes 1048608 | tf_op jit(solution)/shard_map/all_to_all | solution.py:527
  77.4 4.2 %middle.1 = f32[2048,128]{1,0:T(8,128)} custom-call(bf16[2,256,256]{2,1,0:T(8,128)(2,1)} %constant.74.clone.in_table_hbm.table_hbm, bf16[2,256,256]{2,1,0:T(8,128)(2,1)} %constant.73.clone.table_hbm.out_table_hbm, f32[4,2,128,128]{3,2,1,0:T(8,128)} %bubble_hbm.1, f32[2048,128]{1,0:T(8,128)S(1)} %bitcast.35), custom_call_target="tpu_custom_call" | custom-call | flops 805306368 | bytes 2097152 | tf_op jit(solution)/shard_map/middle/pallas_call | solution.py:436
  81.6 0.0 collective-permute-done.9.refs_3_
  81.6 1.0 collective-permute-done.7.refs_1_
  82.6 5.6 %all-to-all-start.2 = ((f32[128,16,128]{2,1,0:T(8,128)}), f32[128,16,128]{2,1,0:T(8,128)S(1)}, u32[]{:S(2)}, u32[]{:S(2)}) async-start(f32[128,16,128]{2,1,0:T(8,128)} %bitcast.16), calls=%async_computation.2 | async-start | bytes 2097152 | tf_op jit(solution)/shard_map/all_to_all | solution.py:527
  88.2 0.1 collective-permute-start.10
  88.3 0.5 collective-permute-start.11
  88.8 0.1 collective-permute-start.12
  88.9 0.4 collective-permute-start.13
  89.3 0.3 collective-permute-done.10.refs_4_
  89.6 0.2 collective-permute-done.11.refs_5_
  89.8 0.3 collective-permute-done.12.refs_6_
  90.1 0.2 collective-permute-done.13.refs_7_
  90.3 4.3 %prepare.3.refs_6_ = f32[1,2,256,512]{3,2,1,0:T(8,128)} custom-call(bf16[512,512]{1,0:T(8,128)(2,1)} %constant.72.clone.order_hbm, f32[1,2,32,512]{3,2,1,0:T(8,128)S(1)} %get-tuple-element.22.refs_0_, f32[1,2,32,512]{3,2,1,0:T(8,128)S(1)} %collective-permute-done.7.refs_1_, f32[1,2,32,512]{3,2,1,0:T(8,128)S(1)} %collective-permute-done.8.refs_2_, ...), custom_call_target="tpu_custom_call" | custom-call | flops 6442450944 | bytes 1572864 | tf_op jit(solution)/shard_map/prepare/pallas_call | solution.py:436
  94.6 12.6 %all-to-all-done.2 = f32[128,16,128]{2,1,0:T(8,128)S(1)} async-done(((f32[128,16,128]{2,1,0:T(8,128)}), f32[128,16,128]{2,1,0:T(8,128)S(1)}, u32[]{:S(2)}, u32[]{:S(2)}) %all-to-all-start.2) | async-done | bytes 1048608 | tf_op jit(solution)/shard_map/all_to_all | solution.py:527
  107.2 4.7 %sigma.1 = f32[32,4,2,8,128]{4,3,2,1,0:T(8,128)S(1)} custom-call(bf16[2,256,256]{2,1,0:T(8,128)(2,1)} %constant.79.clone.refs_0_, bf16[4,2,256,256]{3,2,1,0:T(8,128)(2,1)} %constant.80.clone.refs_1_, bf16[4,2,256,256]{3,2,1,0:T(8,128)(2,1)} %constant.81.clone.refs_2_, bf16[2,256,256]{2,1,0:T(8,128)(2,1)} %constant.75.clone.refs_3_, ...), custom_call_target="tpu_custom_call" | custom-call | flops 1610612736 | bytes 7864320 | tf_op jit(solution)/shard_map/sigma/pallas_call | solution.py:436
  112.0 23.0 %all_to_all.20 = f32[128,16,128]{2,1,0:T(8,128)S(1)} all-to-all(f32[128,16,128]{2,1,0:T(8,128)S(1)} %bitcast.36), channel_id=1, replica_groups=mesh['site'=32,'freq'=4] {'site','freq'}, dimensions={0} | all-to-all | bytes 2097152 | tf_op jit(solution)/shard_map/all_to_all | solution.py:527
  135.0 2.6 %last.1 = f32[4,2,2,128,128]{4,3,2,1,0:T(8,128)} custom-call(bf16[2,256,256]{2,1,0:T(8,128)(2,1)} %constant.74.clone.in_table_hbm.table_hbm, f32[2048,128]{1,0:T(8,128)S(1)} %bitcast.37), custom_call_target="tpu_custom_call" | custom-call | flops 402653184 | bytes 1310720 | tf_op jit(solution)/shard_map/last/pallas_call | solution.py:436
  (3 shorter events, 0.1 us)
Async XLA Ops:
  3.9 23.2 %collective-permute-start.1 = (f32[2,2,32,512]{3,2,1,0:T(8,128)S(1)}, f32[2,2,32,512]{3,2,1,0:T(8,128)S(1)}, u32[]{:S(2)}, u32[]{:S(2)}) collective-permute-start(f32[2,2,32,512]{3,2,1,0:T(8,128)S(1)} %bitcast.45), channel_id=1, source_target_pairs={{64,0},{65,1},{126,2},{127,3},{124,4},{125,5},{122,6},{123,7},{120... | collective-permute-start | bytes 786440 | tf_op jit(solution)/shard_map/ppermute | solution.py:543
  10.7 20.6 %collective-permute-start = (f32[2,2,32,512]{3,2,1,0:T(8,128)S(1)}, f32[2,2,32,512]{3,2,1,0:T(8,128)S(1)}, u32[]{:S(2)}, u32[]{:S(2)}) collective-permute-start(f32[2,2,32,512]{3,2,1,0:T(8,128)S(1)} %bitcast.44), channel_id=1, source_target_pairs={{2,0},{3,1},{0,2},{1,3},{6,4},{7,5},{4,6},{5,7},{10,8},{11,9},{8,1... | collective-permute-start | bytes 786440 | tf_op jit(solution)/shard_map/ppermute | solution.py:543
  14.4 16.8 %collective-permute-start.2 = (f32[2,2,32,512]{3,2,1,0:T(8,128)S(1)}, f32[2,2,32,512]{3,2,1,0:T(8,128)S(1)}, u32[]{:S(2)}, u32[]{:S(2)}) collective-permute-start(f32[2,2,32,512]{3,2,1,0:T(8,128)S(1)} %bitcast.43), channel_id=1, source_target_pairs={{66,0},{67,1},{124,2},{125,3},{126,4},{127,5},{120,6},{121,7},{122... | collective-permute-start | bytes 786440 | tf_op jit(solution)/shard_map/ppermute | solution.py:543
  17.9 28.1 %all-to-all-start = ((f32[128,16,128]{2,1,0:T(8,128)}), f32[128,16,128]{2,1,0:T(8,128)S(1)}, u32[]{:S(2)}, u32[]{:S(2)}) async-start(f32[128,16,128]{2,1,0:T(8,128)} %bitcast), calls=%async_computation | async-start | bytes 2097152 | tf_op jit(solution)/shard_map/all_to_all | solution.py:527
  27.0 4.7 %collective-permute-start.3 = (f32[2,2,32,512]{3,2,1,0:T(8,128)S(1)}, f32[2,2,32,512]{3,2,1,0:T(8,128)S(1)}, u32[]{:S(2)}, u32[]{:S(2)}) collective-permute-start(f32[2,2,32,512]{3,2,1,0:T(8,128)S(1)} %bitcast.39), channel_id=1, source_target_pairs={{0,1},{1,0},{2,3},{3,2},{4,5},{5,4},{6,7},{7,6},{8,9},{9,8},{10,11... | collective-permute-start | bytes 786440 | tf_op jit(solution)/shard_map/ppermute | solution.py:547
  27.2 4.6 %collective-permute-start.5 = (f32[2,2,32,512]{3,2,1,0:T(8,128)S(1)}, f32[2,2,32,512]{3,2,1,0:T(8,128)S(1)}, u32[]{:S(2)}, u32[]{:S(2)}) collective-permute-start(f32[2,2,32,512]{3,2,1,0:T(8,128)S(1)} %collective-permute-done.1.refs_2_), channel_id=1, source_target_pairs={{0,1},{1,0},{2,3},{3,2},{4,5},{5,4},{6,7},{7,6},{8,9},{9,8},{10,11... | collective-permute-start | bytes 786440 | tf_op jit(solution)/shard_map/ppermute | solution.py:547
  31.2 1.5 %collective-permute-start.4 = (f32[2,2,32,512]{3,2,1,0:T(8,128)S(1)}, f32[2,2,32,512]{3,2,1,0:T(8,128)S(1)}, u32[]{:S(2)}, u32[]{:S(2)}) collective-permute-start(f32[2,2,32,512]{3,2,1,0:T(8,128)S(1)} %collective-permute-done.refs_1_), channel_id=1, source_target_pairs={{0,1},{1,0},{2,3},{3,2},{4,5},{5,4},{6,7},{7,6},{8,9},{9,8},{10,11... | collective-permute-start | bytes 786440 | tf_op jit(solution)/shard_map/ppermute | solution.py:547
  31.2 1.9 %collective-permute-start.6 = (f32[2,2,32,512]{3,2,1,0:T(8,128)S(1)}, f32[2,2,32,512]{3,2,1,0:T(8,128)S(1)}, u32[]{:S(2)}, u32[]{:S(2)}) collective-permute-start(f32[2,2,32,512]{3,2,1,0:T(8,128)S(1)} %collective-permute-done.2.refs_3_), channel_id=1, source_target_pairs={{0,1},{1,0},{2,3},{3,2},{4,5},{5,4},{6,7},{7,6},{8,9},{9,8},{10,11... | collective-permute-start | bytes 786440 | tf_op jit(solution)/shard_map/ppermute | solution.py:547
  53.2 4.8 %copy-start = (f32[32,2,4,512]{3,2,1,0:T(4,128)S(1)}, f32[32,2,4,512]{3,2,1,0:T(4,128)}, u32[]{:S(2)}) copy-start(f32[32,2,4,512]{3,2,1,0:T(4,128)} %param.19) | copy-start | bytes 1572868
  53.2 24.1 %all-to-all-start.1 = ((f32[128,16,128]{2,1,0:T(8,128)}), f32[128,16,128]{2,1,0:T(8,128)S(1)}, u32[]{:S(2)}, u32[]{:S(2)}) async-start(f32[128,16,128]{2,1,0:T(8,128)} %bitcast.14), calls=%async_computation.1 | async-start | bytes 2097152 | tf_op jit(solution)/shard_map/all_to_all | solution.py:527
  58.4 23.2 %collective-permute-start.9 = (f32[1,2,32,512]{3,2,1,0:T(8,128)S(1)}, f32[1,2,32,512]{3,2,1,0:T(8,128)S(1)}, u32[]{:S(2)}, u32[]{:S(2)}) collective-permute-start(f32[1,2,32,512]{3,2,1,0:T(8,128)S(1)} %get-tuple-element.31), channel_id=1, source_target_pairs={{66,0},{67,1},{124,2},{125,3},{126,4},{127,5},{120,6},{121,7},{122... | collective-permute-start | bytes 393224 | tf_op jit(solution)/shard_map/ppermute | solution.py:543
  65.8 15.8 %collective-permute-start.8 = (f32[1,2,32,512]{3,2,1,0:T(8,128)S(1)}, f32[1,2,32,512]{3,2,1,0:T(8,128)S(1)}, u32[]{:S(2)}, u32[]{:S(2)}) collective-permute-start(f32[1,2,32,512]{3,2,1,0:T(8,128)S(1)} %get-tuple-element.32), channel_id=1, source_target_pairs={{64,0},{65,1},{126,2},{127,3},{124,4},{125,5},{122,6},{123,7},{120... | collective-permute-start | bytes 393224 | tf_op jit(solution)/shard_map/ppermute | solution.py:543
  65.8 16.8 %collective-permute-start.7 = (f32[1,2,32,512]{3,2,1,0:T(8,128)S(1)}, f32[1,2,32,512]{3,2,1,0:T(8,128)S(1)}, u32[]{:S(2)}, u32[]{:S(2)}) collective-permute-start(f32[1,2,32,512]{3,2,1,0:T(8,128)S(1)} %get-tuple-element.33), channel_id=1, source_target_pairs={{2,0},{3,1},{0,2},{1,3},{6,4},{7,5},{4,6},{5,7},{10,8},{11,9},{8,1... | collective-permute-start | bytes 393224 | tf_op jit(solution)/shard_map/ppermute | solution.py:543
  82.6 24.7 %all-to-all-start.2 = ((f32[128,16,128]{2,1,0:T(8,128)}), f32[128,16,128]{2,1,0:T(8,128)S(1)}, u32[]{:S(2)}, u32[]{:S(2)}) async-start(f32[128,16,128]{2,1,0:T(8,128)} %bitcast.16), calls=%async_computation.2 | async-start | bytes 2097152 | tf_op jit(solution)/shard_map/all_to_all | solution.py:527
  88.2 1.4 %collective-permute-start.10 = (f32[1,2,32,512]{3,2,1,0:T(8,128)S(1)}, f32[1,2,32,512]{3,2,1,0:T(8,128)S(1)}, u32[]{:S(2)}, u32[]{:S(2)}) collective-permute-start(f32[1,2,32,512]{3,2,1,0:T(8,128)S(1)} %get-tuple-element.22.refs_0_), channel_id=1, source_target_pairs={{0,1},{1,0},{2,3},{3,2},{4,5},{5,4},{6,7},{7,6},{8,9},{9,8},{10,11... | collective-permute-start | bytes 393224 | tf_op jit(solution)/shard_map/ppermute | solution.py:547
  88.3 1.5 %collective-permute-start.11 = (f32[1,2,32,512]{3,2,1,0:T(8,128)S(1)}, f32[1,2,32,512]{3,2,1,0:T(8,128)S(1)}, u32[]{:S(2)}, u32[]{:S(2)}) collective-permute-start(f32[1,2,32,512]{3,2,1,0:T(8,128)S(1)} %collective-permute-done.7.refs_1_), channel_id=1, source_target_pairs={{0,1},{1,0},{2,3},{3,2},{4,5},{5,4},{6,7},{7,6},{8,9},{9,8},{10,11... | collective-permute-start | bytes 393224 | tf_op jit(solution)/shard_map/ppermute | solution.py:547
  88.8 1.3 collective-permute-start.12
  88.9 1.4 %collective-permute-start.13 = (f32[1,2,32,512]{3,2,1,0:T(8,128)S(1)}, f32[1,2,32,512]{3,2,1,0:T(8,128)S(1)}, u32[]{:S(2)}, u32[]{:S(2)}) collective-permute-start(f32[1,2,32,512]{3,2,1,0:T(8,128)S(1)} %collective-permute-done.9.refs_3_), channel_id=1, source_target_pairs={{0,1},{1,0},{2,3},{3,2},{4,5},{5,4},{6,7},{7,6},{8,9},{9,8},{10,11... | collective-permute-start | bytes 393224 | tf_op jit(solution)/shard_map/ppermute | solution.py:547

commit v3 on v2

--- a/solution.py
+++ b/solution.py
@@ -69,11 +69,6 @@
 
 def x_in(sign):
     return real_form(phases(IDX, IDX, N, sign, N)).transpose(0, 1, 3, 2).reshape(256, 256)
-
-
-def x_in_pair():
-    minus = x_in(-1).reshape(2, 128, 256) * np.array([1.0, -1.0])[:, None, None]
-    return split(np.concatenate([x_in(1), minus.reshape(256, 256)]))
 
 
 def x_out():
@@ -146,12 +141,43 @@
     return copy.wait
 
 
-def first_kernel(table_hbm, green_hbm, out_ref, table_ref, green_ref, sems):
-    table_here = fetch(table_hbm, table_ref, sems.at[0])
-    green_here = [
-        fetch(green_hbm.at[:, tangent], green_ref.at[tangent], sems.at[1 + tangent])
-        for tangent in range(2)
-    ]
+def leave(core, out_ref, out_hbm, sems):
+    share = pl.ds(core * 16, 16)
+    return fetch(out_ref.reshape(CHIPS, 32, 128).at[:, share], out_hbm.at[:, share], sems.at[3 + core])
+
+
+def sort_rows(sources, outs, sems):
+    site, freq = lax.axis_index("site"), lax.axis_index("freq")
+    z_hi = freq // 2
+    low = (z_hi, 1 - z_hi, 2 + z_hi, 3 - z_hi)
+    high = (2 - z_hi, 1 + z_hi, 3 * z_hi, 3 - 3 * z_hi)
+    gone = []
+    for shift in (1, 2, 3, 0):
+        row = jnp.where(site < 16, low[shift], high[shift])
+        for array, source in enumerate(sources):
+            sem = sems.at[shift * len(sources) + array]
+            gone.append(fetch(source.at[:, :, row], outs[shift].at[array], sem))
+    return gone
+
+
+def pack_kernel(source, out0, out1, out2, out3, sems):
+    for wait in sort_rows((source,), (out0, out1, out2, out3), sems):
+        wait()
+
+
+def begin_kernel(
+    plus_hbm, mirror_hbm, table_hbm, green_hbm, out0, out1, out2, out3, out_hbm,
+    table_ref, green_ref, out_ref, row_sems, sems,
+):
+    rows_gone = sort_rows((plus_hbm, mirror_hbm), (out0, out1, out2, out3), row_sems)
+    green_here = []
+    for tangent in range(2):
+        green_here.append(
+            fetch(green_hbm.at[:, tangent], green_ref.at[tangent], sems.at[1 + tangent])
+        )
+        if tangent == 0:
+            table_here = fetch(table_hbm, table_ref, sems.at[0])
+    left = []
     for tangent in range(2):
         green_here[tangent]()
         source = jnp.concatenate(
@@ -162,6 +188,9 @@
             table_here()
         result = dot3(table_ref[0], table_ref[1], high, low)
         store_columns(result, tangent, out_ref)
+        left.append(leave(tangent, out_ref, out_hbm, sems))
+    for wait in rows_gone + left:
+        wait()
 
 
 def inverse_square(real_part, imag_part):
@@ -171,31 +200,35 @@
     return (inv_real * inv_real - inv_imag * inv_imag, 2.0 * inv_real * inv_imag)
 
 
-def middle_kernel(
-    in_table_hbm, out_table_hbm, bubble_hbm, in_ref, out_ref,
-    in_table_ref, out_table_ref, bubble_ref, sems,
-):
-    bubble_here = fetch(bubble_hbm, bubble_ref, sems.at[0])
-    in_table_here = fetch(in_table_hbm, in_table_ref, sems.at[1])
-    out_table_here = fetch(out_table_hbm, out_table_ref, sems.at[2])
-    columns = [halves(load_columns(core, in_ref)) for core in range(2)]
-    bubble_here()
-    weight_real, weight_imag = [], []
+def weight_kernel(bubble_ref, table_hbm, weight_hbm, table_ref, weight_ref, sems):
+    table_here = fetch(table_hbm, table_ref, sems.at[0])
     for kx in range(4):
         chi_real = bubble_ref[kx, 0]
         chi_imag = bubble_ref[kx, 1]
         spin_real, spin_imag = inverse_square(1.0 - chi_real, -chi_imag)
         charge_real, charge_imag = inverse_square(1.0 + chi_real, chi_imag)
-        weight_real.append(1.5 * spin_real + 0.5 * charge_real - 1.0)
-        weight_imag.append(1.5 * spin_imag + 0.5 * charge_imag)
-    weight_real = jnp.concatenate(weight_real, axis=1)
-    weight_imag = jnp.concatenate(weight_imag, axis=1)
+        lanes = slice(kx * 128, kx * 128 + 128)
+        weight_ref[0, :, lanes] = 1.5 * spin_real + 0.5 * charge_real - 1.0
+        weight_ref[1, :, lanes] = 1.5 * spin_imag + 0.5 * charge_imag
+    gone = fetch(weight_ref, weight_hbm, sems.at[1])
+    table_here()
+    gone()
+
+
+def middle_kernel(
+    in_table_ref, out_table_hbm, weight_hbm, in_ref, out_hbm,
+    out_table_ref, weight_ref, out_ref, sems,
+):
+    left = []
+    weight_here = fetch(weight_hbm, weight_ref, sems.at[1])
+    out_table_here = fetch(out_table_hbm, out_table_ref, sems.at[2])
     for core in range(2):
-        high, low = columns[core]
-        if core == 0:
-            in_table_here()
+        high, low = halves(load_columns(core, in_ref))
         chi = dot3(in_table_ref[0], in_table_ref[1], high, low)
         real, imag = chi[:128], chi[128:]
+        if core == 0:
+            weight_here()
+        weight_real, weight_imag = weight_ref[0], weight_ref[1]
         pot = jnp.concatenate(
             [
                 weight_real * real - weight_imag * imag,
@@ -208,22 +241,22 @@
             out_table_here()
         result = dot3(out_table_ref[0], out_table_ref[1], high, low)
         store_columns(result, core, out_ref)
-
-
-def last_kernel(table_hbm, in_ref, out_hbm, table_ref, out_ref, sems):
-    table_here = fetch(table_hbm, table_ref, sems.at[0])
+        left.append(leave(core, out_ref, out_hbm, sems))
+    for gone in left:
+        gone()
+
+
+def last_kernel(table_ref, in_ref, out_hbm, out_ref, sems):
     sent = []
     for core in range(2):
         high, low = halves(load_columns(core, in_ref))
-        if core == 0:
-            table_here()
         result = dot3(table_ref[0], table_ref[1], high, low)
         for kx in range(4):
             for part in range(2):
                 out_ref[core, kx, part] = result[
                     part * 128 : part * 128 + 128, kx * 128 : kx * 128 + 128
                 ]
-        sent.append(fetch(out_ref.at[core], out_hbm.at[:, core], sems.at[1 + core]))
+        sent.append(fetch(out_ref.at[core], out_hbm.at[:, core], sems.at[core]))
     for gone in sent:
         gone()
 
@@ -261,7 +294,8 @@
     return dot3(first, second, t_in_ref[step, 0], t_in_ref[step, 1])
 
 
-def finish(x_out_ref, acc_ref, out_ref):
+def finish(x_out_ref, acc_ref, out_ref, out_hbm=None, sems=None):
+    left = []
     for slab in range(2):
         rows = slice(slab * 128, slab * 128 + 128)
         source = jnp.concatenate(
@@ -275,6 +309,10 @@
         result = dot3(x_out_ref[0], x_out_ref[1], high, low)
         for freq in range(4):
             out_ref[:, freq, slab] = result[:, freq * 128 : freq * 128 + 128].reshape(32, 8, 128)
+        if out_hbm is not None:
+            left.append(fetch(out_ref.at[:, :, slab], out_hbm.at[:, :, slab], sems.at[slab]))
+    for gone in left:
+        gone()
 
 
 def accumulate(step, first, second, t_out_ref, acc_ref):
@@ -288,11 +326,21 @@
 
 
 def prepare_kernel(order_hbm, *refs):
-    pieces, (out_hbm, order_ref, out_ref, sems) = refs[:8], refs[8:]
+    table_hbm, pieces, (out_hbm, table_ref, order_ref, out_ref, sems) = refs[0], refs[1:9], refs[9:]
     order_here = fetch(order_hbm, order_ref, sems.at[0])
+    table_here = fetch(table_hbm, table_ref, sems.at[2])
     for place, ref in enumerate(pieces):
         arrays = ref.shape[0]
-        value = ref[...].reshape(arrays * 64, NF)
+        value = jnp.concatenate(
+            [
+                jnp.concatenate(
+                    [ref[array, pl.ds(part * 4 + block, 32, stride=8), :] for block in range(4)], axis=1
+                )
+                for array in range(arrays)
+                for part in range(2)
+            ],
+            axis=0,
+        )
         first = value.astype(BF16)
         rest = value - first.astype(F32)
         second, third = halves(rest)
@@ -306,7 +354,9 @@
             for part in range(2):
                 top = (array * 2 + part) * 32
                 out_ref[array, part, rows, :] = moved[top : top + 32]
-    fetch(out_ref, out_hbm, sems.at[1])()
+    gone = fetch(out_ref, out_hbm, sems.at[1])
+    table_here()
+    gone()
 
 
 def time_lanes(step, width):
@@ -329,23 +379,26 @@
 
 
 def chi_kernel(*refs):
-    tables_hbm, in_ref, base_hbm, out_ref, plus_hbm = refs[:4], *refs[4:8]
-    tables, (base_ref, plus_ref, left_ref, acc_ref, sems, base_sems, plus_sems) = refs[8:12], refs[12:]
-    x_in_ref, t_in_ref, t_out_ref, x_out_ref = tables
-    x_in_here, t_in_here, t_out_here, x_out_here = fetch_tables(tables_hbm, tables, sems)
+    x_in_ref, *tables_hbm = refs[:4]
+    (in_ref, base_hbm, out_hbm, plus_hbm), tables = refs[4:8], refs[8:11]
+    base_ref, plus_ref, out_ref, left_ref, acc_ref, sems, base_sems, plus_sems, out_sems = refs[11:]
+    t_in_ref, t_out_ref, x_out_ref = tables
+    t_in_here = fetch(tables_hbm[0], t_in_ref, sems.at[0])
     base_here = fetch_fields(base_hbm, base_ref, base_sems)
+    t_out_here = fetch(tables_hbm[1], t_out_ref, sems.at[1])
+    x_out_here = fetch(tables_hbm[2], x_out_ref, sems.at[2])
     site, freq = lax.axis_index("site"), lax.axis_index("freq")
     alone = jnp.logical_and(site == 0, freq < 2)
+    flip = (1 - 2 * lax.rem(lax.broadcasted_iota(jnp.int32, (256, 512), 0), 2)).astype(F32).astype(BF16)
 
     for slab in range(2):
         high, low = halves(gather_slab(in_ref, slab))
-        if slab == 0:
-            x_in_here()
         result = dot3(x_in_ref[0], x_in_ref[1], high, low)
-        to_left(result[:256], pl.ds(slab * 128, 128), left_ref)
+        to_left(result, pl.ds(slab * 128, 128), left_ref)
+        result = dot3(x_in_ref[0], x_in_ref[1], high * flip, low * flip)
         image = jnp.where(alone, slab, 1 - slab)
         rows = pl.ds(pl.multiple_of(256 + image * 128, 128), 128)
-        to_left(result[256:], rows, left_ref)
+        to_left(result, rows, left_ref)
 
     t_in_here()
     plus_gone = []
@@ -374,25 +427,27 @@
             t_out_here()
         accumulate(step, first, second, t_out_ref, acc_ref)
     x_out_here()
-    finish(x_out_ref, acc_ref, out_ref)
+    finish(x_out_ref, acc_ref, out_ref, out_hbm, out_sems)
     for gone in plus_gone:
         gone()
 
 
 def sigma_kernel(*refs):
-    tables_hbm, (in_ref, base_hbm, pot_hbm, plus_hbm, out_ref) = refs[:4], refs[4:9]
-    tables, refs = refs[9:13], refs[13:]
+    x_in_ref, *tables_hbm = refs[:4]
+    in_ref, base_hbm, pot_hbm, plus_hbm, table_hbm, out_ref, table_ref = refs[4:11]
+    tables, refs = refs[11:14], refs[14:]
     base_ref, pot_ref, plus_ref, left_ref, acc_ref, sems, base_sems, pot_sems, plus_sem = refs
-    x_in_ref, t_in_ref, t_out_ref, x_out_ref = tables
-    x_in_here, t_in_here, t_out_here, x_out_here = fetch_tables(tables_hbm, tables, sems)
+    t_in_ref, t_out_ref, x_out_ref = tables
+    t_in_here = fetch(tables_hbm[0], t_in_ref, sems.at[0])
     plus_here = fetch(plus_hbm, plus_ref, plus_sem.at[0])
     base_here = fetch_fields(base_hbm, base_ref, base_sems)
     pot_here = fetch_fields(pot_hbm, pot_ref, pot_sems)
+    t_out_here = fetch(tables_hbm[1], t_out_ref, sems.at[1])
+    x_out_here = fetch(tables_hbm[2], x_out_ref, sems.at[2])
+    table_here = fetch(table_hbm, table_ref, plus_sem.at[1])
 
     for slab in range(2):
         high, low = halves(gather_slab(in_ref, slab))
-        if slab == 0:
-            x_in_here()
         result = dot3(x_in_ref[0], x_in_ref[1], high, low)
         to_left(result, pl.ds(slab * 128, 128), left_ref)
 
@@ -423,12 +478,14 @@
         accumulate(step, first, second, t_out_ref, acc_ref)
     x_out_here()
     finish(x_out_ref, acc_ref, out_ref)
+    table_here()
 
 
 PARAMS = pltpu.CompilerParams(vmem_limit_bytes=24 * 1024 * 1024)
 WORK = 3 << 31
 HBM = pl.BlockSpec(memory_space=pltpu.HBM)
 HERE = pl.BlockSpec(memory_space=pltpu.VMEM)
+TABLE = pl.BlockSpec(memory_space=pltpu.VMEM)
 
 
 def call(body, name, in_specs, out_specs, out_shape, scratch, flops, *operands):
@@ -438,7 +495,7 @@
         in_specs=in_specs,
         out_specs=out_specs,
         out_shape=[
-            pltpu.HBM(shape, F32) if spec is HBM else jax.ShapeDtypeStruct(shape, F32)
+            pltpu.HBM(shape, F32) if spec is HBM else jax.ShapeDtypeStruct(shape, BF16 if spec is TABLE else F32)
             for shape, spec in zip(out_shape, out_specs)
         ],
         scratch_shapes=scratch,
@@ -463,34 +520,36 @@
 TURN = 2 * 3 * 256 * 256 * 1024
 
 
-def first_call(table, green):
-    scratch = [like(table), pltpu.VMEM((2, 4, 2, 128, 128), F32), sems(3)]
+def weight_call(bubble, table):
+    shape = (2, 128, NF)
+    scratch = [pltpu.VMEM(shape, F32), sems(2)]
     return call(
-        first_kernel, "first", [HBM, HBM], [HERE], [(2048, 128)], scratch, TURN, table, green
-    )[0]
-
-
-def middle_call(momenta, columns, bubble, held):
-    scratch = [like(momenta), like(columns), like(bubble), sems(3)]
+        weight_kernel, "weight", [HERE, HBM], [HBM, TABLE], [shape, table.shape], scratch, TURN, bubble, table
+    )
+
+
+def middle_call(weight, momenta, columns, held):
+    scratch = [like(columns), like(weight), pltpu.VMEM((2048, 128), F32), sems(5)]
     return call(
-        middle_kernel, "middle", [HBM, HBM, HBM, HERE], [HERE], [(2048, 128)], scratch, 2 * TURN,
-        momenta, columns, bubble, held,
+        middle_kernel, "middle", [HERE, HBM, HBM, HERE], [HBM], [(CHIPS, 32, 128)], scratch, 2 * TURN,
+        momenta, columns, weight, held,
     )[0]
 
 
 def last_call(table, held):
     shape = (4, 2, 2, 128, 128)
-    scratch = [like(table), pltpu.VMEM((2, 4, 2, 128, 128), F32), sems(3)]
-    return call(last_kernel, "last", [HBM, HERE], [HBM], [shape], scratch, TURN, table, held)[0]
-
-
-def prepare_call(pieces):
+    scratch = [pltpu.VMEM((2, 4, 2, 128, 128), F32), sems(2)]
+    return call(last_kernel, "last", [HERE, HERE], [HBM], [shape], scratch, TURN, table, held)[0]
+
+
+def prepare_call(pieces, table):
     shape = (pieces[0].shape[0], 2, 256, NF)
     order = jnp.asarray(t_order())
-    scratch = [like(order), pltpu.VMEM(shape, F32), sems(2)]
+    scratch = [like(order), pltpu.VMEM(shape, F32), sems(3)]
     return call(
-        prepare_kernel, "prepare", [HBM] + [HERE] * 8, [HBM], [shape], scratch, WORK, order, *pieces
-    )[0]
+        prepare_kernel, "prepare", [HBM, HBM] + [HERE] * 8, [HBM, TABLE], [shape, table.shape], scratch,
+        WORK, order, table, *pieces,
+    )
 
 
 def field(arrays):
@@ -502,24 +561,24 @@
 
 def chi_call(tables, held, base):
     scratch = [
-        *map(like, tables), field(2), pltpu.VMEM(PLUS, F32), pltpu.VMEM((4, 512, 256), F32),
-        pltpu.VMEM((4, 256, 256), F32), sems(4), sems(4), sems(4),
+        *map(like, tables[1:]), field(2), pltpu.VMEM(PLUS, F32), pltpu.VMEM(SLABS, F32),
+        pltpu.VMEM((4, 512, 256), F32), pltpu.VMEM((4, 256, 256), F32), sems(4), sems(4), sems(4), sems(2),
     ]
     return call(
-        chi_kernel, "chi", [HBM] * 4 + [HERE, HBM], [HERE, HBM], [SLABS, PLUS], scratch, 7 * TURN,
+        chi_kernel, "chi", [HERE, HBM, HBM, HBM, HERE, HBM], [HBM, HBM], [SLABS, PLUS], scratch, 7 * TURN,
         *tables, held.reshape(SLABS), base,
     )
 
 
-def sigma_call(tables, held, base, pot, plus):
+def sigma_call(tables, held, base, pot, plus, table):
     scratch = [
-        *map(like, tables), field(1), field(1), pltpu.VMEM(PLUS, F32),
-        pltpu.VMEM((4, 256, 256), F32), pltpu.VMEM((4, 256, 256), F32), sems(4), sems(4), sems(4), sems(1),
+        *map(like, tables[1:]), field(1), field(1), pltpu.VMEM(PLUS, F32),
+        pltpu.VMEM((4, 256, 256), F32), pltpu.VMEM((4, 256, 256), F32), sems(4), sems(4), sems(4), sems(2),
     ]
     return call(
-        sigma_kernel, "sigma", [HBM] * 4 + [HERE, HBM, HBM, HBM], [HERE], [SLABS], scratch, 4 * TURN,
-        *tables, held.reshape(SLABS), base, pot, plus,
-    )[0]
+        sigma_kernel, "sigma", [HERE, HBM, HBM, HBM, HERE, HBM, HBM, HBM, HBM], [HERE, TABLE],
+        [SLABS, table.shape], scratch, 4 * TURN, *tables, held.reshape(SLABS), base, pot, plus, table,
+    )
 
 
 def exchange(source):
@@ -527,16 +586,34 @@
     return lax.all_to_all(source, BOTH, split_axis=0, concat_axis=0, tiled=True)
 
 
-def pack(arrays):
-    site, freq = lax.axis_index("site"), lax.axis_index("freq")
-    z_hi = freq // 2
-    low = (z_hi, 1 - z_hi, 2 + z_hi, 3 - z_hi)
-    high = (2 - z_hi, 1 + z_hi, 3 * z_hi, 3 - 3 * z_hi)
-    stacked = jnp.stack([array.transpose(2, 1, 0, 3) for array in arrays], axis=1)
+def views(arrays):
     return [
-        lax.dynamic_index_in_dim(stacked, jnp.where(site < 16, low[k], high[k]), 0, keepdims=False)
-        for k in range(4)
+        array.reshape(32, 2, 4, 4, 128).transpose(0, 1, 3, 2, 4).reshape(64, 4, 4, 1, 128)
+        for array in arrays
     ]
+
+
+def pieces_of(packed):
+    return [piece.reshape(-1, 256, 128) for piece in packed]
+
+
+def pack(array):
+    shape = (1, 64, 4, 1, 128)
+    return pieces_of(
+        call(pack_kernel, "pack", [HBM], [HERE] * 4, [shape] * 4, [sems(4)], 1 << 20, *views([array]))
+    )
+
+
+def begin(arrays, table, green):
+    shape = (2, 64, 4, 1, 128)
+    scratch = [
+        like(table), pltpu.VMEM((2, 4, 2, 128, 128), F32), pltpu.VMEM((2048, 128), F32), sems(8), sems(5)
+    ]
+    *packed, sent = call(
+        begin_kernel, "begin", [HBM] * 4, [HERE] * 4 + [HBM], [shape] * 4 + [(CHIPS, 32, 128)],
+        scratch, TURN, *views(arrays), table, green,
+    )
+    return pieces_of(packed), sent
 
 
 def send(rows):
@@ -548,29 +625,26 @@
 
 
 def local(green_tangent, green_plus, green_mirror, potential, bubble):
-    base = prepare_call(both_cores(send(pack([green_plus, green_mirror]))))
     columns, momenta = jnp.asarray(y_to_columns()), jnp.asarray(y_to_momenta())
-    back = jnp.asarray(x_out())
-    chi_tables = (
-        jnp.asarray(x_in_pair()), jnp.asarray(t_in(FERMI, -1)), jnp.asarray(t_out(BOSE, 1)), back
-    )
-    sigma_tables = (
-        jnp.asarray(split(x_in(1))), jnp.asarray(t_in(BOSE, -1)), jnp.asarray(t_out(FERMI, 1)), back
-    )
-    sent = first_call(columns, green_tangent)
+    x_table, back = jnp.asarray(split(x_in(1))), jnp.asarray(x_out())
+    packed, sent = begin([green_plus, green_mirror], columns, green_tangent)
+    base, x_here = prepare_call(both_cores(send(packed)), x_table)
     potential, sent = lax.optimization_barrier((potential, sent))
     held = exchange(sent)
-    sent, plus = chi_call(chi_tables, held, base)
-    potential, sent = lax.optimization_barrier((potential, sent))
-    own = send(pack([potential]))
+    tables = (x_here, jnp.asarray(t_in(FERMI, -1)), jnp.asarray(t_out(BOSE, 1)), back)
+    sent, plus = chi_call(tables, held, base)
+    potential, bubble, sent = lax.optimization_barrier((potential, bubble, sent))
+    own = send(pack(potential))
+    weight, momenta_here = weight_call(bubble, momenta)
     held = exchange(sent).reshape(2048, 128)
-    sent = middle_call(momenta, columns, bubble, held)
+    sent = middle_call(weight, momenta_here, columns, held)
     own, sent = lax.optimization_barrier((own, sent))
-    pot = prepare_call(both_cores(own))
+    pot, x_here = prepare_call(both_cores(own), x_table)
     held = exchange(sent)
-    sent = sigma_call(sigma_tables, held, base, pot, plus)
+    tables = (x_here, jnp.asarray(t_in(BOSE, -1)), jnp.asarray(t_out(FERMI, 1)), back)
+    sent, momenta_here = sigma_call(tables, held, base, pot, plus, momenta)
     held = exchange(sent).reshape(2048, 128)
-    return last_call(momenta, held)
+    return last_call(momenta_here, held)
 
 
 def solution(mesh):

time: 138 us -> 133 us (0.964)
  other arithmetic: 3.85 us -> 0 us
    another operation x1 -> x0, other arithmetic: 3.85 us -> none  [pack(): jnp.stack([array.transpose(2, 1, 0, 3) for array in arrays], axis=1)]
    all_to_all x3, waiting for transfers between devices: 31 us -> 28.6 us  [exchange(): return lax.all_to_all(source, BOTH, split_axis=0, concat_axis=0, tiled=True)]
    all_to_all x3, starting transfers between devices: 19.4 us -> 21.2 us  [exchange(): return lax.all_to_all(source, BOTH, split_axis=0, concat_axis=0, tiled=True)]
    ppermute x6, starting transfers between devices: 19.8 us -> 18.1 us  [send(): lax.ppermute(rows[shift], BOTH, routes(shift))]
    pallas_call x7 -> x9, Pallas kernels: 30.6 us -> 31.4 us  [call(): pl.pallas_call(body, in_specs=in_specs, out_specs=out_specs, out_shape=[p...]
  transfers between devices with their start and end apart: 17 -> 17, of which waited for: 11 -> 10; matrix products, arithmetic and copies ran while one was open for 0% -> 0% of each run, Pallas kernels for 12% -> 11%
where the time goes in v3:
time: 133 us
  starting transfers between devices  41 us (31%)
  waiting for transfers between devices  37 us (28%)
  Pallas kernels  31.4 us (24%)
  blocking collectives  23 us (17%)
    pallas_call x9, Pallas kernels, call(): pl.pallas_call(body, in_specs=in_specs, out_specs=out_specs, out_shape=[p...  31.4 us
    all_to_all x3, waiting for transfers between devices, exchange(): return lax.all_to_all(source, BOTH, split_axis=0, concat_axis=0, tiled=True)  28.6 us
    all_to_all x1, blocking collectives, exchange(): return lax.all_to_all(source, BOTH, split_axis=0, concat_axis=0, tiled=True)  23 us
    all_to_all x3, starting transfers between devices, exchange(): return lax.all_to_all(source, BOTH, split_axis=0, concat_axis=0, tiled=True)  21.2 us
    ppermute x6, starting transfers between devices, send(): lax.ppermute(rows[shift], BOTH, routes(shift))  18.1 us
    ppermute x6, waiting for transfers between devices, send(): lax.ppermute(rows[shift], BOTH, routes(shift))  5.81 us
  transfers between devices with their start and end apart: 17, of which 10 were waited for; matrix products, arithmetic and copies ran while one was open for 0% of the time, Pallas kernels for 11%

profile of v3, /device:TPU:0, one launch (start us, length us, event | category | flops | bytes accessed | tf_op | source)
XLA Modules:
  0.0 132.7 jit_solution(8796487051590551500)
XLA Ops:
  0.0 3.6 %begin.1 = (f32[2,64,4,1,128]{4,3,2,1,0:T(1,128)S(1)}, f32[2,64,4,1,128]{4,3,2,1,0:T(1,128)S(1)}, f32[2,64,4,1,128]{4,3,2,1,0:T(1,128)S(1)}, f32[2,64,4,1,128]{4,3,2,1,0:T(1,128)S(1)}, f32[64,32,128]{2,1,0:T(8,128)}) custom-call(f32[64,4,4,1,128]{4,3,2,1,0:T(1,128)} %bitcast.50, f32[64,4,4,1,128]{4,3,2,1,0:T(1,128)} %bitcast.51, ...), custom_call_target="tpu_custom_call" | custom-call | flops 402653184 | bytes 2359296 | tf_op jit(solution)/shard_map/begin/pallas_call | solution.py:493
  3.6 4.0 %collective-permute-start = (f32[2,256,128]{2,1,0:T(8,128)S(1)}, f32[2,256,128]{2,1,0:T(8,128)S(1)}, u32[]{:S(2)}, u32[]{:S(2)}) collective-permute-start(f32[2,256,128]{2,1,0:T(8,128)S(1)} %bitcast.40), channel_id=1, source_target_pairs={{2,0},{3,1},{0,2},{1,3},{6,4},{7,5},{4,6},{5,7},{10,8},{11,9},{8,1... | collective-permute-start | bytes 786440 | tf_op jit(solution)/shard_map/ppermute | solution.py:620
  7.7 5.7 %collective-permute-start.1 = (f32[2,256,128]{2,1,0:T(8,128)S(1)}, f32[2,256,128]{2,1,0:T(8,128)S(1)}, u32[]{:S(2)}, u32[]{:S(2)}) collective-permute-start(f32[2,256,128]{2,1,0:T(8,128)S(1)} %bitcast.39), channel_id=1, source_target_pairs={{64,0},{65,1},{126,2},{127,3},{124,4},{125,5},{122,6},{123,7},{120... | collective-permute-start | bytes 786440 | tf_op jit(solution)/shard_map/ppermute | solution.py:620
  13.3 0.0 collective-permute-start.2
  13.3 9.0 %all-to-all-start = ((f32[128,16,128]{2,1,0:T(8,128)}), f32[128,16,128]{2,1,0:T(8,128)S(1)}, u32[]{:S(2)}, u32[]{:S(2)}) async-start(f32[128,16,128]{2,1,0:T(8,128)} %bitcast.47), calls=%async_computation | async-start | bytes 2097152 | tf_op jit(solution)/shard_map/all_to_all | solution.py:586
  22.4 0.1 collective-permute-start.3
  22.5 0.0 collective-permute-done.refs_2_
  22.5 0.5 collective-permute-start.4
  23.0 0.0 collective-permute-done.1.refs_3_
  23.0 0.1 collective-permute-start.5
  23.1 5.4 %collective-permute-done.2.refs_4_ = f32[2,256,128]{2,1,0:T(8,128)S(1)} collective-permute-done((f32[2,256,128]{2,1,0:T(8,128)S(1)}, f32[2,256,128]{2,1,0:T(8,128)S(1)}, u32[]{:S(2)}, u32[]{:S(2)}) %collective-permute-start.2) | collective-permute-done | bytes 262176 | tf_op jit(solution)/shard_map/ppermute | solution.py:620
  28.4 0.0 collective-permute-start.6
  28.5 0.0 collective-permute-done.3.refs_5_
  28.5 0.0 collective-permute-done.4.refs_6_
  28.5 0.0 collective-permute-done.5.refs_7_
  28.5 1.5 %collective-permute-done.6.refs_8_ = f32[2,256,128]{2,1,0:T(8,128)S(1)} collective-permute-done((f32[2,256,128]{2,1,0:T(8,128)S(1)}, f32[2,256,128]{2,1,0:T(8,128)S(1)}, u32[]{:S(2)}, u32[]{:S(2)}) %collective-permute-start.6) | collective-permute-done | bytes 262176 | tf_op jit(solution)/shard_map/ppermute | solution.py:624
  30.0 4.2 %prepare.2 = (f32[2,2,256,512]{3,2,1,0:T(8,128)}, bf16[2,256,256]{2,1,0:T(8,128)(2,1)S(1)}) custom-call(bf16[512,512]{1,0:T(8,128)(2,1)} %constant.22.clone.order_hbm, bf16[2,256,256]{2,1,0:T(8,128)(2,1)} %constant.20.clone.refs_0_, f32[2,256,128]{2,1,0:T(8,128)S(1)} %bitcast.37, f32[2,256,128]{2,1,0:T(8,128)S(1)} %collective-permute-done.refs_2_, ...), custom_call_target="tpu_custom_call" | custom-call | flops 6442450944 | bytes 2883584 | tf_op jit(solution)/shard_map/prepare/pallas_call | solution.py:493
  34.2 7.2 %all-to-all-done = f32[128,16,128]{2,1,0:T(8,128)S(1)} async-done(((f32[128,16,128]{2,1,0:T(8,128)}), f32[128,16,128]{2,1,0:T(8,128)S(1)}, u32[]{:S(2)}, u32[]{:S(2)}) %all-to-all-start) | async-done | bytes 1048608 | tf_op jit(solution)/shard_map/all_to_all | solution.py:586
  41.4 6.5 %chi.1 = (f32[32,4,2,8,128]{4,3,2,1,0:T(8,128)}, f32[256,1024]{1,0:T(8,128)}) custom-call(bf16[2,256,256]{2,1,0:T(8,128)(2,1)S(1)} %get-tuple-element.40.refs_0_, bf16[4,2,256,256]{3,2,1,0:T(8,128)(2,1)} %constant.23.clone.refs_1_, bf16[4,2,256,256]{3,2,1,0:T(8,128)(2,1)} %constant.24.clone.refs_2_, bf16[2,256,256]{2,1,0:T(8,128)(2,1)} %constant.21.clone.refs_3_, ...), custom_call_target="tpu_custom_call" | custom-call | flops 2818572288 | bytes 5767168 | tf_op jit(solution)/shard_map/chi/pallas_call | solution.py:493
  47.9 0.0 copy-start
  47.9 4.8 %all-to-all-start.1 = ((f32[128,16,128]{2,1,0:T(8,128)}), f32[128,16,128]{2,1,0:T(8,128)S(1)}, u32[]{:S(2)}, u32[]{:S(2)}) async-start(f32[128,16,128]{2,1,0:T(8,128)} %bitcast.48), calls=%async_computation.1 | async-start | bytes 2097152 | tf_op jit(solution)/shard_map/all_to_all | solution.py:586
  52.7 1.1 pack.1
  53.9 2.9 %collective-permute-start.7 = (f32[1,256,128]{2,1,0:T(8,128)S(1)}, f32[1,256,128]{2,1,0:T(8,128)S(1)}, u32[]{:S(2)}, u32[]{:S(2)}) collective-permute-start(f32[1,256,128]{2,1,0:T(8,128)S(1)} %bitcast.45), channel_id=1, source_target_pairs={{2,0},{3,1},{0,2},{1,3},{6,4},{7,5},{4,6},{5,7},{10,8},{11,9},{8,1... | collective-permute-start | bytes 393224 | tf_op jit(solution)/shard_map/ppermute | solution.py:620
  56.8 5.3 %collective-permute-start.8 = (f32[1,256,128]{2,1,0:T(8,128)S(1)}, f32[1,256,128]{2,1,0:T(8,128)S(1)}, u32[]{:S(2)}, u32[]{:S(2)}) collective-permute-start(f32[1,256,128]{2,1,0:T(8,128)S(1)} %bitcast.44), channel_id=1, source_target_pairs={{64,0},{65,1},{126,2},{127,3},{124,4},{125,5},{122,6},{123,7},{120... | collective-permute-start | bytes 393224 | tf_op jit(solution)/shard_map/ppermute | solution.py:620
  62.1 0.2 collective-permute-start.9
  62.3 0.0 copy-done
  62.3 1.1 weight.1
  63.4 8.8 %all-to-all-done.1 = f32[128,16,128]{2,1,0:T(8,128)S(1)} async-done(((f32[128,16,128]{2,1,0:T(8,128)}), f32[128,16,128]{2,1,0:T(8,128)S(1)}, u32[]{:S(2)}, u32[]{:S(2)}) %all-to-all-start.1) | async-done | bytes 1048608 | tf_op jit(solution)/shard_map/all_to_all | solution.py:586
  72.2 3.8 %middle.1 = f32[64,32,128]{2,1,0:T(8,128)} custom-call(bf16[2,256,256]{2,1,0:T(8,128)(2,1)S(1)} %get-tuple-element.50.in_table_ref, bf16[2,256,256]{2,1,0:T(8,128)(2,1)} %constant.18.clone.table_hbm.out_table_hbm, f32[2,128,512]{2,1,0:T(8,128)} %get-tuple-element.51.weight_hbm, f32[2048,128]{1,0:T(8,128)S(1)} %bitcast.31), custom_call_target="tpu_custom_call" | custom-call | flops 805306368 | bytes 2097152 | tf_op jit(solution)/shard_map/middle/pallas_call | solution.py:493
  76.0 0.4 collective-permute-done.7.refs_2_
  76.4 0.0 collective-permute-done.8.refs_3_
  76.4 0.0 collective-permute-done.9.refs_4_
  76.4 7.3 %all-to-all-start.2 = ((f32[128,16,128]{2,1,0:T(8,128)}), f32[128,16,128]{2,1,0:T(8,128)S(1)}, u32[]{:S(2)}, u32[]{:S(2)}) async-start(f32[128,16,128]{2,1,0:T(8,128)} %bitcast.46), calls=%async_computation.2 | async-start | bytes 2097152 | tf_op jit(solution)/shard_map/all_to_all | solution.py:586
  83.7 0.1 collective-permute-start.10
  83.8 0.5 collective-permute-start.11
  84.3 0.1 collective-permute-start.12
  84.4 0.4 collective-permute-start.13
  84.8 0.3 collective-permute-done.10.refs_5_
  85.2 0.2 collective-permute-done.11.refs_6_
  85.3 0.3 collective-permute-done.12.refs_7_
  85.7 0.2 collective-permute-done.13.refs_8_
  85.9 4.3 %prepare.3 = (f32[1,2,256,512]{3,2,1,0:T(8,128)}, bf16[2,256,256]{2,1,0:T(8,128)(2,1)S(1)}) custom-call(bf16[512,512]{1,0:T(8,128)(2,1)} %constant.22.clone.order_hbm, bf16[2,256,256]{2,1,0:T(8,128)(2,1)} %constant.20.clone.refs_0_, f32[1,256,128]{2,1,0:T(8,128)S(1)} %bitcast.42, f32[1,256,128]{2,1,0:T(8,128)S(1)} %collective-permute-done.7.refs_2_, ...), custom_call_target="tpu_custom_call" | custom-call | flops 6442450944 | bytes 1835008 | tf_op jit(solution)/shard_map/prepare/pallas_call | solution.py:493
  90.2 12.6 %all-to-all-done.2 = f32[128,16,128]{2,1,0:T(8,128)S(1)} async-done(((f32[128,16,128]{2,1,0:T(8,128)}), f32[128,16,128]{2,1,0:T(8,128)S(1)}, u32[]{:S(2)}, u32[]{:S(2)}) %all-to-all-start.2) | async-done | bytes 1048608 | tf_op jit(solution)/shard_map/all_to_all | solution.py:586
  102.8 4.8 %sigma.1 = (f32[32,4,2,8,128]{4,3,2,1,0:T(8,128)S(1)}, bf16[2,256,256]{2,1,0:T(8,128)(2,1)S(1)}) custom-call(bf16[2,256,256]{2,1,0:T(8,128)(2,1)S(1)} %get-tuple-element.57.refs_0_, bf16[4,2,256,256]{3,2,1,0:T(8,128)(2,1)} %constant.25.clone.refs_1_, bf16[4,2,256,256]{3,2,1,0:T(8,128)(2,1)} %constant.26.clone.refs_2_, ...), custom_call_target="tpu_custom_call" | custom-call | flops 1610612736 | bytes 8126464 | tf_op jit(solution)/shard_map/sigma/pallas_call | solution.py:493
  107.6 23.0 %all_to_all.20 = f32[128,16,128]{2,1,0:T(8,128)S(1)} all-to-all(f32[128,16,128]{2,1,0:T(8,128)S(1)} %bitcast.35), channel_id=1, replica_groups=mesh['site'=32,'freq'=4] {'site','freq'}, dimensions={0} | all-to-all | bytes 2097152 | tf_op jit(solution)/shard_map/all_to_all | solution.py:586
  130.7 1.9 %last.1 = f32[4,2,2,128,128]{4,3,2,1,0:T(8,128)} custom-call(bf16[2,256,256]{2,1,0:T(8,128)(2,1)S(1)} %get-tuple-element.61.table_ref, f32[2048,128]{1,0:T(8,128)S(1)} %bitcast.32), custom_call_target="tpu_custom_call" | custom-call | flops 402653184 | bytes 1310720 | tf_op jit(solution)/shard_map/last/pallas_call | solution.py:493
Async XLA Ops:
  3.6 18.9 %collective-permute-start = (f32[2,256,128]{2,1,0:T(8,128)S(1)}, f32[2,256,128]{2,1,0:T(8,128)S(1)}, u32[]{:S(2)}, u32[]{:S(2)}) collective-permute-start(f32[2,256,128]{2,1,0:T(8,128)S(1)} %bitcast.40), channel_id=1, source_target_pairs={{2,0},{3,1},{0,2},{1,3},{6,4},{7,5},{4,6},{5,7},{10,8},{11,9},{8,1... | collective-permute-start | bytes 786440 | tf_op jit(solution)/shard_map/ppermute | solution.py:620
  7.7 15.3 %collective-permute-start.1 = (f32[2,256,128]{2,1,0:T(8,128)S(1)}, f32[2,256,128]{2,1,0:T(8,128)S(1)}, u32[]{:S(2)}, u32[]{:S(2)}) collective-permute-start(f32[2,256,128]{2,1,0:T(8,128)S(1)} %bitcast.39), channel_id=1, source_target_pairs={{64,0},{65,1},{126,2},{127,3},{124,4},{125,5},{122,6},{123,7},{120... | collective-permute-start | bytes 786440 | tf_op jit(solution)/shard_map/ppermute | solution.py:620
  13.3 15.1 %collective-permute-start.2 = (f32[2,256,128]{2,1,0:T(8,128)S(1)}, f32[2,256,128]{2,1,0:T(8,128)S(1)}, u32[]{:S(2)}, u32[]{:S(2)}) collective-permute-start(f32[2,256,128]{2,1,0:T(8,128)S(1)} %bitcast.38), channel_id=1, source_target_pairs={{66,0},{67,1},{124,2},{125,3},{126,4},{127,5},{120,6},{121,7},{122... | collective-permute-start | bytes 786440 | tf_op jit(solution)/shard_map/ppermute | solution.py:620
  13.3 28.1 %all-to-all-start = ((f32[128,16,128]{2,1,0:T(8,128)}), f32[128,16,128]{2,1,0:T(8,128)S(1)}, u32[]{:S(2)}, u32[]{:S(2)}) async-start(f32[128,16,128]{2,1,0:T(8,128)} %bitcast.47), calls=%async_computation | async-start | bytes 2097152 | tf_op jit(solution)/shard_map/all_to_all | solution.py:586
  22.4 6.1 %collective-permute-start.3 = (f32[2,256,128]{2,1,0:T(8,128)S(1)}, f32[2,256,128]{2,1,0:T(8,128)S(1)}, u32[]{:S(2)}, u32[]{:S(2)}) collective-permute-start(f32[2,256,128]{2,1,0:T(8,128)S(1)} %bitcast.36), channel_id=1, source_target_pairs={{0,1},{1,0},{2,3},{3,2},{4,5},{5,4},{6,7},{7,6},{8,9},{9,8},{10,11... | collective-permute-start | bytes 786440 | tf_op jit(solution)/shard_map/ppermute | solution.py:624
  22.5 6.0 %collective-permute-start.4 = (f32[2,256,128]{2,1,0:T(8,128)S(1)}, f32[2,256,128]{2,1,0:T(8,128)S(1)}, u32[]{:S(2)}, u32[]{:S(2)}) collective-permute-start(f32[2,256,128]{2,1,0:T(8,128)S(1)} %collective-permute-done.refs_2_), channel_id=1, source_target_pairs={{0,1},{1,0},{2,3},{3,2},{4,5},{5,4},{6,7},{7,6},{8,9},{9,8},{10,11... | collective-permute-start | bytes 786440 | tf_op jit(solution)/shard_map/ppermute | solution.py:624
  23.0 5.5 %collective-permute-start.5 = (f32[2,256,128]{2,1,0:T(8,128)S(1)}, f32[2,256,128]{2,1,0:T(8,128)S(1)}, u32[]{:S(2)}, u32[]{:S(2)}) collective-permute-start(f32[2,256,128]{2,1,0:T(8,128)S(1)} %collective-permute-done.1.refs_3_), channel_id=1, source_target_pairs={{0,1},{1,0},{2,3},{3,2},{4,5},{5,4},{6,7},{7,6},{8,9},{9,8},{10,11... | collective-permute-start | bytes 786440 | tf_op jit(solution)/shard_map/ppermute | solution.py:624
  28.4 1.5 %collective-permute-start.6 = (f32[2,256,128]{2,1,0:T(8,128)S(1)}, f32[2,256,128]{2,1,0:T(8,128)S(1)}, u32[]{:S(2)}, u32[]{:S(2)}) collective-permute-start(f32[2,256,128]{2,1,0:T(8,128)S(1)} %collective-permute-done.2.refs_4_), channel_id=1, source_target_pairs={{0,1},{1,0},{2,3},{3,2},{4,5},{5,4},{6,7},{7,6},{8,9},{9,8},{10,11... | collective-permute-start | bytes 786440 | tf_op jit(solution)/shard_map/ppermute | solution.py:624
  47.9 14.3 %copy-start = (f32[4,2,128,128]{3,2,1,0:T(8,128)S(1)}, f32[4,2,128,128]{3,2,1,0:T(8,128)}, u32[]{:S(2)}) copy-start(f32[4,2,128,128]{3,2,1,0:T(8,128)} %bubble_ref) | copy-start | bytes 1572868
  47.9 24.2 %all-to-all-start.1 = ((f32[128,16,128]{2,1,0:T(8,128)}), f32[128,16,128]{2,1,0:T(8,128)S(1)}, u32[]{:S(2)}, u32[]{:S(2)}) async-start(f32[128,16,128]{2,1,0:T(8,128)} %bitcast.48), calls=%async_computation.1 | async-start | bytes 2097152 | tf_op jit(solution)/shard_map/all_to_all | solution.py:586
  53.9 22.5 %collective-permute-start.7 = (f32[1,256,128]{2,1,0:T(8,128)S(1)}, f32[1,256,128]{2,1,0:T(8,128)S(1)}, u32[]{:S(2)}, u32[]{:S(2)}) collective-permute-start(f32[1,256,128]{2,1,0:T(8,128)S(1)} %bitcast.45), channel_id=1, source_target_pairs={{2,0},{3,1},{0,2},{1,3},{6,4},{7,5},{4,6},{5,7},{10,8},{11,9},{8,1... | collective-permute-start | bytes 393224 | tf_op jit(solution)/shard_map/ppermute | solution.py:620
  56.8 19.6 %collective-permute-start.8 = (f32[1,256,128]{2,1,0:T(8,128)S(1)}, f32[1,256,128]{2,1,0:T(8,128)S(1)}, u32[]{:S(2)}, u32[]{:S(2)}) collective-permute-start(f32[1,256,128]{2,1,0:T(8,128)S(1)} %bitcast.44), channel_id=1, source_target_pairs={{64,0},{65,1},{126,2},{127,3},{124,4},{125,5},{122,6},{123,7},{120... | collective-permute-start | bytes 393224 | tf_op jit(solution)/shard_map/ppermute | solution.py:620
  62.1 14.3 %collective-permute-start.9 = (f32[1,256,128]{2,1,0:T(8,128)S(1)}, f32[1,256,128]{2,1,0:T(8,128)S(1)}, u32[]{:S(2)}, u32[]{:S(2)}) collective-permute-start(f32[1,256,128]{2,1,0:T(8,128)S(1)} %bitcast.43), channel_id=1, source_target_pairs={{66,0},{67,1},{124,2},{125,3},{126,4},{127,5},{120,6},{121,7},{122... | collective-permute-start | bytes 393224 | tf_op jit(solution)/shard_map/ppermute | solution.py:620
  76.4 26.4 %all-to-all-start.2 = ((f32[128,16,128]{2,1,0:T(8,128)}), f32[128,16,128]{2,1,0:T(8,128)S(1)}, u32[]{:S(2)}, u32[]{:S(2)}) async-start(f32[128,16,128]{2,1,0:T(8,128)} %bitcast.46), calls=%async_computation.2 | async-start | bytes 2097152 | tf_op jit(solution)/shard_map/all_to_all | solution.py:586
  83.7 1.4 %collective-permute-start.10 = (f32[1,256,128]{2,1,0:T(8,128)S(1)}, f32[1,256,128]{2,1,0:T(8,128)S(1)}, u32[]{:S(2)}, u32[]{:S(2)}) collective-permute-start(f32[1,256,128]{2,1,0:T(8,128)S(1)} %bitcast.41), channel_id=1, source_target_pairs={{0,1},{1,0},{2,3},{3,2},{4,5},{5,4},{6,7},{7,6},{8,9},{9,8},{10,11... | collective-permute-start | bytes 393224 | tf_op jit(solution)/shard_map/ppermute | solution.py:624
  83.8 1.5 %collective-permute-start.11 = (f32[1,256,128]{2,1,0:T(8,128)S(1)}, f32[1,256,128]{2,1,0:T(8,128)S(1)}, u32[]{:S(2)}, u32[]{:S(2)}) collective-permute-start(f32[1,256,128]{2,1,0:T(8,128)S(1)} %collective-permute-done.7.refs_2_), channel_id=1, source_target_pairs={{0,1},{1,0},{2,3},{3,2},{4,5},{5,4},{6,7},{7,6},{8,9},{9,8},{10,11... | collective-permute-start | bytes 393224 | tf_op jit(solution)/shard_map/ppermute | solution.py:624
  84.3 1.3 %collective-permute-start.12 = (f32[1,256,128]{2,1,0:T(8,128)S(1)}, f32[1,256,128]{2,1,0:T(8,128)S(1)}, u32[]{:S(2)}, u32[]{:S(2)}) collective-permute-start(f32[1,256,128]{2,1,0:T(8,128)S(1)} %collective-permute-done.8.refs_3_), channel_id=1, source_target_pairs={{0,1},{1,0},{2,3},{3,2},{4,5},{5,4},{6,7},{7,6},{8,9},{9,8},{10,11... | collective-permute-start | bytes 393224 | tf_op jit(solution)/shard_map/ppermute | solution.py:624
  84.4 1.4 %collective-permute-start.13 = (f32[1,256,128]{2,1,0:T(8,128)S(1)}, f32[1,256,128]{2,1,0:T(8,128)S(1)}, u32[]{:S(2)}, u32[]{:S(2)}) collective-permute-start(f32[1,256,128]{2,1,0:T(8,128)S(1)} %collective-permute-done.9.refs_4_), channel_id=1, source_target_pairs={{0,1},{1,0},{2,3},{3,2},{4,5},{5,4},{6,7},{7,6},{8,9},{9,8},{10,11... | collective-permute-start | bytes 393224 | tf_op jit(solution)/shard_map/ppermute | solution.py:624

commit v4 on v3

--- a/solution.py
+++ b/solution.py
@@ -169,14 +169,10 @@
     plus_hbm, mirror_hbm, table_hbm, green_hbm, out0, out1, out2, out3, out_hbm,
     table_ref, green_ref, out_ref, row_sems, sems,
 ):
+    green_here = [fetch(green_hbm.at[:, 0], green_ref.at[0], sems.at[1])]
+    table_here = fetch(table_hbm, table_ref, sems.at[0])
     rows_gone = sort_rows((plus_hbm, mirror_hbm), (out0, out1, out2, out3), row_sems)
-    green_here = []
-    for tangent in range(2):
-        green_here.append(
-            fetch(green_hbm.at[:, tangent], green_ref.at[tangent], sems.at[1 + tangent])
-        )
-        if tangent == 0:
-            table_here = fetch(table_hbm, table_ref, sems.at[0])
+    green_here.append(fetch(green_hbm.at[:, 1], green_ref.at[1], sems.at[2]))
     left = []
     for tangent in range(2):
         green_here[tangent]()
@@ -200,7 +196,7 @@
     return (inv_real * inv_real - inv_imag * inv_imag, 2.0 * inv_real * inv_imag)
 
 
-def weight_kernel(bubble_ref, table_hbm, weight_hbm, table_ref, weight_ref, sems):
+def weight_kernel(bubble_ref, table_hbm, weight_ref, table_ref, sems):
     table_here = fetch(table_hbm, table_ref, sems.at[0])
     for kx in range(4):
         chi_real = bubble_ref[kx, 0]
@@ -210,24 +206,18 @@
         lanes = slice(kx * 128, kx * 128 + 128)
         weight_ref[0, :, lanes] = 1.5 * spin_real + 0.5 * charge_real - 1.0
         weight_ref[1, :, lanes] = 1.5 * spin_imag + 0.5 * charge_imag
-    gone = fetch(weight_ref, weight_hbm, sems.at[1])
     table_here()
-    gone()
 
 
 def middle_kernel(
-    in_table_ref, out_table_hbm, weight_hbm, in_ref, out_hbm,
-    out_table_ref, weight_ref, out_ref, sems,
+    in_table_ref, out_table_hbm, weight_ref, in_ref, out_hbm, out_table_ref, out_ref, sems
 ):
     left = []
-    weight_here = fetch(weight_hbm, weight_ref, sems.at[1])
     out_table_here = fetch(out_table_hbm, out_table_ref, sems.at[2])
     for core in range(2):
         high, low = halves(load_columns(core, in_ref))
         chi = dot3(in_table_ref[0], in_table_ref[1], high, low)
         real, imag = chi[:128], chi[128:]
-        if core == 0:
-            weight_here()
         weight_real, weight_imag = weight_ref[0], weight_ref[1]
         pot = jnp.concatenate(
             [
@@ -363,30 +353,15 @@
     return pl.ds(step * width, width)
 
 
-def fetch_fields(field_hbm, field_ref, sems):
-    return [
-        fetch(
-            field_hbm.at[pl.ds(0, field_ref.shape[0]), :, :, time_lanes(step, 128)],
-            field_ref.at[:, :, :, time_lanes(step, 128)],
-            sems.at[step],
-        )
-        for step in range(4)
-    ]
-
-
-def fetch_tables(hbm_refs, refs, sems):
-    return [fetch(hbm, ref, sems.at[place]) for place, (hbm, ref) in enumerate(zip(hbm_refs, refs))]
-
-
 def chi_kernel(*refs):
     x_in_ref, *tables_hbm = refs[:4]
     (in_ref, base_hbm, out_hbm, plus_hbm), tables = refs[4:8], refs[8:11]
-    base_ref, plus_ref, out_ref, left_ref, acc_ref, sems, base_sems, plus_sems, out_sems = refs[11:]
+    base_ref, plus_ref, out_ref, left_ref, acc_ref, sems, out_sems = refs[11:]
     t_in_ref, t_out_ref, x_out_ref = tables
     t_in_here = fetch(tables_hbm[0], t_in_ref, sems.at[0])
-    base_here = fetch_fields(base_hbm, base_ref, base_sems)
-    t_out_here = fetch(tables_hbm[1], t_out_ref, sems.at[1])
-    x_out_here = fetch(tables_hbm[2], x_out_ref, sems.at[2])
+    base_here = fetch(base_hbm, base_ref, sems.at[1])
+    t_out_here = fetch(tables_hbm[1], t_out_ref, sems.at[2])
+    x_out_here = fetch(tables_hbm[2], x_out_ref, sems.at[3])
     site, freq = lax.axis_index("site"), lax.axis_index("freq")
     alone = jnp.logical_and(site == 0, freq < 2)
     flip = (1 - 2 * lax.rem(lax.broadcasted_iota(jnp.int32, (256, 512), 0), 2)).astype(F32).astype(BF16)
@@ -401,16 +376,17 @@
         to_left(result, rows, left_ref)
 
     t_in_here()
-    plus_gone = []
     for step in range(4):
         times = to_times(step, left_ref, t_in_ref, -1)
         plus, minus = times[:256], times[256:]
         lanes = time_lanes(step, 256)
         plus_ref[:, lanes] = plus
-        plus_gone.append(fetch(plus_ref.at[:, lanes], plus_hbm.at[:, lanes], plus_sems.at[step]))
         plus_real, plus_imag = plus[:, :128], plus[:, 128:]
         minus_real, minus_imag = minus[:, :128], -minus[:, 128:]
-        base_here[step]()
+        if step == 0:
+            base_here()
+            t_out_here()
+            x_out_here()
         block = time_lanes(step, 128)
         base_real, base_imag = base_ref[0, 0, :, block], base_ref[0, 1, :, block]
         mirror_real, mirror_imag = base_ref[1, 0, :, block], base_ref[1, 1, :, block]
@@ -423,28 +399,27 @@
             + base_real * minus_imag + base_imag * minus_real
         )
         first, second = halves(-jnp.concatenate([chi_real, chi_imag], axis=1))
-        if step == 0:
-            t_out_here()
         accumulate(step, first, second, t_out_ref, acc_ref)
-    x_out_here()
+    plus_gone = fetch(plus_ref, plus_hbm, sems.at[4])
     finish(x_out_ref, acc_ref, out_ref, out_hbm, out_sems)
-    for gone in plus_gone:
-        gone()
+    plus_gone()
 
 
 def sigma_kernel(*refs):
     x_in_ref, *tables_hbm = refs[:4]
     in_ref, base_hbm, pot_hbm, plus_hbm, table_hbm, out_ref, table_ref = refs[4:11]
     tables, refs = refs[11:14], refs[14:]
-    base_ref, pot_ref, plus_ref, left_ref, acc_ref, sems, base_sems, pot_sems, plus_sem = refs
+    base_ref, pot_ref, plus_ref, left_ref, acc_ref, sems = refs
     t_in_ref, t_out_ref, x_out_ref = tables
-    t_in_here = fetch(tables_hbm[0], t_in_ref, sems.at[0])
-    plus_here = fetch(plus_hbm, plus_ref, plus_sem.at[0])
-    base_here = fetch_fields(base_hbm, base_ref, base_sems)
-    pot_here = fetch_fields(pot_hbm, pot_ref, pot_sems)
-    t_out_here = fetch(tables_hbm[1], t_out_ref, sems.at[1])
-    x_out_here = fetch(tables_hbm[2], x_out_ref, sems.at[2])
-    table_here = fetch(table_hbm, table_ref, plus_sem.at[1])
+    t_in_here = fetch(tables_hbm[0], t_in_ref, sems.at[2])
+    fields_here = [
+        fetch(plus_hbm, plus_ref, sems.at[3]),
+        fetch(base_hbm.at[pl.ds(0, 1)], base_ref, sems.at[4]),
+        fetch(pot_hbm, pot_ref, sems.at[5]),
+        fetch(tables_hbm[1], t_out_ref, sems.at[6]),
+    ]
+    x_out_here = fetch(tables_hbm[2], x_out_ref, sems.at[0])
+    table_here = fetch(table_hbm, table_ref, sems.at[1])
 
     for slab in range(2):
         high, low = halves(gather_slab(in_ref, slab))
@@ -455,9 +430,9 @@
     for step in range(4):
         change = to_times(step, left_ref, t_in_ref, -1)
         if step == 0:
-            plus_here()
-        base_here[step]()
-        pot_here[step]()
+            for field_here in fields_here:
+                field_here()
+            x_out_here()
         plus = plus_ref[:, time_lanes(step, 256)]
         block = time_lanes(step, 128)
         change_real, change_imag = change[:, :128], change[:, 128:]
@@ -473,10 +448,7 @@
             + change_real * base_imag + change_imag * base_real
         )
         first, second = halves(jnp.concatenate([real, imag], axis=1))
-        if step == 0:
-            t_out_here()
         accumulate(step, first, second, t_out_ref, acc_ref)
-    x_out_here()
     finish(x_out_ref, acc_ref, out_ref)
     table_here()
 
@@ -522,16 +494,15 @@
 
 def weight_call(bubble, table):
     shape = (2, 128, NF)
-    scratch = [pltpu.VMEM(shape, F32), sems(2)]
     return call(
-        weight_kernel, "weight", [HERE, HBM], [HBM, TABLE], [shape, table.shape], scratch, TURN, bubble, table
+        weight_kernel, "weight", [HERE, HBM], [HERE, TABLE], [shape, table.shape], [sems(1)], TURN, bubble, table
     )
 
 
 def middle_call(weight, momenta, columns, held):
-    scratch = [like(columns), like(weight), pltpu.VMEM((2048, 128), F32), sems(5)]
+    scratch = [like(columns), pltpu.VMEM((2048, 128), F32), sems(5)]
     return call(
-        middle_kernel, "middle", [HERE, HBM, HBM, HERE], [HBM], [(CHIPS, 32, 128)], scratch, 2 * TURN,
+        middle_kernel, "middle", [HERE, HBM, HERE, HERE], [HBM], [(CHIPS, 32, 128)], scratch, 2 * TURN,
         momenta, columns, weight, held,
     )[0]
 
@@ -562,7 +533,7 @@
 def chi_call(tables, held, base):
     scratch = [
         *map(like, tables[1:]), field(2), pltpu.VMEM(PLUS, F32), pltpu.VMEM(SLABS, F32),
-        pltpu.VMEM((4, 512, 256), F32), pltpu.VMEM((4, 256, 256), F32), sems(4), sems(4), sems(4), sems(2),
+        pltpu.VMEM((4, 512, 256), F32), pltpu.VMEM((4, 256, 256), F32), sems(5), sems(2),
     ]
     return call(
         chi_kernel, "chi", [HERE, HBM, HBM, HBM, HERE, HBM], [HBM, HBM], [SLABS, PLUS], scratch, 7 * TURN,
@@ -573,7 +544,7 @@
 def sigma_call(tables, held, base, pot, plus, table):
     scratch = [
         *map(like, tables[1:]), field(1), field(1), pltpu.VMEM(PLUS, F32),
-        pltpu.VMEM((4, 256, 256), F32), pltpu.VMEM((4, 256, 256), F32), sems(4), sems(4), sems(4), sems(2),
+        pltpu.VMEM((4, 256, 256), F32), pltpu.VMEM((4, 256, 256), F32), sems(7),
     ]
     return call(
         sigma_kernel, "sigma", [HERE, HBM, HBM, HBM, HERE, HBM, HBM, HBM, HBM], [HERE, TABLE],

time: 133 us -> 133 us (level)
  no operation moved by 1% of the time
where the time goes in v4:
time: 133 us; the launch traced here: 132 us
  starting transfers between devices  40.8 us (31%)
  waiting for transfers between devices  37.4 us (28%)
  Pallas kernels  30.4 us (23%)
  blocking collectives  23 us (17%)
    pallas_call x9, Pallas kernels, call(): pl.pallas_call(body, in_specs=in_specs, out_specs=out_specs, out_shape=[p...  30.4 us
    all_to_all x3, waiting for transfers between devices, exchange(): return lax.all_to_all(source, BOTH, split_axis=0, concat_axis=0, tiled=True)  28.8 us
    all_to_all x1, blocking collectives, exchange(): return lax.all_to_all(source, BOTH, split_axis=0, concat_axis=0, tiled=True)  23 us
    all_to_all x3, starting transfers between devices, exchange(): return lax.all_to_all(source, BOTH, split_axis=0, concat_axis=0, tiled=True)  20.9 us
    ppermute x6, starting transfers between devices, send(): lax.ppermute(rows[shift], BOTH, routes(shift))  18.1 us
    ppermute x6, waiting for transfers between devices, send(): lax.ppermute(rows[shift], BOTH, routes(shift))  6.06 us
  transfers between devices with their start and end apart: 17, of which 10 were waited for; matrix products, arithmetic and copies ran while one was open for 0% of the time, Pallas kernels for 11%

profile of v4, /device:TPU:0, one launch (start us, length us, event | category | flops | bytes accessed | tf_op | source)
XLA Modules:
  0.0 131.9 jit_solution(13321609480946946830)
XLA Ops:
  0.0 3.6 %begin.1 = (f32[2,64,4,1,128]{4,3,2,1,0:T(1,128)S(1)}, f32[2,64,4,1,128]{4,3,2,1,0:T(1,128)S(1)}, f32[2,64,4,1,128]{4,3,2,1,0:T(1,128)S(1)}, f32[2,64,4,1,128]{4,3,2,1,0:T(1,128)S(1)}, f32[64,32,128]{2,1,0:T(8,128)}) custom-call(f32[64,4,4,1,128]{4,3,2,1,0:T(1,128)} %bitcast.50, f32[64,4,4,1,128]{4,3,2,1,0:T(1,128)} %bitcast.51, ...), custom_call_target="tpu_custom_call" | custom-call | flops 402653184 | bytes 2359296 | tf_op jit(solution)/shard_map/begin/pallas_call | solution.py:465
  3.6 4.0 %collective-permute-start = (f32[2,256,128]{2,1,0:T(8,128)S(1)}, f32[2,256,128]{2,1,0:T(8,128)S(1)}, u32[]{:S(2)}, u32[]{:S(2)}) collective-permute-start(f32[2,256,128]{2,1,0:T(8,128)S(1)} %bitcast.40), channel_id=1, source_target_pairs={{2,0},{3,1},{0,2},{1,3},{6,4},{7,5},{4,6},{5,7},{10,8},{11,9},{8,1... | collective-permute-start | bytes 786440 | tf_op jit(solution)/shard_map/ppermute | solution.py:591
  7.6 5.7 %collective-permute-start.1 = (f32[2,256,128]{2,1,0:T(8,128)S(1)}, f32[2,256,128]{2,1,0:T(8,128)S(1)}, u32[]{:S(2)}, u32[]{:S(2)}) collective-permute-start(f32[2,256,128]{2,1,0:T(8,128)S(1)} %bitcast.39), channel_id=1, source_target_pairs={{64,0},{65,1},{126,2},{127,3},{124,4},{125,5},{122,6},{123,7},{120... | collective-permute-start | bytes 786440 | tf_op jit(solution)/shard_map/ppermute | solution.py:591
  13.3 0.0 collective-permute-start.2
  13.3 9.0 %all-to-all-start = ((f32[128,16,128]{2,1,0:T(8,128)}), f32[128,16,128]{2,1,0:T(8,128)S(1)}, u32[]{:S(2)}, u32[]{:S(2)}) async-start(f32[128,16,128]{2,1,0:T(8,128)} %bitcast.47), calls=%async_computation | async-start | bytes 2097152 | tf_op jit(solution)/shard_map/all_to_all | solution.py:557
  22.3 0.1 collective-permute-start.3
  22.4 0.0 collective-permute-done.refs_2_
  22.4 0.5 collective-permute-start.4
  22.9 0.0 collective-permute-done.1.refs_3_
  22.9 0.1 collective-permute-start.5
  23.0 5.4 %collective-permute-done.2.refs_4_ = f32[2,256,128]{2,1,0:T(8,128)S(1)} collective-permute-done((f32[2,256,128]{2,1,0:T(8,128)S(1)}, f32[2,256,128]{2,1,0:T(8,128)S(1)}, u32[]{:S(2)}, u32[]{:S(2)}) %collective-permute-start.2) | collective-permute-done | bytes 262176 | tf_op jit(solution)/shard_map/ppermute | solution.py:591
  28.4 0.0 collective-permute-start.6
  28.4 0.0 collective-permute-done.3.refs_5_
  28.4 0.0 collective-permute-done.4.refs_6_
  28.4 0.0 collective-permute-done.5.refs_7_
  28.4 1.5 %collective-permute-done.6.refs_8_ = f32[2,256,128]{2,1,0:T(8,128)S(1)} collective-permute-done((f32[2,256,128]{2,1,0:T(8,128)S(1)}, f32[2,256,128]{2,1,0:T(8,128)S(1)}, u32[]{:S(2)}, u32[]{:S(2)}) %collective-permute-start.6) | collective-permute-done | bytes 262176 | tf_op jit(solution)/shard_map/ppermute | solution.py:595
  29.9 4.2 %prepare.2 = (f32[2,2,256,512]{3,2,1,0:T(8,128)}, bf16[2,256,256]{2,1,0:T(8,128)(2,1)S(1)}) custom-call(bf16[512,512]{1,0:T(8,128)(2,1)} %constant.22.clone.order_hbm, bf16[2,256,256]{2,1,0:T(8,128)(2,1)} %constant.20.clone.refs_0_, f32[2,256,128]{2,1,0:T(8,128)S(1)} %bitcast.37, f32[2,256,128]{2,1,0:T(8,128)S(1)} %collective-permute-done.refs_2_, ...), custom_call_target="tpu_custom_call" | custom-call | flops 6442450944 | bytes 2883584 | tf_op jit(solution)/shard_map/prepare/pallas_call | solution.py:465
  34.2 7.2 %all-to-all-done = f32[128,16,128]{2,1,0:T(8,128)S(1)} async-done(((f32[128,16,128]{2,1,0:T(8,128)}), f32[128,16,128]{2,1,0:T(8,128)S(1)}, u32[]{:S(2)}, u32[]{:S(2)}) %all-to-all-start) | async-done | bytes 1048608 | tf_op jit(solution)/shard_map/all_to_all | solution.py:557
  41.4 6.1 %chi.1 = (f32[32,4,2,8,128]{4,3,2,1,0:T(8,128)}, f32[256,1024]{1,0:T(8,128)}) custom-call(bf16[2,256,256]{2,1,0:T(8,128)(2,1)S(1)} %get-tuple-element.40.refs_0_, bf16[4,2,256,256]{3,2,1,0:T(8,128)(2,1)} %constant.23.clone.refs_1_, bf16[4,2,256,256]{3,2,1,0:T(8,128)(2,1)} %constant.24.clone.refs_2_, bf16[2,256,256]{2,1,0:T(8,128)(2,1)} %constant.21.clone.refs_3_, ...), custom_call_target="tpu_custom_call" | custom-call | flops 2818572288 | bytes 5767168 | tf_op jit(solution)/shard_map/chi/pallas_call | solution.py:465
  47.5 0.0 copy-start
  47.5 4.8 %all-to-all-start.1 = ((f32[128,16,128]{2,1,0:T(8,128)}), f32[128,16,128]{2,1,0:T(8,128)S(1)}, u32[]{:S(2)}, u32[]{:S(2)}) async-start(f32[128,16,128]{2,1,0:T(8,128)} %bitcast.48), calls=%async_computation.1 | async-start | bytes 2097152 | tf_op jit(solution)/shard_map/all_to_all | solution.py:557
  52.3 1.1 pack.1
  53.4 2.9 %collective-permute-start.7 = (f32[1,256,128]{2,1,0:T(8,128)S(1)}, f32[1,256,128]{2,1,0:T(8,128)S(1)}, u32[]{:S(2)}, u32[]{:S(2)}) collective-permute-start(f32[1,256,128]{2,1,0:T(8,128)S(1)} %bitcast.45), channel_id=1, source_target_pairs={{2,0},{3,1},{0,2},{1,3},{6,4},{7,5},{4,6},{5,7},{10,8},{11,9},{8,1... | collective-permute-start | bytes 393224 | tf_op jit(solution)/shard_map/ppermute | solution.py:591
  56.4 5.3 %collective-permute-start.8 = (f32[1,256,128]{2,1,0:T(8,128)S(1)}, f32[1,256,128]{2,1,0:T(8,128)S(1)}, u32[]{:S(2)}, u32[]{:S(2)}) collective-permute-start(f32[1,256,128]{2,1,0:T(8,128)S(1)} %bitcast.44), channel_id=1, source_target_pairs={{64,0},{65,1},{126,2},{127,3},{124,4},{125,5},{122,6},{123,7},{120... | collective-permute-start | bytes 393224 | tf_op jit(solution)/shard_map/ppermute | solution.py:591
  61.7 0.2 collective-permute-start.9
  61.8 0.0 copy-done
  61.8 1.0 weight.1
  62.8 8.9 %all-to-all-done.1 = f32[128,16,128]{2,1,0:T(8,128)S(1)} async-done(((f32[128,16,128]{2,1,0:T(8,128)}), f32[128,16,128]{2,1,0:T(8,128)S(1)}, u32[]{:S(2)}, u32[]{:S(2)}) %all-to-all-start.1) | async-done | bytes 1048608 | tf_op jit(solution)/shard_map/all_to_all | solution.py:557
  71.7 3.5 %middle.1 = f32[64,32,128]{2,1,0:T(8,128)} custom-call(bf16[2,256,256]{2,1,0:T(8,128)(2,1)S(1)} %get-tuple-element.50.in_table_ref, bf16[2,256,256]{2,1,0:T(8,128)(2,1)} %constant.18.clone.table_hbm.out_table_hbm, f32[2,128,512]{2,1,0:T(8,128)S(1)} %get-tuple-element.51.weight_ref, f32[2048,128]{1,0:T(8,128)S(1)} %bitcast.31), custom_call_target="tpu_custom_call" | custom-call | flops 805306368 | bytes 2097152 | tf_op jit(solution)/shard_map/middle/pallas_call | solution.py:465
  75.2 0.7 collective-permute-done.7.refs_2_
  75.9 0.0 collective-permute-done.8.refs_3_
  75.9 0.0 collective-permute-done.9.refs_4_
  75.9 7.1 %all-to-all-start.2 = ((f32[128,16,128]{2,1,0:T(8,128)}), f32[128,16,128]{2,1,0:T(8,128)S(1)}, u32[]{:S(2)}, u32[]{:S(2)}) async-start(f32[128,16,128]{2,1,0:T(8,128)} %bitcast.46), calls=%async_computation.2 | async-start | bytes 2097152 | tf_op jit(solution)/shard_map/all_to_all | solution.py:557
  83.0 0.1 collective-permute-start.10
  83.1 0.5 collective-permute-start.11
  83.6 0.1 collective-permute-start.12
  83.7 0.4 collective-permute-start.13
  84.1 0.3 collective-permute-done.10.refs_5_
  84.4 0.2 collective-permute-done.11.refs_6_
  84.6 0.3 collective-permute-done.12.refs_7_
  84.9 0.2 collective-permute-done.13.refs_8_
  85.1 4.3 %prepare.3 = (f32[1,2,256,512]{3,2,1,0:T(8,128)}, bf16[2,256,256]{2,1,0:T(8,128)(2,1)S(1)}) custom-call(bf16[512,512]{1,0:T(8,128)(2,1)} %constant.22.clone.order_hbm, bf16[2,256,256]{2,1,0:T(8,128)(2,1)} %constant.20.clone.refs_0_, f32[1,256,128]{2,1,0:T(8,128)S(1)} %bitcast.42, f32[1,256,128]{2,1,0:T(8,128)S(1)} %collective-permute-done.7.refs_2_, ...), custom_call_target="tpu_custom_call" | custom-call | flops 6442450944 | bytes 1835008 | tf_op jit(solution)/shard_map/prepare/pallas_call | solution.py:465
  89.5 12.6 %all-to-all-done.2 = f32[128,16,128]{2,1,0:T(8,128)S(1)} async-done(((f32[128,16,128]{2,1,0:T(8,128)}), f32[128,16,128]{2,1,0:T(8,128)S(1)}, u32[]{:S(2)}, u32[]{:S(2)}) %all-to-all-start.2) | async-done | bytes 1048608 | tf_op jit(solution)/shard_map/all_to_all | solution.py:557
  102.1 4.8 %sigma.1 = (f32[32,4,2,8,128]{4,3,2,1,0:T(8,128)S(1)}, bf16[2,256,256]{2,1,0:T(8,128)(2,1)S(1)}) custom-call(bf16[2,256,256]{2,1,0:T(8,128)(2,1)S(1)} %get-tuple-element.57.refs_0_, bf16[4,2,256,256]{3,2,1,0:T(8,128)(2,1)} %constant.25.clone.refs_1_, bf16[4,2,256,256]{3,2,1,0:T(8,128)(2,1)} %constant.26.clone.refs_2_, ...), custom_call_target="tpu_custom_call" | custom-call | flops 1610612736 | bytes 8126464 | tf_op jit(solution)/shard_map/sigma/pallas_call | solution.py:465
  106.8 23.0 %all_to_all.20 = f32[128,16,128]{2,1,0:T(8,128)S(1)} all-to-all(f32[128,16,128]{2,1,0:T(8,128)S(1)} %bitcast.35), channel_id=1, replica_groups=mesh['site'=32,'freq'=4] {'site','freq'}, dimensions={0} | all-to-all | bytes 2097152 | tf_op jit(solution)/shard_map/all_to_all | solution.py:557
  129.9 1.9 %last.1 = f32[4,2,2,128,128]{4,3,2,1,0:T(8,128)} custom-call(bf16[2,256,256]{2,1,0:T(8,128)(2,1)S(1)} %get-tuple-element.61.table_ref, f32[2048,128]{1,0:T(8,128)S(1)} %bitcast.32), custom_call_target="tpu_custom_call" | custom-call | flops 402653184 | bytes 1310720 | tf_op jit(solution)/shard_map/last/pallas_call | solution.py:465
Async XLA Ops:
  3.6 18.9 %collective-permute-start = (f32[2,256,128]{2,1,0:T(8,128)S(1)}, f32[2,256,128]{2,1,0:T(8,128)S(1)}, u32[]{:S(2)}, u32[]{:S(2)}) collective-permute-start(f32[2,256,128]{2,1,0:T(8,128)S(1)} %bitcast.40), channel_id=1, source_target_pairs={{2,0},{3,1},{0,2},{1,3},{6,4},{7,5},{4,6},{5,7},{10,8},{11,9},{8,1... | collective-permute-start | bytes 786440 | tf_op jit(solution)/shard_map/ppermute | solution.py:591
  7.6 15.3 %collective-permute-start.1 = (f32[2,256,128]{2,1,0:T(8,128)S(1)}, f32[2,256,128]{2,1,0:T(8,128)S(1)}, u32[]{:S(2)}, u32[]{:S(2)}) collective-permute-start(f32[2,256,128]{2,1,0:T(8,128)S(1)} %bitcast.39), channel_id=1, source_target_pairs={{64,0},{65,1},{126,2},{127,3},{124,4},{125,5},{122,6},{123,7},{120... | collective-permute-start | bytes 786440 | tf_op jit(solution)/shard_map/ppermute | solution.py:591
  13.3 15.1 %collective-permute-start.2 = (f32[2,256,128]{2,1,0:T(8,128)S(1)}, f32[2,256,128]{2,1,0:T(8,128)S(1)}, u32[]{:S(2)}, u32[]{:S(2)}) collective-permute-start(f32[2,256,128]{2,1,0:T(8,128)S(1)} %bitcast.38), channel_id=1, source_target_pairs={{66,0},{67,1},{124,2},{125,3},{126,4},{127,5},{120,6},{121,7},{122... | collective-permute-start | bytes 786440 | tf_op jit(solution)/shard_map/ppermute | solution.py:591
  13.3 28.1 %all-to-all-start = ((f32[128,16,128]{2,1,0:T(8,128)}), f32[128,16,128]{2,1,0:T(8,128)S(1)}, u32[]{:S(2)}, u32[]{:S(2)}) async-start(f32[128,16,128]{2,1,0:T(8,128)} %bitcast.47), calls=%async_computation | async-start | bytes 2097152 | tf_op jit(solution)/shard_map/all_to_all | solution.py:557
  22.3 6.1 %collective-permute-start.3 = (f32[2,256,128]{2,1,0:T(8,128)S(1)}, f32[2,256,128]{2,1,0:T(8,128)S(1)}, u32[]{:S(2)}, u32[]{:S(2)}) collective-permute-start(f32[2,256,128]{2,1,0:T(8,128)S(1)} %bitcast.36), channel_id=1, source_target_pairs={{0,1},{1,0},{2,3},{3,2},{4,5},{5,4},{6,7},{7,6},{8,9},{9,8},{10,11... | collective-permute-start | bytes 786440 | tf_op jit(solution)/shard_map/ppermute | solution.py:595
  22.4 6.0 %collective-permute-start.4 = (f32[2,256,128]{2,1,0:T(8,128)S(1)}, f32[2,256,128]{2,1,0:T(8,128)S(1)}, u32[]{:S(2)}, u32[]{:S(2)}) collective-permute-start(f32[2,256,128]{2,1,0:T(8,128)S(1)} %collective-permute-done.refs_2_), channel_id=1, source_target_pairs={{0,1},{1,0},{2,3},{3,2},{4,5},{5,4},{6,7},{7,6},{8,9},{9,8},{10,11... | collective-permute-start | bytes 786440 | tf_op jit(solution)/shard_map/ppermute | solution.py:595
  22.9 5.5 %collective-permute-start.5 = (f32[2,256,128]{2,1,0:T(8,128)S(1)}, f32[2,256,128]{2,1,0:T(8,128)S(1)}, u32[]{:S(2)}, u32[]{:S(2)}) collective-permute-start(f32[2,256,128]{2,1,0:T(8,128)S(1)} %collective-permute-done.1.refs_3_), channel_id=1, source_target_pairs={{0,1},{1,0},{2,3},{3,2},{4,5},{5,4},{6,7},{7,6},{8,9},{9,8},{10,11... | collective-permute-start | bytes 786440 | tf_op jit(solution)/shard_map/ppermute | solution.py:595
  28.4 1.5 %collective-permute-start.6 = (f32[2,256,128]{2,1,0:T(8,128)S(1)}, f32[2,256,128]{2,1,0:T(8,128)S(1)}, u32[]{:S(2)}, u32[]{:S(2)}) collective-permute-start(f32[2,256,128]{2,1,0:T(8,128)S(1)} %collective-permute-done.2.refs_4_), channel_id=1, source_target_pairs={{0,1},{1,0},{2,3},{3,2},{4,5},{5,4},{6,7},{7,6},{8,9},{9,8},{10,11... | collective-permute-start | bytes 786440 | tf_op jit(solution)/shard_map/ppermute | solution.py:595
  47.5 14.3 %copy-start = (f32[4,2,128,128]{3,2,1,0:T(8,128)S(1)}, f32[4,2,128,128]{3,2,1,0:T(8,128)}, u32[]{:S(2)}) copy-start(f32[4,2,128,128]{3,2,1,0:T(8,128)} %bubble_ref) | copy-start | bytes 1572868
  47.5 24.2 %all-to-all-start.1 = ((f32[128,16,128]{2,1,0:T(8,128)}), f32[128,16,128]{2,1,0:T(8,128)S(1)}, u32[]{:S(2)}, u32[]{:S(2)}) async-start(f32[128,16,128]{2,1,0:T(8,128)} %bitcast.48), calls=%async_computation.1 | async-start | bytes 2097152 | tf_op jit(solution)/shard_map/all_to_all | solution.py:557
  53.4 22.5 %collective-permute-start.7 = (f32[1,256,128]{2,1,0:T(8,128)S(1)}, f32[1,256,128]{2,1,0:T(8,128)S(1)}, u32[]{:S(2)}, u32[]{:S(2)}) collective-permute-start(f32[1,256,128]{2,1,0:T(8,128)S(1)} %bitcast.45), channel_id=1, source_target_pairs={{2,0},{3,1},{0,2},{1,3},{6,4},{7,5},{4,6},{5,7},{10,8},{11,9},{8,1... | collective-permute-start | bytes 393224 | tf_op jit(solution)/shard_map/ppermute | solution.py:591
  56.4 19.6 %collective-permute-start.8 = (f32[1,256,128]{2,1,0:T(8,128)S(1)}, f32[1,256,128]{2,1,0:T(8,128)S(1)}, u32[]{:S(2)}, u32[]{:S(2)}) collective-permute-start(f32[1,256,128]{2,1,0:T(8,128)S(1)} %bitcast.44), channel_id=1, source_target_pairs={{64,0},{65,1},{126,2},{127,3},{124,4},{125,5},{122,6},{123,7},{120... | collective-permute-start | bytes 393224 | tf_op jit(solution)/shard_map/ppermute | solution.py:591
  61.7 14.3 %collective-permute-start.9 = (f32[1,256,128]{2,1,0:T(8,128)S(1)}, f32[1,256,128]{2,1,0:T(8,128)S(1)}, u32[]{:S(2)}, u32[]{:S(2)}) collective-permute-start(f32[1,256,128]{2,1,0:T(8,128)S(1)} %bitcast.43), channel_id=1, source_target_pairs={{66,0},{67,1},{124,2},{125,3},{126,4},{127,5},{120,6},{121,7},{122... | collective-permute-start | bytes 393224 | tf_op jit(solution)/shard_map/ppermute | solution.py:591
  75.9 26.1 %all-to-all-start.2 = ((f32[128,16,128]{2,1,0:T(8,128)}), f32[128,16,128]{2,1,0:T(8,128)S(1)}, u32[]{:S(2)}, u32[]{:S(2)}) async-start(f32[128,16,128]{2,1,0:T(8,128)} %bitcast.46), calls=%async_computation.2 | async-start | bytes 2097152 | tf_op jit(solution)/shard_map/all_to_all | solution.py:557
  83.0 1.4 %collective-permute-start.10 = (f32[1,256,128]{2,1,0:T(8,128)S(1)}, f32[1,256,128]{2,1,0:T(8,128)S(1)}, u32[]{:S(2)}, u32[]{:S(2)}) collective-permute-start(f32[1,256,128]{2,1,0:T(8,128)S(1)} %bitcast.41), channel_id=1, source_target_pairs={{0,1},{1,0},{2,3},{3,2},{4,5},{5,4},{6,7},{7,6},{8,9},{9,8},{10,11... | collective-permute-start | bytes 393224 | tf_op jit(solution)/shard_map/ppermute | solution.py:595
  83.1 1.5 %collective-permute-start.11 = (f32[1,256,128]{2,1,0:T(8,128)S(1)}, f32[1,256,128]{2,1,0:T(8,128)S(1)}, u32[]{:S(2)}, u32[]{:S(2)}) collective-permute-start(f32[1,256,128]{2,1,0:T(8,128)S(1)} %collective-permute-done.7.refs_2_), channel_id=1, source_target_pairs={{0,1},{1,0},{2,3},{3,2},{4,5},{5,4},{6,7},{7,6},{8,9},{9,8},{10,11... | collective-permute-start | bytes 393224 | tf_op jit(solution)/shard_map/ppermute | solution.py:595
  83.6 1.3 %collective-permute-start.12 = (f32[1,256,128]{2,1,0:T(8,128)S(1)}, f32[1,256,128]{2,1,0:T(8,128)S(1)}, u32[]{:S(2)}, u32[]{:S(2)}) collective-permute-start(f32[1,256,128]{2,1,0:T(8,128)S(1)} %collective-permute-done.8.refs_3_), channel_id=1, source_target_pairs={{0,1},{1,0},{2,3},{3,2},{4,5},{5,4},{6,7},{7,6},{8,9},{9,8},{10,11... | collective-permute-start | bytes 393224 | tf_op jit(solution)/shard_map/ppermute | solution.py:595
  83.7 1.4 %collective-permute-start.13 = (f32[1,256,128]{2,1,0:T(8,128)S(1)}, f32[1,256,128]{2,1,0:T(8,128)S(1)}, u32[]{:S(2)}, u32[]{:S(2)}) collective-permute-start(f32[1,256,128]{2,1,0:T(8,128)S(1)} %collective-permute-done.9.refs_4_), channel_id=1, source_target_pairs={{0,1},{1,0},{2,3},{3,2},{4,5},{5,4},{6,7},{7,6},{8,9},{9,8},{10,11... | collective-permute-start | bytes 393224 | tf_op jit(solution)/shard_map/ppermute | solution.py:595

commit v5 on v4

--- a/solution.py
+++ b/solution.py
@@ -1,3 +1,4 @@
+import functools
 import math
 
 import jax
@@ -315,10 +316,14 @@
             acc_ref[high] = update
 
 
-def prepare_kernel(order_hbm, *refs):
-    table_hbm, pieces, (out_hbm, table_ref, order_ref, out_ref, sems) = refs[0], refs[1:9], refs[9:]
+def prepare_kernel(count, stay, order_hbm, *refs):
+    tables_hbm, pieces, tables = refs[:count], refs[count : count + 8], refs[count + 8 : 2 * count + 8]
+    result, order_ref, sems, *rest = refs[2 * count + 8 :]
+    out_ref = result if stay else rest[0]
     order_here = fetch(order_hbm, order_ref, sems.at[0])
-    table_here = fetch(table_hbm, table_ref, sems.at[2])
+    tables_here = [
+        fetch(hbm, ref, sems.at[2 + place]) for place, (hbm, ref) in enumerate(zip(tables_hbm, tables))
+    ]
     for place, ref in enumerate(pieces):
         arrays = ref.shape[0]
         value = jnp.concatenate(
@@ -344,9 +349,10 @@
             for part in range(2):
                 top = (array * 2 + part) * 32
                 out_ref[array, part, rows, :] = moved[top : top + 32]
-    gone = fetch(out_ref, out_hbm, sems.at[1])
-    table_here()
-    gone()
+    if not stay:
+        fetch(out_ref, result, sems.at[1])()
+    for table_here in tables_here:
+        table_here()
 
 
 def time_lanes(step, width):
@@ -385,8 +391,6 @@
         minus_real, minus_imag = minus[:, :128], -minus[:, 128:]
         if step == 0:
             base_here()
-            t_out_here()
-            x_out_here()
         block = time_lanes(step, 128)
         base_real, base_imag = base_ref[0, 0, :, block], base_ref[0, 1, :, block]
         mirror_real, mirror_imag = base_ref[1, 0, :, block], base_ref[1, 1, :, block]
@@ -399,7 +403,10 @@
             + base_real * minus_imag + base_imag * minus_real
         )
         first, second = halves(-jnp.concatenate([chi_real, chi_imag], axis=1))
+        if step == 0:
+            t_out_here()
         accumulate(step, first, second, t_out_ref, acc_ref)
+    x_out_here()
     plus_gone = fetch(plus_ref, plus_hbm, sems.at[4])
     finish(x_out_ref, acc_ref, out_ref, out_hbm, out_sems)
     plus_gone()
@@ -407,17 +414,16 @@
 
 def sigma_kernel(*refs):
     x_in_ref, *tables_hbm = refs[:4]
-    in_ref, base_hbm, pot_hbm, plus_hbm, table_hbm, out_ref, table_ref = refs[4:11]
+    in_ref, base_hbm, pot_ref, plus_hbm, table_hbm, out_ref, table_ref = refs[4:11]
     tables, refs = refs[11:14], refs[14:]
-    base_ref, pot_ref, plus_ref, left_ref, acc_ref, sems = refs
+    base_ref, plus_ref, left_ref, acc_ref, sems = refs
     t_in_ref, t_out_ref, x_out_ref = tables
     t_in_here = fetch(tables_hbm[0], t_in_ref, sems.at[2])
     fields_here = [
         fetch(plus_hbm, plus_ref, sems.at[3]),
         fetch(base_hbm.at[pl.ds(0, 1)], base_ref, sems.at[4]),
-        fetch(pot_hbm, pot_ref, sems.at[5]),
-        fetch(tables_hbm[1], t_out_ref, sems.at[6]),
     ]
+    t_out_here = fetch(tables_hbm[1], t_out_ref, sems.at[6])
     x_out_here = fetch(tables_hbm[2], x_out_ref, sems.at[0])
     table_here = fetch(table_hbm, table_ref, sems.at[1])
 
@@ -432,7 +438,6 @@
         if step == 0:
             for field_here in fields_here:
                 field_here()
-            x_out_here()
         plus = plus_ref[:, time_lanes(step, 256)]
         block = time_lanes(step, 128)
         change_real, change_imag = change[:, :128], change[:, 128:]
@@ -448,7 +453,10 @@
             + change_real * base_imag + change_imag * base_real
         )
         first, second = halves(jnp.concatenate([real, imag], axis=1))
+        if step == 0:
+            t_out_here()
         accumulate(step, first, second, t_out_ref, acc_ref)
+    x_out_here()
     finish(x_out_ref, acc_ref, out_ref)
     table_here()
 
@@ -513,13 +521,15 @@
     return call(last_kernel, "last", [HERE, HERE], [HBM], [shape], scratch, TURN, table, held)[0]
 
 
-def prepare_call(pieces, table):
+def prepare_call(pieces, tables, stay):
     shape = (pieces[0].shape[0], 2, 256, NF)
     order = jnp.asarray(t_order())
-    scratch = [like(order), pltpu.VMEM(shape, F32), sems(3)]
+    count = len(tables)
     return call(
-        prepare_kernel, "prepare", [HBM, HBM] + [HERE] * 8, [HBM, TABLE], [shape, table.shape], scratch,
-        WORK, order, table, *pieces,
+        functools.partial(prepare_kernel, count, stay), "prepare", [HBM] * (1 + count) + [HERE] * 8,
+        [TABLE] * count + [HERE if stay else HBM], [*(table.shape for table in tables), shape],
+        [like(order), sems(2 + count)] + ([] if stay else [pltpu.VMEM(shape, F32)]),
+        WORK, order, *tables, *pieces,
     )
 
 
@@ -543,11 +553,11 @@
 
 def sigma_call(tables, held, base, pot, plus, table):
     scratch = [
-        *map(like, tables[1:]), field(1), field(1), pltpu.VMEM(PLUS, F32),
+        *map(like, tables[1:]), field(1), pltpu.VMEM(PLUS, F32),
         pltpu.VMEM((4, 256, 256), F32), pltpu.VMEM((4, 256, 256), F32), sems(7),
     ]
     return call(
-        sigma_kernel, "sigma", [HERE, HBM, HBM, HBM, HERE, HBM, HBM, HBM, HBM], [HERE, TABLE],
+        sigma_kernel, "sigma", [HERE, HBM, HBM, HBM, HERE, HBM, HERE, HBM, HBM], [HERE, TABLE],
         [SLABS, table.shape], scratch, 4 * TURN, *tables, held.reshape(SLABS), base, pot, plus, table,
     )
 
@@ -599,7 +609,7 @@
     columns, momenta = jnp.asarray(y_to_columns()), jnp.asarray(y_to_momenta())
     x_table, back = jnp.asarray(split(x_in(1))), jnp.asarray(x_out())
     packed, sent = begin([green_plus, green_mirror], columns, green_tangent)
-    base, x_here = prepare_call(both_cores(send(packed)), x_table)
+    x_here, base = prepare_call(both_cores(send(packed)), [x_table], False)
     potential, sent = lax.optimization_barrier((potential, sent))
     held = exchange(sent)
     tables = (x_here, jnp.asarray(t_in(FERMI, -1)), jnp.asarray(t_out(BOSE, 1)), back)
@@ -610,7 +620,7 @@
     held = exchange(sent).reshape(2048, 128)
     sent = middle_call(weight, momenta_here, columns, held)
     own, sent = lax.optimization_barrier((own, sent))
-    pot, x_here = prepare_call(both_cores(own), x_table)
+    x_here, pot = prepare_call(both_cores(own), [x_table], True)
     held = exchange(sent)
     tables = (x_here, jnp.asarray(t_in(BOSE, -1)), jnp.asarray(t_out(FERMI, 1)), back)
     sent, momenta_here = sigma_call(tables, held, base, pot, plus, momenta)

time: 133 us -> 132 us (level)
  Pallas kernels: 30.4 us -> 29 us
    pallas_call x9, Pallas kernels: 30.4 us -> 29 us  [call(): pl.pallas_call(body, in_specs=in_specs, out_specs=out_specs, out_shape=[p...]
  transfers between devices with their start and end apart: 17 -> 17, of which waited for: 10 -> 10; matrix products, arithmetic and copies ran while one was open for 0% -> 0% of each run, Pallas kernels for 11% -> 10%
where the time goes in v5:
time: 132 us; the launch traced here: 131 us
  starting transfers between devices  40.8 us (31%)
  waiting for transfers between devices  38.3 us (29%)
  Pallas kernels  29 us (22%)
  blocking collectives  23 us (17%)
    all_to_all x3, waiting for transfers between devices, exchange(): return lax.all_to_all(source, BOTH, split_axis=0, concat_axis=0, tiled=True)  29.7 us
    pallas_call x9, Pallas kernels, call(): pl.pallas_call(body, in_specs=in_specs, out_specs=out_specs, out_shape=[p...  29 us
    all_to_all x1, blocking collectives, exchange(): return lax.all_to_all(source, BOTH, split_axis=0, concat_axis=0, tiled=True)  23 us
    all_to_all x3, starting transfers between devices, exchange(): return lax.all_to_all(source, BOTH, split_axis=0, concat_axis=0, tiled=True)  20.9 us
    ppermute x6, starting transfers between devices, send(): lax.ppermute(rows[shift], BOTH, routes(shift))  18.1 us
    ppermute x6, waiting for transfers between devices, send(): lax.ppermute(rows[shift], BOTH, routes(shift))  6.08 us
  transfers between devices with their start and end apart: 17, of which 10 were waited for; matrix products, arithmetic and copies ran while one was open for 0% of the time, Pallas kernels for 10%

profile of v5, /device:TPU:0, one launch (start us, length us, event | category | flops | bytes accessed | tf_op | source)
XLA Modules:
  0.0 131.5 jit_solution(4395657986044455092)
XLA Ops:
  0.0 3.6 %begin.1 = (f32[2,64,4,1,128]{4,3,2,1,0:T(1,128)S(1)}, f32[2,64,4,1,128]{4,3,2,1,0:T(1,128)S(1)}, f32[2,64,4,1,128]{4,3,2,1,0:T(1,128)S(1)}, f32[2,64,4,1,128]{4,3,2,1,0:T(1,128)S(1)}, f32[64,32,128]{2,1,0:T(8,128)}) custom-call(f32[64,4,4,1,128]{4,3,2,1,0:T(1,128)} %bitcast.50, f32[64,4,4,1,128]{4,3,2,1,0:T(1,128)} %bitcast.51, ...), custom_call_target="tpu_custom_call" | custom-call | flops 402653184 | bytes 2359296 | tf_op jit(solution)/shard_map/begin/pallas_call | solution.py:473
  3.6 4.0 %collective-permute-start = (f32[2,256,128]{2,1,0:T(8,128)S(1)}, f32[2,256,128]{2,1,0:T(8,128)S(1)}, u32[]{:S(2)}, u32[]{:S(2)}) collective-permute-start(f32[2,256,128]{2,1,0:T(8,128)S(1)} %bitcast.40), channel_id=1, source_target_pairs={{2,0},{3,1},{0,2},{1,3},{6,4},{7,5},{4,6},{5,7},{10,8},{11,9},{8,1... | collective-permute-start | bytes 786440 | tf_op jit(solution)/shard_map/ppermute | solution.py:601
  7.6 5.7 %collective-permute-start.1 = (f32[2,256,128]{2,1,0:T(8,128)S(1)}, f32[2,256,128]{2,1,0:T(8,128)S(1)}, u32[]{:S(2)}, u32[]{:S(2)}) collective-permute-start(f32[2,256,128]{2,1,0:T(8,128)S(1)} %bitcast.39), channel_id=1, source_target_pairs={{64,0},{65,1},{126,2},{127,3},{124,4},{125,5},{122,6},{123,7},{120... | collective-permute-start | bytes 786440 | tf_op jit(solution)/shard_map/ppermute | solution.py:601
  13.3 0.0 collective-permute-start.2
  13.3 9.0 %all-to-all-start = ((f32[128,16,128]{2,1,0:T(8,128)}), f32[128,16,128]{2,1,0:T(8,128)S(1)}, u32[]{:S(2)}, u32[]{:S(2)}) async-start(f32[128,16,128]{2,1,0:T(8,128)} %bitcast.47), calls=%async_computation | async-start | bytes 2097152 | tf_op jit(solution)/shard_map/all_to_all | solution.py:567
  22.3 0.1 collective-permute-start.3
  22.4 0.0 collective-permute-done.refs_2_
  22.4 0.5 collective-permute-start.4
  22.9 0.0 collective-permute-done.1.refs_3_
  22.9 0.1 collective-permute-start.5
  23.0 5.4 %collective-permute-done.2.refs_4_ = f32[2,256,128]{2,1,0:T(8,128)S(1)} collective-permute-done((f32[2,256,128]{2,1,0:T(8,128)S(1)}, f32[2,256,128]{2,1,0:T(8,128)S(1)}, u32[]{:S(2)}, u32[]{:S(2)}) %collective-permute-start.2) | collective-permute-done | bytes 262176 | tf_op jit(solution)/shard_map/ppermute | solution.py:601
  28.4 0.0 collective-permute-start.6
  28.4 0.0 collective-permute-done.3.refs_5_
  28.4 0.0 collective-permute-done.4.refs_6_
  28.4 0.0 collective-permute-done.5.refs_7_
  28.4 1.5 %collective-permute-done.6.refs_8_ = f32[2,256,128]{2,1,0:T(8,128)S(1)} collective-permute-done((f32[2,256,128]{2,1,0:T(8,128)S(1)}, f32[2,256,128]{2,1,0:T(8,128)S(1)}, u32[]{:S(2)}, u32[]{:S(2)}) %collective-permute-start.6) | collective-permute-done | bytes 262176 | tf_op jit(solution)/shard_map/ppermute | solution.py:605
  29.9 4.2 %prepare.2 = (bf16[2,256,256]{2,1,0:T(8,128)(2,1)S(1)}, f32[2,2,256,512]{3,2,1,0:T(8,128)}) custom-call(bf16[512,512]{1,0:T(8,128)(2,1)} %constant.22.clone.order_hbm, bf16[2,256,256]{2,1,0:T(8,128)(2,1)} %constant.20.clone.refs_0_, f32[2,256,128]{2,1,0:T(8,128)S(1)} %bitcast.37, f32[2,256,128]{2,1,0:T(8,128)S(1)} %collective-permute-done.refs_2_, ...), custom_call_target="tpu_custom_call" | custom-call | flops 6442450944 | bytes 2883584 | tf_op jit(solution)/shard_map/prepare/pallas_call | solution.py:473
  34.2 7.2 %all-to-all-done = f32[128,16,128]{2,1,0:T(8,128)S(1)} async-done(((f32[128,16,128]{2,1,0:T(8,128)}), f32[128,16,128]{2,1,0:T(8,128)S(1)}, u32[]{:S(2)}, u32[]{:S(2)}) %all-to-all-start) | async-done | bytes 1048608 | tf_op jit(solution)/shard_map/all_to_all | solution.py:567
  41.4 6.1 %chi.1 = (f32[32,4,2,8,128]{4,3,2,1,0:T(8,128)}, f32[256,1024]{1,0:T(8,128)}) custom-call(bf16[2,256,256]{2,1,0:T(8,128)(2,1)S(1)} %get-tuple-element.40.refs_0_, bf16[4,2,256,256]{3,2,1,0:T(8,128)(2,1)} %constant.23.clone.refs_1_, bf16[4,2,256,256]{3,2,1,0:T(8,128)(2,1)} %constant.24.clone.refs_2_, bf16[2,256,256]{2,1,0:T(8,128)(2,1)} %constant.21.clone.refs_3_, ...), custom_call_target="tpu_custom_call" | custom-call | flops 2818572288 | bytes 5767168 | tf_op jit(solution)/shard_map/chi/pallas_call | solution.py:473
  47.5 0.0 copy-start
  47.5 4.8 %all-to-all-start.1 = ((f32[128,16,128]{2,1,0:T(8,128)}), f32[128,16,128]{2,1,0:T(8,128)S(1)}, u32[]{:S(2)}, u32[]{:S(2)}) async-start(f32[128,16,128]{2,1,0:T(8,128)} %bitcast.48), calls=%async_computation.1 | async-start | bytes 2097152 | tf_op jit(solution)/shard_map/all_to_all | solution.py:567
  52.3 1.1 pack.1
  53.4 2.9 %collective-permute-start.7 = (f32[1,256,128]{2,1,0:T(8,128)S(1)}, f32[1,256,128]{2,1,0:T(8,128)S(1)}, u32[]{:S(2)}, u32[]{:S(2)}) collective-permute-start(f32[1,256,128]{2,1,0:T(8,128)S(1)} %bitcast.45), channel_id=1, source_target_pairs={{2,0},{3,1},{0,2},{1,3},{6,4},{7,5},{4,6},{5,7},{10,8},{11,9},{8,1... | collective-permute-start | bytes 393224 | tf_op jit(solution)/shard_map/ppermute | solution.py:601
  56.4 5.3 %collective-permute-start.8 = (f32[1,256,128]{2,1,0:T(8,128)S(1)}, f32[1,256,128]{2,1,0:T(8,128)S(1)}, u32[]{:S(2)}, u32[]{:S(2)}) collective-permute-start(f32[1,256,128]{2,1,0:T(8,128)S(1)} %bitcast.44), channel_id=1, source_target_pairs={{64,0},{65,1},{126,2},{127,3},{124,4},{125,5},{122,6},{123,7},{120... | collective-permute-start | bytes 393224 | tf_op jit(solution)/shard_map/ppermute | solution.py:601
  61.7 0.2 collective-permute-start.9
  61.8 0.0 copy-done
  61.8 1.0 weight.1
  62.8 8.9 %all-to-all-done.1 = f32[128,16,128]{2,1,0:T(8,128)S(1)} async-done(((f32[128,16,128]{2,1,0:T(8,128)}), f32[128,16,128]{2,1,0:T(8,128)S(1)}, u32[]{:S(2)}, u32[]{:S(2)}) %all-to-all-start.1) | async-done | bytes 1048608 | tf_op jit(solution)/shard_map/all_to_all | solution.py:567
  71.7 3.5 %middle.1 = f32[64,32,128]{2,1,0:T(8,128)} custom-call(bf16[2,256,256]{2,1,0:T(8,128)(2,1)S(1)} %get-tuple-element.50.in_table_ref, bf16[2,256,256]{2,1,0:T(8,128)(2,1)} %constant.18.clone.table_hbm.out_table_hbm, f32[2,128,512]{2,1,0:T(8,128)S(1)} %get-tuple-element.51.weight_ref, f32[2048,128]{1,0:T(8,128)S(1)} %bitcast.31), custom_call_target="tpu_custom_call" | custom-call | flops 805306368 | bytes 2097152 | tf_op jit(solution)/shard_map/middle/pallas_call | solution.py:473
  75.2 0.7 collective-permute-done.7.refs_2_
  75.9 0.0 collective-permute-done.8.refs_3_
  75.9 0.0 collective-permute-done.9.refs_4_
  75.9 7.1 %all-to-all-start.2 = ((f32[128,16,128]{2,1,0:T(8,128)}), f32[128,16,128]{2,1,0:T(8,128)S(1)}, u32[]{:S(2)}, u32[]{:S(2)}) async-start(f32[128,16,128]{2,1,0:T(8,128)} %bitcast.46), calls=%async_computation.2 | async-start | bytes 2097152 | tf_op jit(solution)/shard_map/all_to_all | solution.py:567
  83.0 0.1 collective-permute-start.10
  83.1 0.5 collective-permute-start.11
  83.6 0.1 collective-permute-start.12
  83.7 0.4 collective-permute-start.13
  84.1 0.3 collective-permute-done.10.refs_5_
  84.4 0.2 collective-permute-done.11.refs_6_
  84.6 0.3 collective-permute-done.12.refs_7_
  84.9 0.2 collective-permute-done.13.refs_8_
  85.1 3.4 %prepare.3 = (bf16[2,256,256]{2,1,0:T(8,128)(2,1)S(1)}, f32[1,2,256,512]{3,2,1,0:T(8,128)S(1)}) custom-call(bf16[512,512]{1,0:T(8,128)(2,1)} %constant.22.clone.order_hbm, bf16[2,256,256]{2,1,0:T(8,128)(2,1)} %constant.20.clone.refs_0_, f32[1,256,128]{2,1,0:T(8,128)S(1)} %bitcast.42, f32[1,256,128]{2,1,0:T(8,128)S(1)} %collective-permute-done.7.refs_2_, ...), custom_call_target="tpu_custom_call" | custom-call | flops 6442450944 | bytes 1835008 | tf_op jit(solution)/shard_map/prepare/pallas_call | solution.py:473
  88.5 13.6 %all-to-all-done.2 = f32[128,16,128]{2,1,0:T(8,128)S(1)} async-done(((f32[128,16,128]{2,1,0:T(8,128)}), f32[128,16,128]{2,1,0:T(8,128)S(1)}, u32[]{:S(2)}, u32[]{:S(2)}) %all-to-all-start.2) | async-done | bytes 1048608 | tf_op jit(solution)/shard_map/all_to_all | solution.py:567
  102.0 4.3 %sigma.1 = (f32[32,4,2,8,128]{4,3,2,1,0:T(8,128)S(1)}, bf16[2,256,256]{2,1,0:T(8,128)(2,1)S(1)}) custom-call(bf16[2,256,256]{2,1,0:T(8,128)(2,1)S(1)} %get-tuple-element.57.refs_0_, bf16[4,2,256,256]{3,2,1,0:T(8,128)(2,1)} %constant.25.clone.refs_1_, bf16[4,2,256,256]{3,2,1,0:T(8,128)(2,1)} %constant.26.clone.refs_2_, ...), custom_call_target="tpu_custom_call" | custom-call | flops 1610612736 | bytes 8126464 | tf_op jit(solution)/shard_map/sigma/pallas_call | solution.py:473
  106.4 23.0 %all_to_all.20 = f32[128,16,128]{2,1,0:T(8,128)S(1)} all-to-all(f32[128,16,128]{2,1,0:T(8,128)S(1)} %bitcast.35), channel_id=1, replica_groups=mesh['site'=32,'freq'=4] {'site','freq'}, dimensions={0} | all-to-all | bytes 2097152 | tf_op jit(solution)/shard_map/all_to_all | solution.py:567
  129.4 1.9 %last.1 = f32[4,2,2,128,128]{4,3,2,1,0:T(8,128)} custom-call(bf16[2,256,256]{2,1,0:T(8,128)(2,1)S(1)} %get-tuple-element.61.table_ref, f32[2048,128]{1,0:T(8,128)S(1)} %bitcast.32), custom_call_target="tpu_custom_call" | custom-call | flops 402653184 | bytes 1310720 | tf_op jit(solution)/shard_map/last/pallas_call | solution.py:473
Async XLA Ops:
  3.6 18.9 %collective-permute-start = (f32[2,256,128]{2,1,0:T(8,128)S(1)}, f32[2,256,128]{2,1,0:T(8,128)S(1)}, u32[]{:S(2)}, u32[]{:S(2)}) collective-permute-start(f32[2,256,128]{2,1,0:T(8,128)S(1)} %bitcast.40), channel_id=1, source_target_pairs={{2,0},{3,1},{0,2},{1,3},{6,4},{7,5},{4,6},{5,7},{10,8},{11,9},{8,1... | collective-permute-start | bytes 786440 | tf_op jit(solution)/shard_map/ppermute | solution.py:601
  7.6 15.3 %collective-permute-start.1 = (f32[2,256,128]{2,1,0:T(8,128)S(1)}, f32[2,256,128]{2,1,0:T(8,128)S(1)}, u32[]{:S(2)}, u32[]{:S(2)}) collective-permute-start(f32[2,256,128]{2,1,0:T(8,128)S(1)} %bitcast.39), channel_id=1, source_target_pairs={{64,0},{65,1},{126,2},{127,3},{124,4},{125,5},{122,6},{123,7},{120... | collective-permute-start | bytes 786440 | tf_op jit(solution)/shard_map/ppermute | solution.py:601
  13.3 15.1 %collective-permute-start.2 = (f32[2,256,128]{2,1,0:T(8,128)S(1)}, f32[2,256,128]{2,1,0:T(8,128)S(1)}, u32[]{:S(2)}, u32[]{:S(2)}) collective-permute-start(f32[2,256,128]{2,1,0:T(8,128)S(1)} %bitcast.38), channel_id=1, source_target_pairs={{66,0},{67,1},{124,2},{125,3},{126,4},{127,5},{120,6},{121,7},{122... | collective-permute-start | bytes 786440 | tf_op jit(solution)/shard_map/ppermute | solution.py:601
  13.3 28.1 %all-to-all-start = ((f32[128,16,128]{2,1,0:T(8,128)}), f32[128,16,128]{2,1,0:T(8,128)S(1)}, u32[]{:S(2)}, u32[]{:S(2)}) async-start(f32[128,16,128]{2,1,0:T(8,128)} %bitcast.47), calls=%async_computation | async-start | bytes 2097152 | tf_op jit(solution)/shard_map/all_to_all | solution.py:567
  22.3 6.1 %collective-permute-start.3 = (f32[2,256,128]{2,1,0:T(8,128)S(1)}, f32[2,256,128]{2,1,0:T(8,128)S(1)}, u32[]{:S(2)}, u32[]{:S(2)}) collective-permute-start(f32[2,256,128]{2,1,0:T(8,128)S(1)} %bitcast.36), channel_id=1, source_target_pairs={{0,1},{1,0},{2,3},{3,2},{4,5},{5,4},{6,7},{7,6},{8,9},{9,8},{10,11... | collective-permute-start | bytes 786440 | tf_op jit(solution)/shard_map/ppermute | solution.py:605
  22.4 6.0 %collective-permute-start.4 = (f32[2,256,128]{2,1,0:T(8,128)S(1)}, f32[2,256,128]{2,1,0:T(8,128)S(1)}, u32[]{:S(2)}, u32[]{:S(2)}) collective-permute-start(f32[2,256,128]{2,1,0:T(8,128)S(1)} %collective-permute-done.refs_2_), channel_id=1, source_target_pairs={{0,1},{1,0},{2,3},{3,2},{4,5},{5,4},{6,7},{7,6},{8,9},{9,8},{10,11... | collective-permute-start | bytes 786440 | tf_op jit(solution)/shard_map/ppermute | solution.py:605
  22.9 5.5 %collective-permute-start.5 = (f32[2,256,128]{2,1,0:T(8,128)S(1)}, f32[2,256,128]{2,1,0:T(8,128)S(1)}, u32[]{:S(2)}, u32[]{:S(2)}) collective-permute-start(f32[2,256,128]{2,1,0:T(8,128)S(1)} %collective-permute-done.1.refs_3_), channel_id=1, source_target_pairs={{0,1},{1,0},{2,3},{3,2},{4,5},{5,4},{6,7},{7,6},{8,9},{9,8},{10,11... | collective-permute-start | bytes 786440 | tf_op jit(solution)/shard_map/ppermute | solution.py:605
  28.4 1.5 %collective-permute-start.6 = (f32[2,256,128]{2,1,0:T(8,128)S(1)}, f32[2,256,128]{2,1,0:T(8,128)S(1)}, u32[]{:S(2)}, u32[]{:S(2)}) collective-permute-start(f32[2,256,128]{2,1,0:T(8,128)S(1)} %collective-permute-done.2.refs_4_), channel_id=1, source_target_pairs={{0,1},{1,0},{2,3},{3,2},{4,5},{5,4},{6,7},{7,6},{8,9},{9,8},{10,11... | collective-permute-start | bytes 786440 | tf_op jit(solution)/shard_map/ppermute | solution.py:605
  47.5 14.3 %copy-start = (f32[4,2,128,128]{3,2,1,0:T(8,128)S(1)}, f32[4,2,128,128]{3,2,1,0:T(8,128)}, u32[]{:S(2)}) copy-start(f32[4,2,128,128]{3,2,1,0:T(8,128)} %bubble_ref) | copy-start | bytes 1572868
  47.5 24.2 %all-to-all-start.1 = ((f32[128,16,128]{2,1,0:T(8,128)}), f32[128,16,128]{2,1,0:T(8,128)S(1)}, u32[]{:S(2)}, u32[]{:S(2)}) async-start(f32[128,16,128]{2,1,0:T(8,128)} %bitcast.48), calls=%async_computation.1 | async-start | bytes 2097152 | tf_op jit(solution)/shard_map/all_to_all | solution.py:567
  53.4 22.5 %collective-permute-start.7 = (f32[1,256,128]{2,1,0:T(8,128)S(1)}, f32[1,256,128]{2,1,0:T(8,128)S(1)}, u32[]{:S(2)}, u32[]{:S(2)}) collective-permute-start(f32[1,256,128]{2,1,0:T(8,128)S(1)} %bitcast.45), channel_id=1, source_target_pairs={{2,0},{3,1},{0,2},{1,3},{6,4},{7,5},{4,6},{5,7},{10,8},{11,9},{8,1... | collective-permute-start | bytes 393224 | tf_op jit(solution)/shard_map/ppermute | solution.py:601
  56.4 19.6 %collective-permute-start.8 = (f32[1,256,128]{2,1,0:T(8,128)S(1)}, f32[1,256,128]{2,1,0:T(8,128)S(1)}, u32[]{:S(2)}, u32[]{:S(2)}) collective-permute-start(f32[1,256,128]{2,1,0:T(8,128)S(1)} %bitcast.44), channel_id=1, source_target_pairs={{64,0},{65,1},{126,2},{127,3},{124,4},{125,5},{122,6},{123,7},{120... | collective-permute-start | bytes 393224 | tf_op jit(solution)/shard_map/ppermute | solution.py:601
  61.7 14.3 %collective-permute-start.9 = (f32[1,256,128]{2,1,0:T(8,128)S(1)}, f32[1,256,128]{2,1,0:T(8,128)S(1)}, u32[]{:S(2)}, u32[]{:S(2)}) collective-permute-start(f32[1,256,128]{2,1,0:T(8,128)S(1)} %bitcast.43), channel_id=1, source_target_pairs={{66,0},{67,1},{124,2},{125,3},{126,4},{127,5},{120,6},{121,7},{122... | collective-permute-start | bytes 393224 | tf_op jit(solution)/shard_map/ppermute | solution.py:601
  75.9 26.1 %all-to-all-start.2 = ((f32[128,16,128]{2,1,0:T(8,128)}), f32[128,16,128]{2,1,0:T(8,128)S(1)}, u32[]{:S(2)}, u32[]{:S(2)}) async-start(f32[128,16,128]{2,1,0:T(8,128)} %bitcast.46), calls=%async_computation.2 | async-start | bytes 2097152 | tf_op jit(solution)/shard_map/all_to_all | solution.py:567
  83.0 1.4 %collective-permute-start.10 = (f32[1,256,128]{2,1,0:T(8,128)S(1)}, f32[1,256,128]{2,1,0:T(8,128)S(1)}, u32[]{:S(2)}, u32[]{:S(2)}) collective-permute-start(f32[1,256,128]{2,1,0:T(8,128)S(1)} %bitcast.41), channel_id=1, source_target_pairs={{0,1},{1,0},{2,3},{3,2},{4,5},{5,4},{6,7},{7,6},{8,9},{9,8},{10,11... | collective-permute-start | bytes 393224 | tf_op jit(solution)/shard_map/ppermute | solution.py:605
  83.1 1.5 %collective-permute-start.11 = (f32[1,256,128]{2,1,0:T(8,128)S(1)}, f32[1,256,128]{2,1,0:T(8,128)S(1)}, u32[]{:S(2)}, u32[]{:S(2)}) collective-permute-start(f32[1,256,128]{2,1,0:T(8,128)S(1)} %collective-permute-done.7.refs_2_), channel_id=1, source_target_pairs={{0,1},{1,0},{2,3},{3,2},{4,5},{5,4},{6,7},{7,6},{8,9},{9,8},{10,11... | collective-permute-start | bytes 393224 | tf_op jit(solution)/shard_map/ppermute | solution.py:605
  83.6 1.3 %collective-permute-start.12 = (f32[1,256,128]{2,1,0:T(8,128)S(1)}, f32[1,256,128]{2,1,0:T(8,128)S(1)}, u32[]{:S(2)}, u32[]{:S(2)}) collective-permute-start(f32[1,256,128]{2,1,0:T(8,128)S(1)} %collective-permute-done.8.refs_3_), channel_id=1, source_target_pairs={{0,1},{1,0},{2,3},{3,2},{4,5},{5,4},{6,7},{7,6},{8,9},{9,8},{10,11... | collective-permute-start | bytes 393224 | tf_op jit(solution)/shard_map/ppermute | solution.py:605
  83.7 1.4 %collective-permute-start.13 = (f32[1,256,128]{2,1,0:T(8,128)S(1)}, f32[1,256,128]{2,1,0:T(8,128)S(1)}, u32[]{:S(2)}, u32[]{:S(2)}) collective-permute-start(f32[1,256,128]{2,1,0:T(8,128)S(1)} %collective-permute-done.9.refs_4_), channel_id=1, source_target_pairs={{0,1},{1,0},{2,3},{3,2},{4,5},{5,4},{6,7},{7,6},{8,9},{9,8},{10,11... | collective-permute-start | bytes 393224 | tf_op jit(solution)/shard_map/ppermute | solution.py:605

commit v6 on v5

--- a/solution.py
+++ b/solution.py
@@ -413,18 +413,16 @@
 
 
 def sigma_kernel(*refs):
-    x_in_ref, *tables_hbm = refs[:4]
+    x_in_ref, t_in_ref, *tables_hbm = refs[:4]
     in_ref, base_hbm, pot_ref, plus_hbm, table_hbm, out_ref, table_ref = refs[4:11]
-    tables, refs = refs[11:14], refs[14:]
+    (t_out_ref, x_out_ref), refs = refs[11:13], refs[13:]
     base_ref, plus_ref, left_ref, acc_ref, sems = refs
-    t_in_ref, t_out_ref, x_out_ref = tables
-    t_in_here = fetch(tables_hbm[0], t_in_ref, sems.at[2])
     fields_here = [
         fetch(plus_hbm, plus_ref, sems.at[3]),
         fetch(base_hbm.at[pl.ds(0, 1)], base_ref, sems.at[4]),
     ]
-    t_out_here = fetch(tables_hbm[1], t_out_ref, sems.at[6])
-    x_out_here = fetch(tables_hbm[2], x_out_ref, sems.at[0])
+    t_out_here = fetch(tables_hbm[0], t_out_ref, sems.at[6])
+    x_out_here = fetch(tables_hbm[1], x_out_ref, sems.at[0])
     table_here = fetch(table_hbm, table_ref, sems.at[1])
 
     for slab in range(2):
@@ -432,7 +430,6 @@
         result = dot3(x_in_ref[0], x_in_ref[1], high, low)
         to_left(result, pl.ds(slab * 128, 128), left_ref)
 
-    t_in_here()
     for step in range(4):
         change = to_times(step, left_ref, t_in_ref, -1)
         if step == 0:
@@ -553,11 +550,11 @@
 
 def sigma_call(tables, held, base, pot, plus, table):
     scratch = [
-        *map(like, tables[1:]), field(1), pltpu.VMEM(PLUS, F32),
+        *map(like, tables[2:]), field(1), pltpu.VMEM(PLUS, F32),
         pltpu.VMEM((4, 256, 256), F32), pltpu.VMEM((4, 256, 256), F32), sems(7),
     ]
     return call(
-        sigma_kernel, "sigma", [HERE, HBM, HBM, HBM, HERE, HBM, HERE, HBM, HBM], [HERE, TABLE],
+        sigma_kernel, "sigma", [HERE, HERE, HBM, HBM, HERE, HBM, HERE, HBM, HBM], [HERE, TABLE],
         [SLABS, table.shape], scratch, 4 * TURN, *tables, held.reshape(SLABS), base, pot, plus, table,
     )
 
@@ -620,9 +617,10 @@
     held = exchange(sent).reshape(2048, 128)
     sent = middle_call(weight, momenta_here, columns, held)
     own, sent = lax.optimization_barrier((own, sent))
-    x_here, pot = prepare_call(both_cores(own), [x_table], True)
+    t_table = jnp.asarray(t_in(BOSE, -1))
+    x_here, t_here, pot = prepare_call(both_cores(own), [x_table, t_table], True)
     held = exchange(sent)
-    tables = (x_here, jnp.asarray(t_in(BOSE, -1)), jnp.asarray(t_out(FERMI, 1)), back)
+    tables = (x_here, t_here, jnp.asarray(t_out(FERMI, 1)), back)
     sent, momenta_here = sigma_call(tables, held, base, pot, plus, momenta)
     held = exchange(sent).reshape(2048, 128)
     return last_call(momenta_here, held)

time: 132 us -> 132 us (level)
  local copies, waits for them, and re-layouts: 0.01 us -> 2.73 us
  waiting for transfers between devices: 38.3 us -> 35.6 us
    all_to_all x3, waiting for transfers between devices: 29.7 us -> 27 us  [exchange(): return lax.all_to_all(source, BOTH, split_axis=0, concat_axis=0, tiled=True)]
    unnamed x2 -> x14, local copies, waits for them, and re-layouts: 0.01 us -> 2.73 us
where the time goes in v6:
time: 132 us; the launch traced here: 131 us
  starting transfers between devices  40.8 us (31%)
  waiting for transfers between devices  35.6 us (27%)
  Pallas kernels  28.4 us (22%)
  blocking collectives  23 us (17%)
  local copies, waits for them, and re-layouts  2.73 us (2%)
    pallas_call x9, Pallas kernels, call(): pl.pallas_call(body, in_specs=in_specs, out_specs=out_specs, out_shape=[p...  28.4 us
    all_to_all x3, waiting for transfers between devices, exchange(): return lax.all_to_all(source, BOTH, split_axis=0, concat_axis=0, tiled=True)  27 us
    all_to_all x1, blocking collectives, exchange(): return lax.all_to_all(source, BOTH, split_axis=0, concat_axis=0, tiled=True)  23 us
    all_to_all x3, starting transfers between devices, exchange(): return lax.all_to_all(source, BOTH, split_axis=0, concat_axis=0, tiled=True)  20.9 us
    ppermute x6, starting transfers between devices, send(): lax.ppermute(rows[shift], BOTH, routes(shift))  18.1 us
    ppermute x6, waiting for transfers between devices, send(): lax.ppermute(rows[shift], BOTH, routes(shift))  6.08 us
    unnamed x14, local copies, waits for them, and re-layouts  2.73 us
  transfers between devices with their start and end apart: 17, of which 10 were waited for; matrix products, arithmetic and copies ran while one was open for 0% of the time, Pallas kernels for 10%

profile of v6, /device:TPU:0, one launch (start us, length us, event | category | flops | bytes accessed | tf_op | source)
XLA Modules:
  0.0 130.8 jit_solution(12180196459462705561)
XLA Ops:
  0.0 3.6 %begin.1 = (f32[2,64,4,1,128]{4,3,2,1,0:T(1,128)S(1)}, f32[2,64,4,1,128]{4,3,2,1,0:T(1,128)S(1)}, f32[2,64,4,1,128]{4,3,2,1,0:T(1,128)S(1)}, f32[2,64,4,1,128]{4,3,2,1,0:T(1,128)S(1)}, f32[64,32,128]{2,1,0:T(8,128)}) custom-call(f32[64,4,4,1,128]{4,3,2,1,0:T(1,128)} %bitcast.50, f32[64,4,4,1,128]{4,3,2,1,0:T(1,128)} %bitcast.51, ...), custom_call_target="tpu_custom_call" | custom-call | flops 402653184 | bytes 2359296 | tf_op jit(solution)/shard_map/begin/pallas_call | solution.py:470
  3.6 4.0 %collective-permute-start = (f32[2,256,128]{2,1,0:T(8,128)S(1)}, f32[2,256,128]{2,1,0:T(8,128)S(1)}, u32[]{:S(2)}, u32[]{:S(2)}) collective-permute-start(f32[2,256,128]{2,1,0:T(8,128)S(1)} %bitcast.40), channel_id=1, source_target_pairs={{2,0},{3,1},{0,2},{1,3},{6,4},{7,5},{4,6},{5,7},{10,8},{11,9},{8,1... | collective-permute-start | bytes 786440 | tf_op jit(solution)/shard_map/ppermute | solution.py:598
  7.6 5.7 %collective-permute-start.1 = (f32[2,256,128]{2,1,0:T(8,128)S(1)}, f32[2,256,128]{2,1,0:T(8,128)S(1)}, u32[]{:S(2)}, u32[]{:S(2)}) collective-permute-start(f32[2,256,128]{2,1,0:T(8,128)S(1)} %bitcast.39), channel_id=1, source_target_pairs={{64,0},{65,1},{126,2},{127,3},{124,4},{125,5},{122,6},{123,7},{120... | collective-permute-start | bytes 786440 | tf_op jit(solution)/shard_map/ppermute | solution.py:598
  13.3 0.0 collective-permute-start.2
  13.3 9.0 %all-to-all-start = ((f32[128,16,128]{2,1,0:T(8,128)}), f32[128,16,128]{2,1,0:T(8,128)S(1)}, u32[]{:S(2)}, u32[]{:S(2)}) async-start(f32[128,16,128]{2,1,0:T(8,128)} %bitcast.47), calls=%async_computation | async-start | bytes 2097152 | tf_op jit(solution)/shard_map/all_to_all | solution.py:564
  22.3 0.1 collective-permute-start.3
  22.4 0.0 collective-permute-done.refs_2_
  22.4 0.5 collective-permute-start.4
  22.9 0.0 collective-permute-done.1.refs_3_
  22.9 0.1 collective-permute-start.5
  23.0 5.4 %collective-permute-done.2.refs_4_ = f32[2,256,128]{2,1,0:T(8,128)S(1)} collective-permute-done((f32[2,256,128]{2,1,0:T(8,128)S(1)}, f32[2,256,128]{2,1,0:T(8,128)S(1)}, u32[]{:S(2)}, u32[]{:S(2)}) %collective-permute-start.2) | collective-permute-done | bytes 262176 | tf_op jit(solution)/shard_map/ppermute | solution.py:598
  28.4 0.0 collective-permute-start.6
  28.4 0.0 collective-permute-done.3.refs_5_
  28.4 0.0 collective-permute-done.4.refs_6_
  28.4 0.0 collective-permute-done.5.refs_7_
  28.4 1.5 %collective-permute-done.6.refs_8_ = f32[2,256,128]{2,1,0:T(8,128)S(1)} collective-permute-done((f32[2,256,128]{2,1,0:T(8,128)S(1)}, f32[2,256,128]{2,1,0:T(8,128)S(1)}, u32[]{:S(2)}, u32[]{:S(2)}) %collective-permute-start.6) | collective-permute-done | bytes 262176 | tf_op jit(solution)/shard_map/ppermute | solution.py:602
  29.9 4.2 %prepare.2 = (bf16[2,256,256]{2,1,0:T(8,128)(2,1)S(1)}, f32[2,2,256,512]{3,2,1,0:T(8,128)}) custom-call(bf16[512,512]{1,0:T(8,128)(2,1)} %constant.22.clone.order_hbm, bf16[2,256,256]{2,1,0:T(8,128)(2,1)} %constant.20.clone.refs_0_, f32[2,256,128]{2,1,0:T(8,128)S(1)} %bitcast.37, f32[2,256,128]{2,1,0:T(8,128)S(1)} %collective-permute-done.refs_2_, ...), custom_call_target="tpu_custom_call" | custom-call | flops 6442450944 | bytes 2883584 | tf_op jit(solution)/shard_map/prepare/pallas_call | solution.py:470
  34.2 7.2 %all-to-all-done = f32[128,16,128]{2,1,0:T(8,128)S(1)} async-done(((f32[128,16,128]{2,1,0:T(8,128)}), f32[128,16,128]{2,1,0:T(8,128)S(1)}, u32[]{:S(2)}, u32[]{:S(2)}) %all-to-all-start) | async-done | bytes 1048608 | tf_op jit(solution)/shard_map/all_to_all | solution.py:564
  41.4 6.1 %chi.1 = (f32[32,4,2,8,128]{4,3,2,1,0:T(8,128)}, f32[256,1024]{1,0:T(8,128)}) custom-call(bf16[2,256,256]{2,1,0:T(8,128)(2,1)S(1)} %get-tuple-element.41.refs_0_, bf16[4,2,256,256]{3,2,1,0:T(8,128)(2,1)} %constant.23.clone.refs_1_, bf16[4,2,256,256]{3,2,1,0:T(8,128)(2,1)} %constant.24.clone.refs_2_, bf16[2,256,256]{2,1,0:T(8,128)(2,1)} %constant.21.clone.refs_3_, ...), custom_call_target="tpu_custom_call" | custom-call | flops 2818572288 | bytes 5767168 | tf_op jit(solution)/shard_map/chi/pallas_call | solution.py:470
  47.5 0.0 copy-start
  47.5 4.8 %all-to-all-start.1 = ((f32[128,16,128]{2,1,0:T(8,128)}), f32[128,16,128]{2,1,0:T(8,128)S(1)}, u32[]{:S(2)}, u32[]{:S(2)}) async-start(f32[128,16,128]{2,1,0:T(8,128)} %bitcast.48), calls=%async_computation.1 | async-start | bytes 2097152 | tf_op jit(solution)/shard_map/all_to_all | solution.py:564
  52.3 1.1 pack.1
  53.4 2.9 %collective-permute-start.7 = (f32[1,256,128]{2,1,0:T(8,128)S(1)}, f32[1,256,128]{2,1,0:T(8,128)S(1)}, u32[]{:S(2)}, u32[]{:S(2)}) collective-permute-start(f32[1,256,128]{2,1,0:T(8,128)S(1)} %bitcast.45), channel_id=1, source_target_pairs={{2,0},{3,1},{0,2},{1,3},{6,4},{7,5},{4,6},{5,7},{10,8},{11,9},{8,1... | collective-permute-start | bytes 393224 | tf_op jit(solution)/shard_map/ppermute | solution.py:598
  56.4 5.3 %collective-permute-start.8 = (f32[1,256,128]{2,1,0:T(8,128)S(1)}, f32[1,256,128]{2,1,0:T(8,128)S(1)}, u32[]{:S(2)}, u32[]{:S(2)}) collective-permute-start(f32[1,256,128]{2,1,0:T(8,128)S(1)} %bitcast.44), channel_id=1, source_target_pairs={{64,0},{65,1},{126,2},{127,3},{124,4},{125,5},{122,6},{123,7},{120... | collective-permute-start | bytes 393224 | tf_op jit(solution)/shard_map/ppermute | solution.py:598
  61.7 0.2 collective-permute-start.9
  61.8 1.0 weight.1
  62.8 8.9 %all-to-all-done.1 = f32[128,16,128]{2,1,0:T(8,128)S(1)} async-done(((f32[128,16,128]{2,1,0:T(8,128)}), f32[128,16,128]{2,1,0:T(8,128)S(1)}, u32[]{:S(2)}, u32[]{:S(2)}) %all-to-all-start.1) | async-done | bytes 1048608 | tf_op jit(solution)/shard_map/all_to_all | solution.py:564
  71.7 3.5 %middle.1 = f32[64,32,128]{2,1,0:T(8,128)} custom-call(bf16[2,256,256]{2,1,0:T(8,128)(2,1)S(1)} %get-tuple-element.51.in_table_ref, bf16[2,256,256]{2,1,0:T(8,128)(2,1)} %constant.18.clone.table_hbm.out_table_hbm, f32[2,128,512]{2,1,0:T(8,128)S(1)} %get-tuple-element.52.weight_ref, f32[2048,128]{1,0:T(8,128)S(1)} %bitcast.31), custom_call_target="tpu_custom_call" | custom-call | flops 805306368 | bytes 2097152 | tf_op jit(solution)/shard_map/middle/pallas_call | solution.py:470
  75.2 0.7 collective-permute-done.7.refs_3_
  75.9 0.0 collective-permute-done.8.refs_4_
  75.9 0.0 collective-permute-done.9.refs_5_
  75.9 7.1 %all-to-all-start.2 = ((f32[128,16,128]{2,1,0:T(8,128)}), f32[128,16,128]{2,1,0:T(8,128)S(1)}, u32[]{:S(2)}, u32[]{:S(2)}) async-start(f32[128,16,128]{2,1,0:T(8,128)} %bitcast.46), calls=%async_computation.2 | async-start | bytes 2097152 | tf_op jit(solution)/shard_map/all_to_all | solution.py:564
  83.0 0.1 collective-permute-start.10
  83.1 0.5 collective-permute-start.11
  83.6 0.1 collective-permute-start.12
  83.7 0.4 collective-permute-start.13
  84.1 0.3 collective-permute-done.10.refs_6_
  84.4 0.2 collective-permute-done.11.refs_7_
  84.6 0.3 collective-permute-done.12.refs_8_
  85.0 0.2 collective-permute-done.13.refs_9_
  85.2 0.9 copy-done.2
  86.1 0.9 copy-done.4
  87.0 0.9 copy-done.6
  87.9 3.4 %prepare.3 = (bf16[2,256,256]{2,1,0:T(8,128)(2,1)S(1)}, bf16[4,2,256,256]{3,2,1,0:T(8,128)(2,1)S(1)}, f32[1,2,256,512]{3,2,1,0:T(8,128)S(1)}) custom-call(bf16[512,512]{1,0:T(8,128)(2,1)} %constant.22.clone.order_hbm, bf16[2,256,256]{2,1,0:T(8,128)(2,1)} %constant.20.clone.refs_0_, bf16[4,2,256,256]{3,2,1,0:T(8,128)(2,1)} %constant.25.clone.refs_1_, ...), custom_call_target="tpu_custom_call" | custom-call | flops 6442450944 | bytes 2883584 | tf_op jit(solution)/shard_map/prepare/pallas_call | solution.py:470
  91.2 10.8 %all-to-all-done.2 = f32[128,16,128]{2,1,0:T(8,128)S(1)} async-done(((f32[128,16,128]{2,1,0:T(8,128)}), f32[128,16,128]{2,1,0:T(8,128)S(1)}, u32[]{:S(2)}, u32[]{:S(2)}) %all-to-all-start.2) | async-done | bytes 1048608 | tf_op jit(solution)/shard_map/all_to_all | solution.py:564
  102.1 3.6 %sigma.1 = (f32[32,4,2,8,128]{4,3,2,1,0:T(8,128)S(1)}, bf16[2,256,256]{2,1,0:T(8,128)(2,1)S(1)}) custom-call(bf16[2,256,256]{2,1,0:T(8,128)(2,1)S(1)} %get-tuple-element.58.refs_0_, bf16[4,2,256,256]{3,2,1,0:T(8,128)(2,1)S(1)} %get-tuple-element.59.refs_1_, bf16[4,2,256,256]{3,2,1,0:T(8,128)(2,1)} %constant.26.clone.refs_2_, ...), custom_call_target="tpu_custom_call" | custom-call | flops 1610612736 | bytes 8126464 | tf_op jit(solution)/shard_map/sigma/pallas_call | solution.py:470
  105.7 23.0 %all_to_all.20 = f32[128,16,128]{2,1,0:T(8,128)S(1)} all-to-all(f32[128,16,128]{2,1,0:T(8,128)S(1)} %bitcast.35), channel_id=1, replica_groups=mesh['site'=32,'freq'=4] {'site','freq'}, dimensions={0} | all-to-all | bytes 2097152 | tf_op jit(solution)/shard_map/all_to_all | solution.py:564
  128.8 1.9 %last.1 = f32[4,2,2,128,128]{4,3,2,1,0:T(8,128)} custom-call(bf16[2,256,256]{2,1,0:T(8,128)(2,1)S(1)} %get-tuple-element.63.table_ref, f32[2048,128]{1,0:T(8,128)S(1)} %bitcast.32), custom_call_target="tpu_custom_call" | custom-call | flops 402653184 | bytes 1310720 | tf_op jit(solution)/shard_map/last/pallas_call | solution.py:470
  (10 shorter events, 0.0 us)
Async XLA Ops:
  3.6 18.9 %collective-permute-start = (f32[2,256,128]{2,1,0:T(8,128)S(1)}, f32[2,256,128]{2,1,0:T(8,128)S(1)}, u32[]{:S(2)}, u32[]{:S(2)}) collective-permute-start(f32[2,256,128]{2,1,0:T(8,128)S(1)} %bitcast.40), channel_id=1, source_target_pairs={{2,0},{3,1},{0,2},{1,3},{6,4},{7,5},{4,6},{5,7},{10,8},{11,9},{8,1... | collective-permute-start | bytes 786440 | tf_op jit(solution)/shard_map/ppermute | solution.py:598
  7.6 15.3 %collective-permute-start.1 = (f32[2,256,128]{2,1,0:T(8,128)S(1)}, f32[2,256,128]{2,1,0:T(8,128)S(1)}, u32[]{:S(2)}, u32[]{:S(2)}) collective-permute-start(f32[2,256,128]{2,1,0:T(8,128)S(1)} %bitcast.39), channel_id=1, source_target_pairs={{64,0},{65,1},{126,2},{127,3},{124,4},{125,5},{122,6},{123,7},{120... | collective-permute-start | bytes 786440 | tf_op jit(solution)/shard_map/ppermute | solution.py:598
  13.3 15.1 %collective-permute-start.2 = (f32[2,256,128]{2,1,0:T(8,128)S(1)}, f32[2,256,128]{2,1,0:T(8,128)S(1)}, u32[]{:S(2)}, u32[]{:S(2)}) collective-permute-start(f32[2,256,128]{2,1,0:T(8,128)S(1)} %bitcast.38), channel_id=1, source_target_pairs={{66,0},{67,1},{124,2},{125,3},{126,4},{127,5},{120,6},{121,7},{122... | collective-permute-start | bytes 786440 | tf_op jit(solution)/shard_map/ppermute | solution.py:598
  13.3 28.1 %all-to-all-start = ((f32[128,16,128]{2,1,0:T(8,128)}), f32[128,16,128]{2,1,0:T(8,128)S(1)}, u32[]{:S(2)}, u32[]{:S(2)}) async-start(f32[128,16,128]{2,1,0:T(8,128)} %bitcast.47), calls=%async_computation | async-start | bytes 2097152 | tf_op jit(solution)/shard_map/all_to_all | solution.py:564
  22.3 6.1 %collective-permute-start.3 = (f32[2,256,128]{2,1,0:T(8,128)S(1)}, f32[2,256,128]{2,1,0:T(8,128)S(1)}, u32[]{:S(2)}, u32[]{:S(2)}) collective-permute-start(f32[2,256,128]{2,1,0:T(8,128)S(1)} %bitcast.36), channel_id=1, source_target_pairs={{0,1},{1,0},{2,3},{3,2},{4,5},{5,4},{6,7},{7,6},{8,9},{9,8},{10,11... | collective-permute-start | bytes 786440 | tf_op jit(solution)/shard_map/ppermute | solution.py:602
  22.4 6.0 %collective-permute-start.4 = (f32[2,256,128]{2,1,0:T(8,128)S(1)}, f32[2,256,128]{2,1,0:T(8,128)S(1)}, u32[]{:S(2)}, u32[]{:S(2)}) collective-permute-start(f32[2,256,128]{2,1,0:T(8,128)S(1)} %collective-permute-done.refs_2_), channel_id=1, source_target_pairs={{0,1},{1,0},{2,3},{3,2},{4,5},{5,4},{6,7},{7,6},{8,9},{9,8},{10,11... | collective-permute-start | bytes 786440 | tf_op jit(solution)/shard_map/ppermute | solution.py:602
  22.9 5.5 %collective-permute-start.5 = (f32[2,256,128]{2,1,0:T(8,128)S(1)}, f32[2,256,128]{2,1,0:T(8,128)S(1)}, u32[]{:S(2)}, u32[]{:S(2)}) collective-permute-start(f32[2,256,128]{2,1,0:T(8,128)S(1)} %collective-permute-done.1.refs_3_), channel_id=1, source_target_pairs={{0,1},{1,0},{2,3},{3,2},{4,5},{5,4},{6,7},{7,6},{8,9},{9,8},{10,11... | collective-permute-start | bytes 786440 | tf_op jit(solution)/shard_map/ppermute | solution.py:602
  28.4 1.5 %collective-permute-start.6 = (f32[2,256,128]{2,1,0:T(8,128)S(1)}, f32[2,256,128]{2,1,0:T(8,128)S(1)}, u32[]{:S(2)}, u32[]{:S(2)}) collective-permute-start(f32[2,256,128]{2,1,0:T(8,128)S(1)} %collective-permute-done.2.refs_4_), channel_id=1, source_target_pairs={{0,1},{1,0},{2,3},{3,2},{4,5},{5,4},{6,7},{7,6},{8,9},{9,8},{10,11... | collective-permute-start | bytes 786440 | tf_op jit(solution)/shard_map/ppermute | solution.py:602
  47.5 14.3 %copy-start = (f32[4,2,128,128]{3,2,1,0:T(8,128)S(1)}, f32[4,2,128,128]{3,2,1,0:T(8,128)}, u32[]{:S(2)}) copy-start(f32[4,2,128,128]{3,2,1,0:T(8,128)} %bubble_ref) | copy-start | bytes 1572868
  47.5 24.2 %all-to-all-start.1 = ((f32[128,16,128]{2,1,0:T(8,128)}), f32[128,16,128]{2,1,0:T(8,128)S(1)}, u32[]{:S(2)}, u32[]{:S(2)}) async-start(f32[128,16,128]{2,1,0:T(8,128)} %bitcast.48), calls=%async_computation.1 | async-start | bytes 2097152 | tf_op jit(solution)/shard_map/all_to_all | solution.py:564
  53.4 22.5 %collective-permute-start.7 = (f32[1,256,128]{2,1,0:T(8,128)S(1)}, f32[1,256,128]{2,1,0:T(8,128)S(1)}, u32[]{:S(2)}, u32[]{:S(2)}) collective-permute-start(f32[1,256,128]{2,1,0:T(8,128)S(1)} %bitcast.45), channel_id=1, source_target_pairs={{2,0},{3,1},{0,2},{1,3},{6,4},{7,5},{4,6},{5,7},{10,8},{11,9},{8,1... | collective-permute-start | bytes 393224 | tf_op jit(solution)/shard_map/ppermute | solution.py:598
  56.4 19.6 %collective-permute-start.8 = (f32[1,256,128]{2,1,0:T(8,128)S(1)}, f32[1,256,128]{2,1,0:T(8,128)S(1)}, u32[]{:S(2)}, u32[]{:S(2)}) collective-permute-start(f32[1,256,128]{2,1,0:T(8,128)S(1)} %bitcast.44), channel_id=1, source_target_pairs={{64,0},{65,1},{126,2},{127,3},{124,4},{125,5},{122,6},{123,7},{120... | collective-permute-start | bytes 393224 | tf_op jit(solution)/shard_map/ppermute | solution.py:598
  61.7 14.3 %collective-permute-start.9 = (f32[1,256,128]{2,1,0:T(8,128)S(1)}, f32[1,256,128]{2,1,0:T(8,128)S(1)}, u32[]{:S(2)}, u32[]{:S(2)}) collective-permute-start(f32[1,256,128]{2,1,0:T(8,128)S(1)} %bitcast.43), channel_id=1, source_target_pairs={{66,0},{67,1},{124,2},{125,3},{126,4},{127,5},{120,6},{121,7},{122... | collective-permute-start | bytes 393224 | tf_op jit(solution)/shard_map/ppermute | solution.py:598
  75.9 9.1 %copy-start.1 = (f32[1,256,128]{2,1,0:T(8,128)}, f32[1,256,128]{2,1,0:T(8,128)S(1)}, u32[]{:S(2)}) copy-start(f32[1,256,128]{2,1,0:T(8,128)S(1)} %collective-permute-done.7.refs_3_) | copy-start | bytes 393220
  75.9 9.0 %copy-start.3 = (f32[1,256,128]{2,1,0:T(8,128)}, f32[1,256,128]{2,1,0:T(8,128)S(1)}, u32[]{:S(2)}) copy-start(f32[1,256,128]{2,1,0:T(8,128)S(1)} %collective-permute-done.8.refs_4_) | copy-start | bytes 393220
  75.9 9.0 %copy-start.5 = (f32[1,256,128]{2,1,0:T(8,128)}, f32[1,256,128]{2,1,0:T(8,128)S(1)}, u32[]{:S(2)}) copy-start(f32[1,256,128]{2,1,0:T(8,128)S(1)} %collective-permute-done.9.refs_5_) | copy-start | bytes 393220
  75.9 26.1 %all-to-all-start.2 = ((f32[128,16,128]{2,1,0:T(8,128)}), f32[128,16,128]{2,1,0:T(8,128)S(1)}, u32[]{:S(2)}, u32[]{:S(2)}) async-start(f32[128,16,128]{2,1,0:T(8,128)} %bitcast.46), calls=%async_computation.2 | async-start | bytes 2097152 | tf_op jit(solution)/shard_map/all_to_all | solution.py:564
  83.0 1.4 %collective-permute-start.10 = (f32[1,256,128]{2,1,0:T(8,128)S(1)}, f32[1,256,128]{2,1,0:T(8,128)S(1)}, u32[]{:S(2)}, u32[]{:S(2)}) collective-permute-start(f32[1,256,128]{2,1,0:T(8,128)S(1)} %bitcast.41), channel_id=1, source_target_pairs={{0,1},{1,0},{2,3},{3,2},{4,5},{5,4},{6,7},{7,6},{8,9},{9,8},{10,11... | collective-permute-start | bytes 393224 | tf_op jit(solution)/shard_map/ppermute | solution.py:602
  83.1 1.5 %collective-permute-start.11 = (f32[1,256,128]{2,1,0:T(8,128)S(1)}, f32[1,256,128]{2,1,0:T(8,128)S(1)}, u32[]{:S(2)}, u32[]{:S(2)}) collective-permute-start(f32[1,256,128]{2,1,0:T(8,128)S(1)} %collective-permute-done.7.refs_3_), channel_id=1, source_target_pairs={{0,1},{1,0},{2,3},{3,2},{4,5},{5,4},{6,7},{7,6},{8,9},{9,8},{10,11... | collective-permute-start | bytes 393224 | tf_op jit(solution)/shard_map/ppermute | solution.py:602
  83.6 1.3 %collective-permute-start.12 = (f32[1,256,128]{2,1,0:T(8,128)S(1)}, f32[1,256,128]{2,1,0:T(8,128)S(1)}, u32[]{:S(2)}, u32[]{:S(2)}) collective-permute-start(f32[1,256,128]{2,1,0:T(8,128)S(1)} %collective-permute-done.8.refs_4_), channel_id=1, source_target_pairs={{0,1},{1,0},{2,3},{3,2},{4,5},{5,4},{6,7},{7,6},{8,9},{9,8},{10,11... | collective-permute-start | bytes 393224 | tf_op jit(solution)/shard_map/ppermute | solution.py:602
  83.7 1.4 %collective-permute-start.13 = (f32[1,256,128]{2,1,0:T(8,128)S(1)}, f32[1,256,128]{2,1,0:T(8,128)S(1)}, u32[]{:S(2)}, u32[]{:S(2)}) collective-permute-start(f32[1,256,128]{2,1,0:T(8,128)S(1)} %collective-permute-done.9.refs_5_), channel_id=1, source_target_pairs={{0,1},{1,0},{2,3},{3,2},{4,5},{5,4},{6,7},{7,6},{8,9},{9,8},{10,11... | collective-permute-start | bytes 393224 | tf_op jit(solution)/shard_map/ppermute | solution.py:602
  85.1 0.9 copy-start.2
  86.1 0.9 copy-start.4
  87.0 0.9 copy-start.6
